TPU v7x, 32 devices: a whole 2x2x4 slice. The times are simulated.
32 devices in a mesh: hash: 4 (over y, core), dp: 8 (over z, x).
Axes of the slice: x: 2, y: 2, z: 4, core: 2. Of those that a mesh axis runs over, the one named last changes fastest.
Arguments:
- histories: bfloat16 [128, 256, 512], P(('hash', 'dp')), may hold values from -6 to 6
- weight_in: bfloat16 [512, 2048], replicated, may hold values from -0.25 to 0.25
- weight_out: bfloat16 [512, 512], replicated, may hold values from -0.25 to 0.25
- candidates: bfloat16 [8192, 512], P(('hash', 'dp')), may hold values from -6 to 6
- cotangent: bfloat16 [8192, 512], P(('hash', 'dp')), may hold values from -6 to 6
- owner_ids: int32 [8192, 1], P(('hash', 'dp')), may hold values from 0 to 31; in each aligned block of 256 rows (0 to 255, 256 to 511, ...) at most 16 rows name the same one
- hist_slot: int32 [8192], P(('hash', 'dp')), may hold values from 0 to 3
- lengths: int32 [8192], P(('hash', 'dp')), may hold values from 1 to 256
Outputs:
- history_grad: bfloat16 [128, 256, 512], P(('hash', 'dp'))
- candidate_grad: bfloat16 [8192, 512], P(('hash', 'dp'))
- weight_in_grad: float32 [512, 2048], P(('hash', 'dp'))
- weight_out_grad: float32 [512, 512], P(('hash', 'dp'))
Inputs may be any that keep to these rules, and one draw needn't show every extreme that they name: `owner_ids`: in the rows of one device, at most 16 impressions name the same owner; the bound is reached.
All inputs are finite; a program needn't handle non-finite values.
Results may differ from a plain program's by a relative error of at most 0.012.
Values may be sent and summed in bfloat16 or wider, within the bound.
No kernel may reach another device: no remote copies, remote signals or barrier semaphores. Data moves between devices by JAX's collectives and lax.ppermute only.
A program may use at most 128 MiB of HBM per device.

v0:
```python
import functools

import jax
import jax.numpy as jnp
from jax import lax
from jax.experimental import pallas as pl
from jax.experimental.pallas import tpu as pltpu
from jax.sharding import PartitionSpec as P

HEADS = 8
TILE = 128
META = 128
AXES = ("hash_hi", "core", "dp_hi", "dp_lo")
norm_eps = 1e-05
f32 = jnp.float32
bf16 = jnp.bfloat16
MIB = 1024 * 1024


def dot_nn(a, b):
    return lax.dot_general(a, b, (((1,), (0,)), ((), ())), preferred_element_type=f32)


def dot_nt(a, b):
    return lax.dot_general(a, b, (((1,), (1,)), ((), ())), preferred_element_type=f32)


def dot_tn(a, b):
    return lax.dot_general(a, b, (((0,), (0,)), ((), ())), preferred_element_type=f32)


def iota(shape, axis):
    return lax.broadcasted_iota(jnp.int32, shape, axis)


def silu_pair(half):
    t = jnp.tanh(half)
    u = 1.0 + t
    act = half * u
    return act, u + act * (1.0 - t)


def lane_masks(width, part):
    lane = iota((1, width), 1)
    return [((lane >= j * part) & (lane < (j + 1) * part)).astype(bf16) for j in range(width // part)]


def both_heads(pair, masks):
    return jnp.concatenate([pair * m for m in masks], axis=0)


def pick_lanes(stacked, head):
    rows = stacked.shape[0] // 2
    lane = iota((1, 2 * head), 1)
    return jnp.where(lane < head, stacked[:rows], stacked[rows:])


def params(mib):
    return pltpu.CompilerParams(dimension_semantics=("arbitrary",), vmem_limit_bytes=mib * MIB)


def whole(shape):
    return pl.BlockSpec(shape, lambda i: (0,) * len(shape))


def cost(flops, nbytes, trans=0):
    return pl.CostEstimate(flops=int(flops), bytes_accessed=int(nbytes), transcendentals=int(trans))


def route_kernel(devices, capacity, own_ref, slot_ref, len_ref, cand_ref, cot_ref, send_ref, pick_ref):
    rows, width = cand_ref.shape
    slots = devices * capacity
    own = own_ref[...]
    hot = (own == iota((devices, rows), 0)).astype(f32)
    before = (iota((rows, rows), 0) < iota((rows, rows), 1)).astype(f32).astype(bf16)
    earlier = dot_nn(hot.astype(bf16), before)
    position = jnp.sum(earlier * hot, axis=0, keepdims=True).astype(jnp.int32)
    target = own * capacity + position
    pick = (target == iota((slots, rows), 0)).astype(f32).astype(bf16)
    pick_ref[...] = pick
    send_ref[:, :width] = dot_nn(pick, cand_ref[...]).astype(bf16)
    send_ref[:, width : 2 * width] = dot_nn(pick, cot_ref[...]).astype(bf16)
    line = iota((META, rows), 0)
    meta = jnp.where(line == 0, slot_ref[...], jnp.where(line == 1, len_ref[...], 0))
    send_ref[:, 2 * width :] = dot_nt(pick, meta.astype(f32).astype(bf16)).astype(bf16)


def route(own, slot, length, cand, cot, devices, capacity):
    rows, width = cand.shape
    slots = devices * capacity
    line = whole((1, rows))
    return pl.pallas_call(
        functools.partial(route_kernel, devices, capacity),
        grid=(1,),
        in_specs=[line, line, line, whole(cand.shape), whole(cot.shape)],
        out_specs=[whole((slots, 2 * width + META)), whole((slots, rows))],
        out_shape=(
            jax.ShapeDtypeStruct((slots, 2 * width + META), bf16),
            jax.ShapeDtypeStruct((slots, rows), bf16),
        ),
        compiler_params=params(60),
        cost_estimate=cost(2e9, 4 * rows * width * 4),
        name="route",
    )(own.reshape(1, rows), slot.reshape(1, rows), length.reshape(1, rows), cand, cot)


def forward_kernel(
    x_ref, win_ref, wout_ref, perm_ref,
    enc_ref, slope_ref, slope_t_ref, v_ref, q_ref, k_ref, q_t_ref, attn_t_ref, grad_ref,
    normed_ref, nu_ref, gi_ref, xt_ref, mt_ref,
    gate_ref, mixed_ref,
):
    seq, width = x_ref.shape[1:]
    head = width // HEADS
    half_seq = seq // 2
    x = x_ref[0]
    for branch in range(4):
        cols = slice(branch * width, (branch + 1) * width)
        act, slope = silu_pair(0.5 * dot_nn(x, win_ref[:, cols]))
        if branch == 3:
            slope_t_ref[0] = jnp.transpose(0.5 * slope).astype(bf16)
        else:
            slope_ref[0, :, cols] = (0.5 * slope).astype(bf16)
        if branch == 0:
            gate_ref[...] = act
        else:
            (v_ref, q_ref, k_ref)[branch - 1][0] = act.astype(bf16)
        if branch == 2:
            q_t_ref[0] = jnp.transpose(act).astype(bf16)
    masks = lane_masks(2 * head, head)
    scale = 0.5 * head**-0.5
    tri = iota((half_seq, half_seq), 0) >= iota((half_seq, half_seq), 1)
    zero = jnp.zeros((half_seq, half_seq), f32)
    for pair in range(HEADS // 2):
        cols = slice(pair * 2 * head, (pair + 1) * 2 * head)
        q_p = q_ref[0, :, cols] * jnp.asarray(scale, bf16)
        half = dot_nt(both_heads(q_p, masks), k_ref[0, :, cols])
        stack = []
        for j in range(2):
            h = 2 * pair + j
            top = silu_pair(half[j * seq : j * seq + half_seq, :half_seq])
            bot = silu_pair(half[j * seq + half_seq : (j + 1) * seq])
            full = []
            for a, b in zip(top, bot):
                a = jnp.concatenate([jnp.where(tri, a, 0.0), zero], axis=1)
                b = jnp.concatenate([b[:, :half_seq], jnp.where(tri, b[:, half_seq:], 0.0)], axis=1)
                full.append(jnp.concatenate([a, b], axis=0))
            stack.append(full[0].astype(bf16))
            attn_t_ref[0, h] = jnp.transpose(full[0]).astype(bf16)
            grad_ref[0, h] = full[1].astype(bf16)
        mixed = dot_nn(jnp.concatenate(stack, axis=0), v_ref[0, :, cols])
        mixed_ref[:, cols] = pick_lanes(mixed, head) * (1.0 / seq)
    mixed = mixed_ref[...]
    centred = mixed - jnp.mean(mixed, axis=1, keepdims=True)
    inv_std = lax.rsqrt(jnp.mean(centred * centred, axis=1, keepdims=True) + norm_eps)
    normed = centred * inv_std
    gate = gate_ref[...]
    merged = (normed * gate).astype(bf16)
    normed_ref[0] = normed.astype(bf16)
    nu_ref[0] = (normed * slope_ref[0, :, :width].astype(f32)).astype(bf16)
    gi_ref[0] = (gate * inv_std).astype(bf16)
    enc_ref[0] = (x.astype(f32) + dot_nn(merged, wout_ref[...])).astype(bf16)
    perm = perm_ref[...]
    xt_ref[...] = dot_nt(perm, x).astype(bf16)
    mt_ref[...] = dot_nt(perm, merged).astype(bf16)


def layer_forward(x, w_in, w_out, perm):
    hist, seq, width = x.shape
    row = pl.BlockSpec((1, seq, width), lambda i: (i, 0, 0))
    wide = pl.BlockSpec((1, seq, 3 * width), lambda i: (i, 0, 0))
    column = pl.BlockSpec((1, width, seq), lambda i: (i, 0, 0))
    square = pl.BlockSpec((1, HEADS, seq, seq), lambda i: (i, 0, 0, 0))
    turned = pl.BlockSpec((width, seq), lambda i: (0, i))
    row_s = jax.ShapeDtypeStruct((hist, seq, width), bf16)
    column_s = jax.ShapeDtypeStruct((hist, width, seq), bf16)
    square_s = jax.ShapeDtypeStruct((hist, HEADS, seq, seq), bf16)
    turned_s = jax.ShapeDtypeStruct((width, hist * seq), bf16)
    return pl.pallas_call(
        forward_kernel,
        grid=(hist,),
        in_specs=[row, whole(w_in.shape), whole(w_out.shape), whole(perm.shape)],
        out_specs=[
            row, wide, column, row, row, row, column, square, square, row, row, row, turned, turned,
        ],
        out_shape=[
            row_s, jax.ShapeDtypeStruct((hist, seq, 3 * width), bf16), column_s, row_s, row_s, row_s,
            column_s, square_s, square_s, row_s, row_s, row_s, turned_s, turned_s,
        ],
        scratch_shapes=[pltpu.VMEM((seq, width), f32), pltpu.VMEM((seq, width), f32)],
        compiler_params=params(60),
        cost_estimate=cost(18e9, 24e6),
        name="forward",
    )(x, w_in, w_out, perm)


def target_kernel(recv_ref, enc_ref, dq_ref, denc_ref, grouped_ref, turned_ref):
    hist, seq, width = enc_ref.shape
    slots = recv_ref.shape[0]
    padded = grouped_ref.shape[0]
    head = width // HEADS
    meta = recv_ref[:, 2 * width :].astype(f32)
    slot_h = meta[:, 0:1]
    valid = meta[:, 1:2] > 0.0
    lane = iota((slots, META), 1).astype(f32)
    hot = jnp.where(valid & (slot_h == lane), 1.0, 0.0)
    lower = (iota((slots, slots), 0) > iota((slots, slots), 1)).astype(f32).astype(bf16)
    rank = jnp.sum(dot_nn(lower, hot.astype(bf16)) * hot, axis=1, keepdims=True)
    starts, start = [], jnp.int32(0)
    begin = jnp.zeros((slots, 1), f32)
    for h in range(hist):
        starts.append(start)
        begin = jnp.where(slot_h == float(h), (start * TILE).astype(f32), begin)
        count = jnp.sum(hot[:, h : h + 1]).astype(jnp.int32)
        start = start + (count + (TILE - 1)) // TILE
    tiles = start
    dest = jnp.where(valid, begin + rank, -1.0)
    eye = iota((slots, slots), 0) == iota((slots, slots), 1)
    dest_row = jnp.sum(jnp.where(eye, dest, 0.0), axis=0, keepdims=True).astype(jnp.int32)
    dest_col = dest.astype(jnp.int32)
    grouped_ref[...] = jnp.zeros_like(grouped_ref)
    turned_ref[...] = jnp.zeros_like(turned_ref)
    masks = lane_masks(2 * head, head)
    scale = 0.5 * head**-0.5
    positions = iota((TILE, seq), 1).astype(f32)

    def one_tile(tile, carry):
        base = pl.multiple_of(tile * TILE, TILE)
        hist_t = jnp.int32(0)
        for h in range(1, hist):
            hist_t = hist_t + (tile >= starts[h]).astype(jnp.int32)
        choose = (iota((TILE, slots), 0) + base == dest_row).astype(f32).astype(bf16)
        rows = dot_nn(choose, recv_ref[...])
        q_all = rows[:, :width] * scale
        g_all = rows[:, width : 2 * width]
        q_t = jnp.transpose(q_all).astype(bf16)
        g_t = jnp.transpose(g_all).astype(bf16)
        q_all = q_all.astype(bf16)
        g_all = g_all.astype(bf16)
        length = rows[:, 2 * width + 1 : 2 * width + 2]
        weight = jnp.where(positions < length, 1.0 / jnp.maximum(length, 1.0), 0.0)
        for pair in range(HEADS // 2):
            cols = slice(pair * 2 * head, (pair + 1) * 2 * head)
            k_p = enc_ref[hist_t, :, cols]
            both = dot_nt(
                jnp.concatenate(
                    [both_heads(q_all[:, cols], masks), both_heads(g_all[:, cols], masks)], axis=0
                ),
                k_p,
            )
            slopes = []
            for j in range(2):
                h = 2 * pair + j
                mine = slice(h * head, (h + 1) * head)
                act, slope = silu_pair(both[j * TILE : (j + 1) * TILE])
                d_attn = both[(2 + j) * TILE : (3 + j) * TILE]
                attn = (act * weight).astype(bf16)
                d_s = (d_attn * weight * slope).astype(bf16)
                turned_ref[hist_t, mine, :] += dot_nn(
                    jnp.concatenate([g_t[mine], q_t[mine]], axis=1),
                    jnp.concatenate([attn, d_s], axis=0),
                )
                slopes.append(d_s)
            d_q = pick_lanes(dot_nn(jnp.concatenate(slopes, axis=0), k_p), head)
            grouped_ref[pl.ds(base, TILE), cols] = (d_q * scale).astype(bf16)
        return carry

    lax.fori_loop(0, tiles, one_tile, 0)
    back = (dest_col == iota((slots, padded), 1)).astype(f32).astype(bf16)
    dq_ref[...] = dot_nn(back, grouped_ref[...]).astype(bf16)
    for h in range(hist):
        denc_ref[h] = jnp.transpose(turned_ref[h]).astype(bf16)


def target_backward(recv, enc):
    hist, seq, width = enc.shape
    slots = recv.shape[0]
    padded = ((slots - hist) // TILE + hist) * TILE
    return pl.pallas_call(
        target_kernel,
        grid=(1,),
        in_specs=[whole(recv.shape), whole(enc.shape)],
        out_specs=[whole((slots, width)), whole(enc.shape)],
        out_shape=(
            jax.ShapeDtypeStruct((slots, width), bf16),
            jax.ShapeDtypeStruct(enc.shape, bf16),
        ),
        scratch_shapes=[pltpu.VMEM((padded, width), bf16), pltpu.VMEM((hist, width, seq), f32)],
        compiler_params=params(60),
        cost_estimate=cost(12e9, 4e6),
        name="target",
    )(recv, enc)


def backward_kernel(
    denc_ref, wout_ref, normed_ref, nu_ref, gi_ref, v_ref, k_ref, q_t_ref, attn_t_ref, grad_ref,
    sv_ref, sq_ref, sk_ref, xt_hbm, mt_hbm,
    dpre_ref, dk_ref, keep_ref, send_ref,
    xt_ref, mt_ref, all_ref, all_k_ref, all_enc_ref, dmix_ref, sem_ref,
):
    step = pl.program_id(0)
    seq, width = denc_ref.shape[1:]
    head = width // HEADS
    kept = keep_ref.shape[0]
    copies = [
        pltpu.make_async_copy(xt_hbm, xt_ref, sem_ref.at[0]),
        pltpu.make_async_copy(mt_hbm, mt_ref, sem_ref.at[1]),
    ]

    @pl.when(step == 0)
    def _():
        for copy in copies:
            copy.start()

    here = pl.ds(pl.multiple_of(step * seq, seq), seq)
    d_enc = denc_ref[0]
    all_enc_ref[here, :] = d_enc
    d_merged = dot_nt(d_enc, wout_ref[...])
    d_pre = (d_merged * nu_ref[0].astype(f32)).astype(bf16)
    dpre_ref[0, :, :width] = d_pre
    all_ref[here, :width] = d_pre
    normed = normed_ref[0].astype(f32)
    d_norm = d_merged * gi_ref[0].astype(f32)
    d_mix = (
        d_norm
        - jnp.mean(d_norm, axis=1, keepdims=True)
        - normed * jnp.mean(d_norm * normed, axis=1, keepdims=True)
    )
    dmix_ref[...] = d_mix.astype(bf16)
    masks = lane_masks(2 * head, head)
    scale = 0.5 * head**-0.5 / seq
    for pair in range(HEADS // 2):
        cols = slice(pair * 2 * head, (pair + 1) * 2 * head)
        d_p = dmix_ref[:, cols]
        d_attn = dot_nt(both_heads(d_p, masks), v_ref[0, :, cols])
        d_s = [
            (d_attn[j * seq : (j + 1) * seq] * grad_ref[0, 2 * pair + j].astype(f32)).astype(bf16)
            for j in range(2)
        ]
        attn_t = jnp.concatenate([attn_t_ref[0, 2 * pair], attn_t_ref[0, 2 * pair + 1]], axis=0)
        d_v = pick_lanes(dot_nn(attn_t, d_p), head) * (1.0 / seq)
        d_q = pick_lanes(dot_nn(jnp.concatenate(d_s, axis=0), k_ref[0, :, cols]), head) * scale
        for branch, grad, slope_ref in ((1, d_v, sv_ref), (2, d_q, sq_ref)):
            at = slice(branch * width + pair * 2 * head, branch * width + (pair + 1) * 2 * head)
            d_pre = (grad * slope_ref[0, :, cols].astype(f32)).astype(bf16)
            dpre_ref[0, :, at] = d_pre
            all_ref[here, at] = d_pre
        for j in range(2):
            mine = slice((2 * pair + j) * head, (2 * pair + j + 1) * head)
            d_k = dot_nn(q_t_ref[0, mine], d_s[j]) * scale
            d_pre = (d_k * sk_ref[0, mine].astype(f32)).astype(bf16)
            dk_ref[0, mine] = d_pre
            all_k_ref[mine, here] = d_pre

    @pl.when(step == pl.num_programs(0) - 1)
    def _():
        for copy in copies:
            copy.wait()
        for block in range(5):
            cols = slice(block * width, (block + 1) * width)
            if block == 0:
                part = dot_nn(mt_ref[...], all_enc_ref[...])
            elif block == 4:
                part = dot_nt(xt_ref[...], all_k_ref[...])
            else:
                part = dot_nn(xt_ref[...], all_ref[:, (block - 1) * width : block * width])
            keep_ref[:, cols] = part[:kept].astype(bf16)
            send_ref[:, cols] = part[kept:].astype(bf16)


def layer_backward(denc, w_out, state, xt, mt, kept):
    hist, seq, width = denc.shape
    normed, nu, gi, v, k, q_t, attn_t, grad, slope, slope_t = state
    row = pl.BlockSpec((1, seq, width), lambda i: (i, 0, 0))
    column = pl.BlockSpec((1, width, seq), lambda i: (i, 0, 0))
    slope_spec = lambda b: pl.BlockSpec((1, seq, width), lambda i: (i, 0, b))
    square = pl.BlockSpec((1, HEADS, seq, seq), lambda i: (i, 0, 0, 0))
    raw = pl.BlockSpec(memory_space=pl.ANY)
    rows = hist * seq
    return pl.pallas_call(
        backward_kernel,
        grid=(hist,),
        in_specs=[
            row, whole(w_out.shape), row, row, row, row, row, column, square, square,
            slope_spec(1), slope_spec(2), column, raw, raw,
        ],
        out_specs=[
            pl.BlockSpec((1, seq, 3 * width), lambda i: (i, 0, 0)),
            column,
            whole((kept, 5 * width)),
            whole((width - kept, 5 * width)),
        ],
        out_shape=[
            jax.ShapeDtypeStruct((hist, seq, 3 * width), bf16),
            jax.ShapeDtypeStruct((hist, width, seq), bf16),
            jax.ShapeDtypeStruct((kept, 5 * width), bf16),
            jax.ShapeDtypeStruct((width - kept, 5 * width), bf16),
        ],
        scratch_shapes=[
            pltpu.VMEM((width, rows), bf16),
            pltpu.VMEM((width, rows), bf16),
            pltpu.VMEM((rows, 3 * width), bf16),
            pltpu.VMEM((width, rows), bf16),
            pltpu.VMEM((rows, width), bf16),
            pltpu.VMEM((seq, width), bf16),
            pltpu.SemaphoreType.DMA((2,)),
        ],
        compiler_params=params(60),
        cost_estimate=cost(22e9, 30e6),
        name="layer_backward",
    )(denc, w_out, normed, nu, gi, v, k, q_t, attn_t, grad, slope, slope, slope_t, xt, mt)


def input_kernel(denc_ref, win_ref, dpre_ref, dk_ref, out_ref):
    width = denc_ref.shape[2]
    total = denc_ref[0].astype(f32) + dot_nt(dpre_ref[0], win_ref[:, : 3 * width])
    total = total + dot_nt(jnp.transpose(dk_ref[0]), win_ref[:, 3 * width :])
    out_ref[0] = total.astype(bf16)


def input_backward(denc, w_in, dpre, dk):
    hist, seq, width = denc.shape
    block = lambda a: pl.BlockSpec((1,) + a.shape[1:], lambda i: (i, 0, 0))
    return pl.pallas_call(
        input_kernel,
        grid=(hist,),
        in_specs=[block(denc), whole(w_in.shape), block(dpre), block(dk)],
        out_specs=block(denc),
        out_shape=jax.ShapeDtypeStruct(denc.shape, bf16),
        compiler_params=params(60),
        cost_estimate=cost(6e9, 8e6),
        name="input_backward",
    )(denc, w_in, dpre, dk)


def owner_order(width):
    n_y, n_core, n_z, n_x = (lax.axis_size(a) for a in AXES)
    rows = width // (n_y * n_core * n_z * n_x)
    place = jnp.arange(width, dtype=jnp.int32)
    inner = place % rows
    place = place // rows
    z, place = place % n_z, place // n_z
    x, place = place % n_x, place // n_x
    y, d_core = place % n_y, place // n_y
    core = (lax.axis_index(AXES[1]) + d_core) % n_core
    y, x = (lax.axis_index(AXES[0]) + y) % n_y, (lax.axis_index(AXES[3]) + x) % n_x
    z = (lax.axis_index(AXES[2]) + z) % n_z
    source = (((y * n_core + core) * n_z + z) * n_x + x) * rows + inner
    return (source[:, None] == jnp.arange(width, dtype=jnp.int32)[None, :]).astype(bf16)


def add_up(blocks):
    total = blocks[0].astype(f32)
    for block in blocks[1:]:
        total = total + block.astype(f32)
    return total


def core_stage(keep, send):
    n_core = lax.axis_size(AXES[1])
    step = keep.shape[0]
    parts = [keep]
    for d in range(1, n_core):
        pairs = [(c, (c + d) % n_core) for c in range(n_core)]
        parts.append(lax.ppermute(send[(d - 1) * step : d * step], AXES[1], pairs))
    return add_up(parts).astype(bf16)


def group_stage(blocks, axes):
    count = len(blocks)
    sizes = [lax.axis_size(a) for a in axes]
    parts = [blocks[0]]
    for d in range(1, count):
        pairs = []
        for c in range(count):
            there, stride, rest_c, rest_d = 0, 1, c, d
            for n in reversed(sizes):
                there += (rest_c + rest_d) % n * stride
                stride, rest_c, rest_d = stride * n, rest_c // n, rest_d // n
            pairs.append((c, there))
        parts.append(lax.ppermute(blocks[d], axes, pairs))
    return add_up(parts)


def scatter_rest(rows):
    plane, line = (AXES[0], AXES[3]), (AXES[2],)
    n_plane, n_line = lax.axis_size(plane), lax.axis_size(line)
    columns = rows.shape[1]
    cut = columns * 13 // 20 // 128 * 128
    each = rows.shape[0] // (n_plane * n_line)
    split = rows.reshape(n_plane, n_line, each, columns)
    one = [split[i, :, :, :cut].reshape(n_line * each, cut) for i in range(n_plane)]
    two = [split[:, i, :, cut:].reshape(n_plane * each, columns - cut) for i in range(n_line)]
    one = group_stage(one, plane).astype(bf16)
    two = group_stage(two, line).astype(bf16)
    one = group_stage([one[i * each : (i + 1) * each] for i in range(n_line)], line)
    two = group_stage([two[i * each : (i + 1) * each] for i in range(n_plane)], plane)
    return jnp.concatenate([one, two], axis=1)


def local(histories, weight_in, weight_out, candidates, cotangent, owner_ids, hist_slot, lengths):
    devices = lax.axis_size(AXES)
    imp_rows, width = candidates.shape
    capacity = max(2, 2 * imp_rows // devices)
    slots = devices * capacity
    kept = width // lax.axis_size(AXES[1])
    after = lax.optimization_barrier

    def exchange(rows):
        shaped = rows.reshape(devices, capacity, rows.shape[1])
        moved = lax.all_to_all(shaped, AXES, split_axis=0, concat_axis=0, tiled=True)
        return moved.reshape(slots, rows.shape[1])

    send, pick = route(owner_ids, hist_slot, lengths, candidates, cotangent, devices, capacity)
    recv = exchange(send)
    perm = owner_order(width)
    enc, slope, slope_t, v, q, k, q_t, attn_t, grad, normed, nu, gi, xt, mt = layer_forward(
        histories, weight_in, weight_out, perm
    )
    d_query, d_enc = target_backward(recv, enc)
    returned = exchange(d_query)

    state = (normed, nu, gi, v, k, q_t, attn_t, grad, slope, slope_t)
    dpre, dk, keep, send = layer_backward(d_enc, weight_out, state, xt, mt, kept)
    send, returned = after((send, returned))
    rows = core_stage(keep, send)
    d_enc, rows = after((d_enc, rows))
    d_inputs = input_backward(d_enc, weight_in, dpre, dk)
    total = scatter_rest(rows)
    candidate_grad = lax.dot_general(
        pick, returned, (((0,), (0,)), ((), ())), preferred_element_type=f32
    ).astype(bf16)
    return d_inputs, candidate_grad, total[:, width:], total[:, :width]


def solution(mesh):
    n_hash, n_dp = mesh.devices.shape
    fine = jax.sharding.Mesh(mesh.devices.reshape(n_hash // 2, 2, n_dp // 2, 2), AXES)
    return jax.shard_map(
        local,
        mesh=fine,
        in_specs=(
            P(AXES, None, None),
            P(),
            P(),
            P(AXES, None),
            P(AXES, None),
            P(AXES, None),
            P(AXES),
            P(AXES),
        ),
        out_specs=(
            P(AXES, None, None),
            P(AXES, None),
            P(AXES, None),
            P(AXES, None),
        ),
        check_vma=False,
    )
```

profile of v0, /device:TPU:0, one launch (start us, length us, event | category | flops | bytes accessed | tf_op | source)
XLA Modules:
  0.0 112.2 jit_solution(5551318635996683455)
XLA Ops:
  0.6 2.8 %route.1 = (bf16[512,1152]{1,0:T(8,128)(2,1)}, bf16[512,256]{1,0:T(8,128)(2,1)}) custom-call(s32[1,256]{1,0:T(1,128)} %bitcast.34, s32[1,256]{1,0:T(1,128)} %bitcast.35, s32[1,256]{1,0:T(1,128)} %bitcast.36, bf16[256,512]{1,0:T(8,128)(2,1)} %cand_ref.1, bf16[256,512]{1,0:T(8,128)(2,1)} %cot_ref.1), custom_call_target="tpu_custom_call" | custom-call | flops 2000000000 | bytes 2097152 | tf_op jit(solution)/shard_map/route/pallas_call | solution.py:92
  3.5 7.3 %all-to-all-start = ((bf16[32,16,1152]{2,1,0:T(8,128)(2,1)}), bf16[32,16,1152]{2,1,0:T(8,128)(2,1)S(1)}, u32[]{:S(2)}, u32[]{:S(2)}) async-start(bf16[32,16,1152]{2,1,0:T(8,128)(2,1)} %bitcast.26), calls=%async_computation | async-start | bytes 2359296 | tf_op jit(solution)/shard_map/all_to_all | solution.py:511
  10.8 0.9 fusion.perm_ref
  11.8 14.4 %forward.1 = (bf16[4,256,512]{2,1,0:T(8,128)(2,1)}, bf16[4,256,1536]{2,1,0:T(8,128)(2,1)}, bf16[4,512,256]{2,1,0:T(8,128)(2,1)}, bf16[4,256,512]{2,1,0:T(8,128)(...) custom-call(bf16[4,256,512]{2,1,0:T(8,128)(2,1)} %x_ref.1, ...), custom_call_target="tpu_custom_call" | custom-call | flops 17999998976 | bytes 24000000 | tf_op jit(solution)/shard_map/forward/pallas_call | solution.py:179
  26.1 15.1 %all-to-all-done = bf16[32,16,1152]{2,1,0:T(8,128)(2,1)S(1)} async-done(((bf16[32,16,1152]{2,1,0:T(8,128)(2,1)}), bf16[32,16,1152]{2,1,0:T(8,128)(2,1)S(1)}, u32[]{:S(2)}, u32[]{:S(2)}) %all-to-all-start) | async-done | bytes 1179680 | tf_op jit(solution)/shard_map/all_to_all | solution.py:511
  41.2 0.0 copy-start
  41.2 1.0 copy-done
  42.2 11.8 %target.1 = (bf16[512,512]{1,0:T(8,128)(2,1)}, bf16[4,256,512]{2,1,0:T(8,128)(2,1)}) custom-call(bf16[512,1152]{1,0:T(8,128)(2,1)} %bitcast.25, bf16[4,256,512]{2,1,0:T(8,128)(2,1)} %get-tuple-element.30.enc_ref), custom_call_target="tpu_custom_call" | custom-call | flops 12000000000 | bytes 4000000 | tf_op jit(solution)/shard_map/target/pallas_call | solution.py:279
  54.0 4.6 %all-to-all-start.1 = ((bf16[32,16,512]{2,1,0:T(8,128)(2,1)}), bf16[32,16,512]{2,1,0:T(8,128)(2,1)S(1)}, u32[]{:S(2)}, u32[]{:S(2)}) async-start(bf16[32,16,512]{2,1,0:T(8,128)(2,1)} %bitcast.27), calls=%async_computation.1 | async-start | bytes 1048576 | tf_op jit(solution)/shard_map/all_to_all | solution.py:511
  58.6 0.0 copy-start.1
  58.6 16.6 %layer_backward.1 = (bf16[4,256,1536]{2,1,0:T(8,128)(2,1)}, bf16[4,512,256]{2,1,0:T(8,128)(2,1)}, bf16[256,2560]{1,0:T(8,128)(2,1)}, bf16[256,2560]{1,0:T(8,128)(2,1)}) custom-call(bf16[4,256,512]{2,1,0:T(8,128)(2,1)} %get-tuple-element.48.denc_ref, bf16[512,512]{1,0:T(8,128)(2,1)} %wout_ref.3, bf16[4,256,512]{2,1,0:T(8,128)(2,1)} %get-tuple-element.32.normed_ref, ...), custom_call_target="tpu_custom_call" | custom-call | flops 22000001024 | bytes 30000000 | tf_op jit(solution)/shard_map/layer_backward/pallas_call | solution.py:380
  75.2 0.0 all-to-all-done.1
  75.2 0.3 collective-permute-start
  75.5 0.0 copy-done.1
  75.5 1.0 convolution_convert_fusion
  76.6 2.0 %collective-permute-done = bf16[256,2560]{1,0:T(8,128)(2,1)S(1)} collective-permute-done((bf16[256,2560]{1,0:T(8,128)(2,1)}, bf16[256,2560]{1,0:T(8,128)(2,1)S(1)}, u32[]{:S(2)}, u32[]{:S(2)}) %collective-permute-start) | collective-permute-done | bytes 1310752 | tf_op jit(solution)/shard_map/ppermute | solution.py:465
  78.5 1.7 %add_convert_fusion = bf16[256,2560]{1,0:T(8,128)(2,1)S(1)} fusion(bf16[256,2560]{1,0:T(8,128)(2,1)S(1)} %collective-permute-done, bf16[256,2560]{1,0:T(8,128)(2,1)} %get-tuple-element.44), kind=kLoop, calls=%fused_computation | loop fusion | flops 2621440 | bytes 3932160 | tf_op jit(solution)/shard_map/convert_element_type | solution.py:466
  80.3 0.1 fusion.37
  80.3 3.6 %collective-permute-start.9 = (bf16[64,896]{1,0:T(8,128)(2,1)S(1)}, bf16[64,896]{1,0:T(8,128)(2,1)S(1)}, u32[]{:S(2)}, u32[]{:S(2)}) collective-permute-start(bf16[64,896]{1,0:T(8,128)(2,1)S(1)} %bitcast.33), channel_id=1, source_target_pairs={{0,6},{2,0},{4,2},{6,4},{1,7},{3,1},{5,3},{7,5},{8,14},{10,8},{12,... | collective-permute-start | bytes 344072 | tf_op jit(solution)/shard_map/ppermute | solution.py:481
  84.0 0.0 collective-permute-start.8
  84.0 1.1 collective-permute-start.7
  85.1 2.4 %collective-permute-start.3 = (bf16[64,1664]{1,0:T(8,128)(2,1)S(1)}, bf16[64,1664]{1,0:T(8,128)(2,1)S(1)}, u32[]{:S(2)}, u32[]{:S(2)}) collective-permute-start(bf16[64,1664]{1,0:T(8,128)(2,1)S(1)} %bitcast.30), channel_id=1, source_target_pairs={{0,17},{1,16},{16,1},{17,0},{2,19},{3,18},{18,3},{19,2},{4,21},{5,... | collective-permute-start | bytes 638984 | tf_op jit(solution)/shard_map/ppermute | solution.py:481
  87.5 0.5 collective-permute-start.2
  88.0 6.7 %input_backward.1 = bf16[4,256,512]{2,1,0:T(8,128)(2,1)} custom-call(bf16[4,256,512]{2,1,0:T(8,128)(2,1)} %get-tuple-element.48.denc_ref, bf16[512,2048]{1,0:T(8,128)(2,1)} %win_ref.3, bf16[4,256,1536]{2,1,0:T(8,128)(2,1)} %get-tuple-element.49.dpre_ref, bf16[4,512,256]{2,1,0:T(8,128)(2,1)} %get-tuple-element.50.dk_ref), custom_call_target="tpu_custom_call" | custom-call | flops 6000000000 | bytes 8000000 | tf_op jit(solution)/shard_map/input_backward/pallas_call | solution.py:424
  94.7 0.0 collective-permute-done.9
  94.7 0.6 collective-permute-start.1
  95.2 0.0 collective-permute-done.8
  95.2 0.0 collective-permute-done.7
  95.2 0.1 fusion.6
  95.3 1.5 %collective-permute-start.10 = (bf16[16,896]{1,0:T(8,128)(2,1)S(1)}, bf16[16,896]{1,0:T(8,128)(2,1)S(1)}, u32[]{:S(2)}, u32[]{:S(2)}) collective-permute-start(bf16[16,896]{1,0:T(8,128)(2,1)S(1)} %get-tuple-element.65), channel_id=1, source_target_pairs={{0,1},{1,0},{16,17},{17,16},{2,3},{3,2},{18,19},{19,18},{4,5},{5,4... | collective-permute-start | bytes 86024 | tf_op jit(solution)/shard_map/ppermute | solution.py:481
  96.9 1.5 %collective-permute-start.12 = (bf16[16,896]{1,0:T(8,128)(2,1)S(1)}, bf16[16,896]{1,0:T(8,128)(2,1)S(1)}, u32[]{:S(2)}, u32[]{:S(2)}) collective-permute-start(bf16[16,896]{1,0:T(8,128)(2,1)S(1)} %get-tuple-element.66), channel_id=1, source_target_pairs={{0,17},{1,16},{16,1},{17,0},{2,19},{3,18},{18,3},{19,2},{4,21},{5,... | collective-permute-start | bytes 86024 | tf_op jit(solution)/shard_map/ppermute | solution.py:481
  98.3 0.0 collective-permute-done.3
  98.3 0.6 collective-permute-start.11
  98.9 0.0 collective-permute-done.2
  98.9 2.3 %collective-permute-done.1 = bf16[64,1664]{1,0:T(8,128)(2,1)S(1)} collective-permute-done((bf16[64,1664]{1,0:T(8,128)(2,1)S(1)}, bf16[64,1664]{1,0:T(8,128)(2,1)S(1)}, u32[]{:S(2)}, u32[]{:S(2)}) %collective-permute-start.1) | collective-permute-done | bytes 213024 | tf_op jit(solution)/shard_map/ppermute | solution.py:481
  101.2 0.1 fusion.3
  101.4 2.4 %collective-permute-start.4 = (bf16[16,1664]{1,0:T(8,128)(2,1)S(1)}, bf16[16,1664]{1,0:T(8,128)(2,1)S(1)}, u32[]{:S(2)}, u32[]{:S(2)}) collective-permute-start(bf16[16,1664]{1,0:T(8,128)(2,1)S(1)} %get-tuple-element.62), channel_id=1, source_target_pairs={{0,2},{2,4},{4,6},{6,0},{1,3},{3,5},{5,7},{7,1},{8,10},{10,12},{12... | collective-permute-start | bytes 159752 | tf_op jit(solution)/shard_map/ppermute | solution.py:481
  103.8 1.4 %collective-permute-start.6 = (bf16[16,1664]{1,0:T(8,128)(2,1)S(1)}, bf16[16,1664]{1,0:T(8,128)(2,1)S(1)}, u32[]{:S(2)}, u32[]{:S(2)}) collective-permute-start(bf16[16,1664]{1,0:T(8,128)(2,1)S(1)} %get-tuple-element.63), channel_id=1, source_target_pairs={{0,6},{2,0},{4,2},{6,4},{1,7},{3,1},{5,3},{7,5},{8,14},{10,8},{12,... | collective-permute-start | bytes 159752 | tf_op jit(solution)/shard_map/ppermute | solution.py:481
  105.3 0.0 collective-permute-done.10
  105.3 0.3 collective-permute-start.5
  105.6 0.0 collective-permute-done.12
  105.6 0.0 collective-permute-done.11
  105.6 1.8 %collective-permute-done.4 = bf16[16,1664]{1,0:T(8,128)(2,1)S(1)} collective-permute-done((bf16[16,1664]{1,0:T(8,128)(2,1)S(1)}, bf16[16,1664]{1,0:T(8,128)(2,1)S(1)}, u32[]{:S(2)}, u32[]{:S(2)}) %collective-permute-start.4) | collective-permute-done | bytes 53280 | tf_op jit(solution)/shard_map/ppermute | solution.py:481
  107.4 0.6 collective-permute-done.6
  108.0 2.9 %collective-permute-done.5 = bf16[16,1664]{1,0:T(8,128)(2,1)S(1)} collective-permute-done((bf16[16,1664]{1,0:T(8,128)(2,1)S(1)}, bf16[16,1664]{1,0:T(8,128)(2,1)S(1)}, u32[]{:S(2)}, u32[]{:S(2)}) %collective-permute-start.5) | collective-permute-done | bytes 53280 | tf_op jit(solution)/shard_map/ppermute | solution.py:481
  110.9 0.6 slice.88
  111.5 0.7 pad_maximum_fusion
  (6 shorter events, 0.2 us)
Async XLA Ops:
  3.5 37.7 %all-to-all-start = ((bf16[32,16,1152]{2,1,0:T(8,128)(2,1)}), bf16[32,16,1152]{2,1,0:T(8,128)(2,1)S(1)}, u32[]{:S(2)}, u32[]{:S(2)}) async-start(bf16[32,16,1152]{2,1,0:T(8,128)(2,1)} %bitcast.26), calls=%async_computation | async-start | bytes 2359296 | tf_op jit(solution)/shard_map/all_to_all | solution.py:511
  41.2 1.1 copy-start
  54.0 21.2 %all-to-all-start.1 = ((bf16[32,16,512]{2,1,0:T(8,128)(2,1)}), bf16[32,16,512]{2,1,0:T(8,128)(2,1)S(1)}, u32[]{:S(2)}, u32[]{:S(2)}) async-start(bf16[32,16,512]{2,1,0:T(8,128)(2,1)} %bitcast.27), calls=%async_computation.1 | async-start | bytes 1048576 | tf_op jit(solution)/shard_map/all_to_all | solution.py:511
  58.6 16.9 %copy-start.1 = (bf16[512,256]{1,0:T(8,128)(2,1)S(1)}, bf16[512,256]{1,0:T(8,128)(2,1)}, u32[]{:S(2)}) copy-start(bf16[512,256]{1,0:T(8,128)(2,1)} %get-tuple-element.51) | copy-start | bytes 786436
  75.2 3.3 %collective-permute-start = (bf16[256,2560]{1,0:T(8,128)(2,1)}, bf16[256,2560]{1,0:T(8,128)(2,1)S(1)}, u32[]{:S(2)}, u32[]{:S(2)}) collective-permute-start(bf16[256,2560]{1,0:T(8,128)(2,1)} %get-tuple-element.47), channel_id=1, source_target_pairs={{0,8},{8,0},{1,9},{9,1},{2,10},{10,2},{3,11},{11,3},{4,12},{12,4},... | collective-permute-start | bytes 3932168 | tf_op jit(solution)/shard_map/ppermute | solution.py:465
  80.3 14.3 %collective-permute-start.9 = (bf16[64,896]{1,0:T(8,128)(2,1)S(1)}, bf16[64,896]{1,0:T(8,128)(2,1)S(1)}, u32[]{:S(2)}, u32[]{:S(2)}) collective-permute-start(bf16[64,896]{1,0:T(8,128)(2,1)S(1)} %bitcast.33), channel_id=1, source_target_pairs={{0,6},{2,0},{4,2},{6,4},{1,7},{3,1},{5,3},{7,5},{8,14},{10,8},{12,... | collective-permute-start | bytes 344072 | tf_op jit(solution)/shard_map/ppermute | solution.py:481
  84.0 11.3 %collective-permute-start.8 = (bf16[64,896]{1,0:T(8,128)(2,1)S(1)}, bf16[64,896]{1,0:T(8,128)(2,1)S(1)}, u32[]{:S(2)}, u32[]{:S(2)}) collective-permute-start(bf16[64,896]{1,0:T(8,128)(2,1)S(1)} %bitcast.32), channel_id=1, source_target_pairs={{0,4},{2,6},{4,0},{6,2},{1,5},{3,7},{5,1},{7,3},{8,12},{10,14},{12... | collective-permute-start | bytes 344072 | tf_op jit(solution)/shard_map/ppermute | solution.py:481
  84.0 11.3 %collective-permute-start.7 = (bf16[64,896]{1,0:T(8,128)(2,1)S(1)}, bf16[64,896]{1,0:T(8,128)(2,1)S(1)}, u32[]{:S(2)}, u32[]{:S(2)}) collective-permute-start(bf16[64,896]{1,0:T(8,128)(2,1)S(1)} %bitcast.31), channel_id=1, source_target_pairs={{0,2},{2,4},{4,6},{6,0},{1,3},{3,5},{5,7},{7,1},{8,10},{10,12},{12... | collective-permute-start | bytes 344072 | tf_op jit(solution)/shard_map/ppermute | solution.py:481
  85.1 13.3 %collective-permute-start.3 = (bf16[64,1664]{1,0:T(8,128)(2,1)S(1)}, bf16[64,1664]{1,0:T(8,128)(2,1)S(1)}, u32[]{:S(2)}, u32[]{:S(2)}) collective-permute-start(bf16[64,1664]{1,0:T(8,128)(2,1)S(1)} %bitcast.30), channel_id=1, source_target_pairs={{0,17},{1,16},{16,1},{17,0},{2,19},{3,18},{18,3},{19,2},{4,21},{5,... | collective-permute-start | bytes 638984 | tf_op jit(solution)/shard_map/ppermute | solution.py:481
  87.5 11.4 %collective-permute-start.2 = (bf16[64,1664]{1,0:T(8,128)(2,1)S(1)}, bf16[64,1664]{1,0:T(8,128)(2,1)S(1)}, u32[]{:S(2)}, u32[]{:S(2)}) collective-permute-start(bf16[64,1664]{1,0:T(8,128)(2,1)S(1)} %bitcast.29), channel_id=1, source_target_pairs={{0,16},{1,17},{16,0},{17,1},{2,18},{3,19},{18,2},{19,3},{4,20},{5,... | collective-permute-start | bytes 638984 | tf_op jit(solution)/shard_map/ppermute | solution.py:481
  94.7 6.6 %collective-permute-start.1 = (bf16[64,1664]{1,0:T(8,128)(2,1)S(1)}, bf16[64,1664]{1,0:T(8,128)(2,1)S(1)}, u32[]{:S(2)}, u32[]{:S(2)}) collective-permute-start(bf16[64,1664]{1,0:T(8,128)(2,1)S(1)} %bitcast.28), channel_id=1, source_target_pairs={{0,1},{1,0},{16,17},{17,16},{2,3},{3,2},{18,19},{19,18},{4,5},{5,4... | collective-permute-start | bytes 638984 | tf_op jit(solution)/shard_map/ppermute | solution.py:481
  95.3 9.9 %collective-permute-start.10 = (bf16[16,896]{1,0:T(8,128)(2,1)S(1)}, bf16[16,896]{1,0:T(8,128)(2,1)S(1)}, u32[]{:S(2)}, u32[]{:S(2)}) collective-permute-start(bf16[16,896]{1,0:T(8,128)(2,1)S(1)} %get-tuple-element.65), channel_id=1, source_target_pairs={{0,1},{1,0},{16,17},{17,16},{2,3},{3,2},{18,19},{19,18},{4,5},{5,4... | collective-permute-start | bytes 86024 | tf_op jit(solution)/shard_map/ppermute | solution.py:481
  96.9 8.7 %collective-permute-start.12 = (bf16[16,896]{1,0:T(8,128)(2,1)S(1)}, bf16[16,896]{1,0:T(8,128)(2,1)S(1)}, u32[]{:S(2)}, u32[]{:S(2)}) collective-permute-start(bf16[16,896]{1,0:T(8,128)(2,1)S(1)} %get-tuple-element.66), channel_id=1, source_target_pairs={{0,17},{1,16},{16,1},{17,0},{2,19},{3,18},{18,3},{19,2},{4,21},{5,... | collective-permute-start | bytes 86024 | tf_op jit(solution)/shard_map/ppermute | solution.py:481
  98.3 7.2 %collective-permute-start.11 = (bf16[16,896]{1,0:T(8,128)(2,1)S(1)}, bf16[16,896]{1,0:T(8,128)(2,1)S(1)}, u32[]{:S(2)}, u32[]{:S(2)}) collective-permute-start(bf16[16,896]{1,0:T(8,128)(2,1)S(1)} %get-tuple-element.67), channel_id=1, source_target_pairs={{0,16},{1,17},{16,0},{17,1},{2,18},{3,19},{18,2},{19,3},{4,20},{5,... | collective-permute-start | bytes 86024 | tf_op jit(solution)/shard_map/ppermute | solution.py:481
  101.4 6.0 %collective-permute-start.4 = (bf16[16,1664]{1,0:T(8,128)(2,1)S(1)}, bf16[16,1664]{1,0:T(8,128)(2,1)S(1)}, u32[]{:S(2)}, u32[]{:S(2)}) collective-permute-start(bf16[16,1664]{1,0:T(8,128)(2,1)S(1)} %get-tuple-element.62), channel_id=1, source_target_pairs={{0,2},{2,4},{4,6},{6,0},{1,3},{3,5},{5,7},{7,1},{8,10},{10,12},{12... | collective-permute-start | bytes 159752 | tf_op jit(solution)/shard_map/ppermute | solution.py:481
  103.8 4.1 %collective-permute-start.6 = (bf16[16,1664]{1,0:T(8,128)(2,1)S(1)}, bf16[16,1664]{1,0:T(8,128)(2,1)S(1)}, u32[]{:S(2)}, u32[]{:S(2)}) collective-permute-start(bf16[16,1664]{1,0:T(8,128)(2,1)S(1)} %get-tuple-element.63), channel_id=1, source_target_pairs={{0,6},{2,0},{4,2},{6,4},{1,7},{3,1},{5,3},{7,5},{8,14},{10,8},{12,... | collective-permute-start | bytes 159752 | tf_op jit(solution)/shard_map/ppermute | solution.py:481
  105.3 5.6 %collective-permute-start.5 = (bf16[16,1664]{1,0:T(8,128)(2,1)S(1)}, bf16[16,1664]{1,0:T(8,128)(2,1)S(1)}, u32[]{:S(2)}, u32[]{:S(2)}) collective-permute-start(bf16[16,1664]{1,0:T(8,128)(2,1)S(1)} %get-tuple-element.64), channel_id=1, source_target_pairs={{0,4},{2,6},{4,0},{6,2},{1,5},{3,7},{5,1},{7,3},{8,12},{10,14},{12... | collective-permute-start | bytes 159752 | tf_op jit(solution)/shard_map/ppermute | solution.py:481
where the time goes:
time: 114 us; the launch traced here: 112 us
  Pallas kernels  52.3 us (46%)
  starting transfers between devices  28.1 us (25%)
  waiting for transfers between devices  24.6 us (22%)
  other arithmetic  3.57 us (3%)
  local copies, waits for them, and re-layouts  1.81 us (2%)
    pallas_call x1, Pallas kernels, layer_backward(): pl.pallas_call(backward_kernel, grid=(hist,), in_specs=[row, whole(w_out....  16.6 us
    ppermute x12, starting transfers between devices, group_stage(): parts.append(lax.ppermute(blocks[d], axes, pairs))  16 us
    all_to_all x2, waiting for transfers between devices, exchange(): lax.all_to_all(shaped, AXES, split_axis=0, concat_axis=0, tiled=True)  15.1 us
    pallas_call x1, Pallas kernels, layer_forward(): pl.pallas_call(forward_kernel, grid=(hist,), in_specs=[row, whole(w_in.sh...  14.4 us
    all_to_all x2, starting transfers between devices, exchange(): lax.all_to_all(shaped, AXES, split_axis=0, concat_axis=0, tiled=True)  11.9 us
    pallas_call x1, Pallas kernels, target_backward(): pl.pallas_call(target_kernel, grid=(1,), in_specs=[whole(recv.shape), who...  11.8 us
    ppermute x12, waiting for transfers between devices, group_stage(): parts.append(lax.ppermute(blocks[d], axes, pairs))  7.62 us
    pallas_call x1, Pallas kernels, input_backward(): pl.pallas_call(input_kernel, grid=(hist,), in_specs=[block(denc), whole(w...  6.68 us
  transfers between devices with their start and end apart: 15, of which 6 were waited for; matrix products, arithmetic and copies ran while one was open for 2% of the time, Pallas kernels for 34%

commit v1 on v0

v1 whole, which is shorter than its diff:
```python
import functools

import jax
import jax.numpy as jnp
from jax import lax
from jax.experimental import pallas as pl
from jax.experimental.pallas import tpu as pltpu
from jax.sharding import PartitionSpec as P

HEADS = 8
TILE = 128
META = 128
AXES = ("hash_hi", "core", "dp_hi", "dp_lo")
norm_eps = 1e-05
f32 = jnp.float32
bf16 = jnp.bfloat16
MIB = 1024 * 1024


def dot_nn(a, b):
    return lax.dot_general(a, b, (((1,), (0,)), ((), ())), preferred_element_type=f32)


def dot_nt(a, b):
    return lax.dot_general(a, b, (((1,), (1,)), ((), ())), preferred_element_type=f32)


def dot_tn(a, b):
    return lax.dot_general(a, b, (((0,), (0,)), ((), ())), preferred_element_type=f32)


def iota(shape, axis):
    return lax.broadcasted_iota(jnp.int32, shape, axis)


def silu_pair(half):
    t = jnp.tanh(half)
    u = 1.0 + t
    act = half * u
    return act, u + act * (1.0 - t)


def lane_masks(width, part):
    lane = iota((1, width), 1)
    return [((lane >= j * part) & (lane < (j + 1) * part)).astype(bf16) for j in range(width // part)]


def both_heads(pair, masks):
    return jnp.concatenate([pair * m for m in masks], axis=0)


def pick_lanes(stacked, head):
    rows = stacked.shape[0] // 2
    lane = iota((1, 2 * head), 1)
    return jnp.where(lane < head, stacked[:rows], stacked[rows:])


def params(mib):
    return pltpu.CompilerParams(dimension_semantics=("arbitrary",), vmem_limit_bytes=mib * MIB)


def whole(shape):
    return pl.BlockSpec(shape, lambda i: (0,) * len(shape))


def cost(flops, nbytes, trans=0):
    return pl.CostEstimate(flops=int(flops), bytes_accessed=int(nbytes), transcendentals=int(trans))


def route_kernel(devices, capacity, own_ref, slot_ref, len_ref, cand_ref, cot_ref, send_ref, pick_ref):
    rows, width = cand_ref.shape
    slots = devices * capacity
    own = own_ref[...]
    hot = (own == iota((devices, rows), 0)).astype(f32)
    before = (iota((rows, rows), 0) < iota((rows, rows), 1)).astype(f32).astype(bf16)
    earlier = dot_nn(hot.astype(bf16), before)
    position = jnp.sum(earlier * hot, axis=0, keepdims=True).astype(jnp.int32)
    target = own * capacity + position
    pick = (target == iota((slots, rows), 0)).astype(f32).astype(bf16)
    pick_ref[...] = pick
    send_ref[:, :width] = dot_nn(pick, cand_ref[...]).astype(bf16)
    send_ref[:, width : 2 * width] = dot_nn(pick, cot_ref[...]).astype(bf16)
    line = iota((META, rows), 0)
    meta = jnp.where(line == 0, slot_ref[...], jnp.where(line == 1, len_ref[...], 0))
    send_ref[:, 2 * width :] = dot_nt(pick, meta.astype(f32).astype(bf16)).astype(bf16)


def route(own, slot, length, cand, cot, devices, capacity):
    rows, width = cand.shape
    slots = devices * capacity
    line = whole((1, rows))
    return pl.pallas_call(
        functools.partial(route_kernel, devices, capacity),
        grid=(1,),
        in_specs=[line, line, line, whole(cand.shape), whole(cot.shape)],
        out_specs=[whole((slots, 2 * width + META)), whole((slots, rows))],
        out_shape=(
            jax.ShapeDtypeStruct((slots, 2 * width + META), bf16),
            jax.ShapeDtypeStruct((slots, rows), bf16),
        ),
        compiler_params=params(60),
        cost_estimate=cost(2e9, 4 * rows * width * 4),
        name="route",
    )(own.reshape(1, rows), slot.reshape(1, rows), length.reshape(1, rows), cand, cot)


def forward_kernel(
    x_ref, win_ref, wout_ref, perm_ref,
    enc_ref, slope_ref, slope_t_ref, v_ref, q_ref, k_ref, q_t_ref, attn_t_ref, grad_ref,
    normed_ref, nu_ref, gi_ref, xt_ref, mt_ref,
    gate_ref, mixed_ref, slope_u_ref,
):
    seq, width = x_ref.shape[1:]
    head = width // HEADS
    half_seq = seq // 2
    x = x_ref[0]
    for branch in range(4):
        cols = slice(branch * width, (branch + 1) * width)
        act, slope = silu_pair(0.5 * dot_nn(x, win_ref[:, cols]))
        if branch == 3:
            slope_t_ref[0] = jnp.transpose(0.5 * slope).astype(bf16)
        elif branch > 0:
            slope_ref[0, :, (branch - 1) * width : branch * width] = (0.5 * slope).astype(bf16)
        if branch == 0:
            gate_ref[...] = act
            slope_u_ref[...] = 0.5 * slope
        else:
            (v_ref, q_ref, k_ref)[branch - 1][0] = act.astype(bf16)
        if branch == 2:
            q_t_ref[0] = jnp.transpose(act).astype(bf16)
    masks = lane_masks(2 * head, head)
    scale = 0.5 * head**-0.5
    tri = iota((half_seq, half_seq), 0) >= iota((half_seq, half_seq), 1)
    zero = jnp.zeros((half_seq, half_seq), f32)
    for pair in range(HEADS // 2):
        cols = slice(pair * 2 * head, (pair + 1) * 2 * head)
        q_p = q_ref[0, :, cols] * jnp.asarray(scale, bf16)
        half = dot_nt(both_heads(q_p, masks), k_ref[0, :, cols])
        stack = []
        for j in range(2):
            h = 2 * pair + j
            top = silu_pair(half[j * seq : j * seq + half_seq, :half_seq])
            bot = silu_pair(half[j * seq + half_seq : (j + 1) * seq])
            full = []
            for a, b in zip(top, bot):
                a = jnp.concatenate([jnp.where(tri, a, 0.0), zero], axis=1)
                b = jnp.concatenate([b[:, :half_seq], jnp.where(tri, b[:, half_seq:], 0.0)], axis=1)
                full.append(jnp.concatenate([a, b], axis=0))
            stack.append(full[0].astype(bf16))
            attn_t_ref[0, h] = jnp.transpose(full[0]).astype(bf16)
            grad_ref[0, h] = full[1].astype(bf16)
        mixed = dot_nn(jnp.concatenate(stack, axis=0), v_ref[0, :, cols])
        mixed_ref[:, cols] = pick_lanes(mixed, head) * (1.0 / seq)
    mixed = mixed_ref[...]
    centred = mixed - jnp.mean(mixed, axis=1, keepdims=True)
    inv_std = lax.rsqrt(jnp.mean(centred * centred, axis=1, keepdims=True) + norm_eps)
    normed = centred * inv_std
    gate = gate_ref[...]
    merged = (normed * gate).astype(bf16)
    normed_ref[0] = normed.astype(bf16)
    nu_ref[0] = (normed * slope_u_ref[...]).astype(bf16)
    gi_ref[0] = (gate * inv_std).astype(bf16)
    enc_ref[0] = (x.astype(f32) + dot_nn(merged, wout_ref[...])).astype(bf16)
    perm = perm_ref[...]
    xt_ref[...] = dot_nt(perm, x).astype(bf16)
    mt_ref[...] = dot_nt(perm, merged).astype(bf16)


def layer_forward(x, w_in, w_out, perm):
    hist, seq, width = x.shape
    row = pl.BlockSpec((1, seq, width), lambda i: (i, 0, 0))
    wide = pl.BlockSpec((1, seq, 2 * width), lambda i: (i, 0, 0))
    column = pl.BlockSpec((1, width, seq), lambda i: (i, 0, 0))
    square = pl.BlockSpec((1, HEADS, seq, seq), lambda i: (i, 0, 0, 0))
    turned = pl.BlockSpec((width, seq), lambda i: (0, i))
    row_s = jax.ShapeDtypeStruct((hist, seq, width), bf16)
    column_s = jax.ShapeDtypeStruct((hist, width, seq), bf16)
    square_s = jax.ShapeDtypeStruct((hist, HEADS, seq, seq), bf16)
    turned_s = jax.ShapeDtypeStruct((width, hist * seq), bf16)
    return pl.pallas_call(
        forward_kernel,
        grid=(hist,),
        in_specs=[row, whole(w_in.shape), whole(w_out.shape), whole(perm.shape)],
        out_specs=[
            row, wide, column, row, row, row, column, square, square, row, row, row, turned, turned,
        ],
        out_shape=[
            row_s, jax.ShapeDtypeStruct((hist, seq, 2 * width), bf16), column_s, row_s, row_s, row_s,
            column_s, square_s, square_s, row_s, row_s, row_s, turned_s, turned_s,
        ],
        scratch_shapes=[pltpu.VMEM((seq, width), f32)] * 3,
        compiler_params=params(60),
        cost_estimate=cost(18e9, 24e6),
        name="forward",
    )(x, w_in, w_out, perm)


def group_slots(recv_ref, hist):
    slots, width = recv_ref.shape
    meta = recv_ref[:, width - META :].astype(f32)
    slot_h = meta[:, 0:1]
    valid = meta[:, 1:2] > 0.0
    lane = iota((slots, META), 1).astype(f32)
    hot = jnp.where(valid & (slot_h == lane), 1.0, 0.0)
    lower = (iota((slots, slots), 0) > iota((slots, slots), 1)).astype(f32).astype(bf16)
    rank = jnp.sum(dot_nn(lower, hot.astype(bf16)) * hot, axis=1, keepdims=True)
    starts, start = [], jnp.int32(0)
    begin = jnp.zeros((slots, 1), f32)
    for h in range(hist):
        starts.append(start)
        begin = jnp.where(slot_h == float(h), (start * TILE).astype(f32), begin)
        count = jnp.sum(hot[:, h : h + 1]).astype(jnp.int32)
        start = start + (count + (TILE - 1)) // TILE
    dest = jnp.where(valid, begin + rank, -1.0)
    eye = iota((slots, slots), 0) == iota((slots, slots), 1)
    dest_row = jnp.sum(jnp.where(eye, dest, 0.0), axis=0, keepdims=True).astype(jnp.int32)
    return dest.astype(jnp.int32), dest_row, starts, start


def target_tile(tile, starts, dest_row, recv_ref, enc_ref, grouped_ref, turned_ref):
    seq, width = enc_ref.shape[1:]
    head = width // HEADS
    masks = lane_masks(2 * head, head)
    scale = 0.5 * head**-0.5
    base = pl.multiple_of(tile * TILE, TILE)
    hist = jnp.int32(0)
    for start in starts[1:]:
        hist = hist + (tile >= start).astype(jnp.int32)
    choose = (iota((TILE, dest_row.shape[1]), 0) + base == dest_row).astype(f32).astype(bf16)
    rows = dot_nn(choose, recv_ref[...])
    q_all = rows[:, :width] * scale
    g_all = rows[:, width : 2 * width]
    q_t = jnp.transpose(q_all).astype(bf16)
    g_t = jnp.transpose(g_all).astype(bf16)
    q_all = q_all.astype(bf16)
    g_all = g_all.astype(bf16)
    length = rows[:, 2 * width + 1 : 2 * width + 2]
    positions = iota((TILE, seq), 1).astype(f32)
    weight = jnp.where(positions < length, 1.0 / jnp.maximum(length, 1.0), 0.0)
    for pair in range(HEADS // 2):
        cols = slice(pair * 2 * head, (pair + 1) * 2 * head)
        k_p = enc_ref[hist, :, cols]
        both = dot_nt(
            jnp.concatenate(
                [both_heads(q_all[:, cols], masks), both_heads(g_all[:, cols], masks)], axis=0
            ),
            k_p,
        )
        slopes = []
        for j in range(2):
            h = 2 * pair + j
            mine = slice(h * head, (h + 1) * head)
            act, slope = silu_pair(both[j * TILE : (j + 1) * TILE])
            d_attn = both[(2 + j) * TILE : (3 + j) * TILE]
            attn = (act * weight).astype(bf16)
            d_s = (d_attn * weight * slope).astype(bf16)
            turned_ref[hist, mine, :] += dot_nn(
                jnp.concatenate([g_t[mine], q_t[mine]], axis=1),
                jnp.concatenate([attn, d_s], axis=0),
            )
            slopes.append(d_s)
        d_q = pick_lanes(dot_nn(jnp.concatenate(slopes, axis=0), k_p), head)
        grouped_ref[pl.ds(base, TILE), cols] = (d_q * scale).astype(bf16)


def history_backward(
    at, denc_ref, wout_ref, normed_ref, nu_ref, gi_ref, v_ref, k_ref, q_t_ref, attn_t_ref, grad_ref,
    slope_ref, slope_t_ref, dmix_ref, dpre_ref, dk_ref,
):
    seq, width = denc_ref.shape[1:]
    head = width // HEADS
    here = pl.ds(pl.multiple_of(at * seq, seq), seq)
    d_merged = dot_nt(denc_ref[at], wout_ref[...])
    dpre_ref[here, :width] = (d_merged * nu_ref[at].astype(f32)).astype(bf16)
    normed = normed_ref[at].astype(f32)
    d_norm = d_merged * gi_ref[at].astype(f32)
    d_mix = (
        d_norm
        - jnp.mean(d_norm, axis=1, keepdims=True)
        - normed * jnp.mean(d_norm * normed, axis=1, keepdims=True)
    )
    dmix_ref[...] = d_mix.astype(bf16)
    masks = lane_masks(2 * head, head)
    scale = 0.5 * head**-0.5 / seq
    for pair in range(HEADS // 2):
        cols = slice(pair * 2 * head, (pair + 1) * 2 * head)
        d_p = dmix_ref[:, cols]
        d_attn = dot_nt(both_heads(d_p, masks), v_ref[at, :, cols])
        d_s = [
            (d_attn[j * seq : (j + 1) * seq] * grad_ref[at, 2 * pair + j].astype(f32)).astype(bf16)
            for j in range(2)
        ]
        attn_t = jnp.concatenate([attn_t_ref[at, 2 * pair], attn_t_ref[at, 2 * pair + 1]], axis=0)
        d_v = pick_lanes(dot_nn(attn_t, d_p), head) * (1.0 / seq)
        d_q = pick_lanes(dot_nn(jnp.concatenate(d_s, axis=0), k_ref[at, :, cols]), head) * scale
        for branch, grad in ((0, d_v), (1, d_q)):
            old = slice(branch * width + pair * 2 * head, branch * width + (pair + 1) * 2 * head)
            new = slice(old.start + width, old.stop + width)
            dpre_ref[here, new] = (grad * slope_ref[at, :, old].astype(f32)).astype(bf16)
        for j in range(2):
            mine = slice((2 * pair + j) * head, (2 * pair + j + 1) * head)
            d_k = dot_nn(q_t_ref[at, mine], d_s[j]) * scale
            dk_ref[mine, here] = (d_k * slope_t_ref[at, mine].astype(f32)).astype(bf16)


def owner_kernel(*refs):
    n_in, n_out = 15, 6
    sources, outs, refs = refs[:n_in], refs[n_in : n_in + n_out], refs[n_in + n_out :]
    held, refs = refs[:n_in], refs[n_in:]
    (
        recv_ref, enc_ref, wout_ref, normed_ref, nu_ref, gi_ref, v_ref, k_ref, q_t_ref,
        attn_t_ref, grad_ref, slope_ref, slope_t_ref, mt_ref, xt_ref,
    ) = held
    grouped_ref, turned_ref, dmix_ref, dq_ref, denc_ref, dpre_ref, dk_ref, keep_ref, send_ref, sem_in, sem_out = refs
    dq_hbm, denc_hbm, dpre_hbm, dk_hbm, keep_hbm, send_hbm = outs
    hist, seq, width = enc_ref.shape
    slots, padded = recv_ref.shape[0], grouped_ref.shape[0]
    kept = keep_ref.shape[0]
    loads = [
        pltpu.make_async_copy(source, held[i], sem_in.at[i]) for i, source in enumerate(sources)
    ]
    for load in loads:
        load.start()
    grouped_ref[...] = jnp.zeros_like(grouped_ref)
    turned_ref[...] = jnp.zeros_like(turned_ref)
    loads[0].wait()
    dest, dest_row, starts, tiles = group_slots(recv_ref, hist)
    loads[1].wait()

    def one_tile(tile, carry):
        target_tile(tile, starts, dest_row, recv_ref, enc_ref, grouped_ref, turned_ref)
        return carry

    lax.fori_loop(0, tiles, one_tile, 0)
    back = (dest == iota((slots, padded), 1)).astype(f32).astype(bf16)
    dq_ref[...] = dot_nn(back, grouped_ref[...]).astype(bf16)
    for h in range(hist):
        denc_ref[h] = jnp.transpose(turned_ref[h]).astype(bf16)
    stores = [
        pltpu.make_async_copy(dq_ref, dq_hbm, sem_out.at[0]),
        pltpu.make_async_copy(denc_ref, denc_hbm, sem_out.at[1]),
    ]
    for store in stores:
        store.start()
    for load in loads[2:]:
        load.wait()

    def one_history(at, carry):
        history_backward(
            at, denc_ref, wout_ref, normed_ref, nu_ref, gi_ref, v_ref, k_ref, q_t_ref, attn_t_ref,
            grad_ref, slope_ref, slope_t_ref, dmix_ref, dpre_ref, dk_ref,
        )
        return carry

    lax.fori_loop(0, hist, one_history, 0)
    late = [
        pltpu.make_async_copy(dpre_ref, dpre_hbm, sem_out.at[2]),
        pltpu.make_async_copy(dk_ref, dk_hbm, sem_out.at[3]),
    ]
    for store in late:
        store.start()
    stores += late
    for block in range(5):
        cols = slice(block * width, (block + 1) * width)
        if block == 0:
            part = dot_nn(mt_ref[...], denc_ref[...].reshape(hist * seq, width))
        elif block == 4:
            part = dot_nt(xt_ref[...], dk_ref[...])
        else:
            part = dot_nn(xt_ref[...], dpre_ref[:, (block - 1) * width : block * width])
        for half, (ref, hbm) in enumerate(((keep_ref, keep_hbm), (send_ref, send_hbm))):
            ref[:, cols] = (part[:kept] if half == 0 else part[kept:]).astype(bf16)
            store = pltpu.make_async_copy(
                ref.at[:, cols], hbm.at[:, cols], sem_out.at[4 + 2 * block + half]
            )
            store.start()
            stores.append(store)
    for store in stores:
        store.wait()


def owner_backward(recv, enc, w_out, state, mt, xt, kept):
    hist, seq, width = enc.shape
    slots = recv.shape[0]
    rows = hist * seq
    padded = ((slots - hist) // TILE + hist) * TILE
    operands = (recv, enc, w_out) + state + (mt, xt)
    raw = pl.BlockSpec(memory_space=pl.ANY)
    outs = [
        jax.ShapeDtypeStruct((slots, width), bf16),
        jax.ShapeDtypeStruct(enc.shape, bf16),
        jax.ShapeDtypeStruct((rows, 3 * width), bf16),
        jax.ShapeDtypeStruct((width, rows), bf16),
        jax.ShapeDtypeStruct((kept, 5 * width), bf16),
        jax.ShapeDtypeStruct((width - kept, 5 * width), bf16),
    ]
    return pl.pallas_call(
        owner_kernel,
        grid=(1,),
        in_specs=[raw] * len(operands),
        out_specs=[raw] * len(outs),
        out_shape=outs,
        scratch_shapes=[pltpu.VMEM(a.shape, a.dtype) for a in operands]
        + [
            pltpu.VMEM((padded, width), bf16),
            pltpu.VMEM((hist, width, seq), f32),
            pltpu.VMEM((seq, width), bf16),
        ]
        + [pltpu.VMEM(a.shape, a.dtype) for a in outs]
        + [pltpu.SemaphoreType.DMA((len(operands),)), pltpu.SemaphoreType.DMA((14,))],
        compiler_params=params(60),
        cost_estimate=cost(30e9, 30e6),
        name="owner_backward",
    )(*operands)


def input_kernel(denc_ref, win_ref, dpre_ref, dk_ref, out_ref):
    width = denc_ref.shape[2]
    total = denc_ref[0].astype(f32) + dot_nt(dpre_ref[...], win_ref[:, : 3 * width])
    total = total + dot_nt(jnp.transpose(dk_ref[...]), win_ref[:, 3 * width :])
    out_ref[0] = total.astype(bf16)


def input_backward(denc, w_in, dpre, dk):
    hist, seq, width = denc.shape
    block = lambda a: pl.BlockSpec((1,) + a.shape[1:], lambda i: (i, 0, 0))
    return pl.pallas_call(
        input_kernel,
        grid=(hist,),
        in_specs=[
            block(denc),
            whole(w_in.shape),
            pl.BlockSpec((seq, 3 * width), lambda i: (i, 0)),
            pl.BlockSpec((width, seq), lambda i: (0, i)),
        ],
        out_specs=block(denc),
        out_shape=jax.ShapeDtypeStruct(denc.shape, bf16),
        compiler_params=params(60),
        cost_estimate=cost(6e9, 8e6),
        name="input_backward",
    )(denc, w_in, dpre, dk)


def owner_order(width):
    n_y, n_core, n_z, n_x = (lax.axis_size(a) for a in AXES)
    rows = width // (n_y * n_core * n_z * n_x)
    place = jnp.arange(width, dtype=jnp.int32)
    inner = place % rows
    place = place // rows
    z, place = place % n_z, place // n_z
    x, place = place % n_x, place // n_x
    y, d_core = place % n_y, place // n_y
    core = (lax.axis_index(AXES[1]) + d_core) % n_core
    y, x = (lax.axis_index(AXES[0]) + y) % n_y, (lax.axis_index(AXES[3]) + x) % n_x
    z = (lax.axis_index(AXES[2]) + z) % n_z
    source = (((y * n_core + core) * n_z + z) * n_x + x) * rows + inner
    return (source[:, None] == jnp.arange(width, dtype=jnp.int32)[None, :]).astype(bf16)


def add_up(blocks):
    total = blocks[0].astype(f32)
    for block in blocks[1:]:
        total = total + block.astype(f32)
    return total


def core_stage(keep, send):
    n_core = lax.axis_size(AXES[1])
    step = keep.shape[0]
    parts = [keep]
    for d in range(1, n_core):
        pairs = [(c, (c + d) % n_core) for c in range(n_core)]
        parts.append(lax.ppermute(send[(d - 1) * step : d * step], AXES[1], pairs))
    return add_up(parts).astype(bf16)


def send_blocks(rows, axes):
    count = lax.axis_size(axes)
    step = rows.shape[0] // count
    sizes = [lax.axis_size(a) for a in axes]
    parts = [rows[:step]]
    for d in range(1, count):
        pairs = []
        for c in range(count):
            there, stride, rest_c, rest_d = 0, 1, c, d
            for n in reversed(sizes):
                there += (rest_c + rest_d) % n * stride
                stride, rest_c, rest_d = stride * n, rest_c // n, rest_d // n
            pairs.append((c, there))
        parts.append(lax.ppermute(rows[d * step : (d + 1) * step], axes, pairs))
    return parts


def local(histories, weight_in, weight_out, candidates, cotangent, owner_ids, hist_slot, lengths):
    devices = lax.axis_size(AXES)
    imp_rows, width = candidates.shape
    capacity = max(2, 2 * imp_rows // devices)
    slots = devices * capacity
    kept = width // lax.axis_size(AXES[1])
    after = lax.optimization_barrier

    def exchange(rows):
        shaped = rows.reshape(devices, capacity, rows.shape[1])
        moved = lax.all_to_all(shaped, AXES, split_axis=0, concat_axis=0, tiled=True)
        return moved.reshape(slots, rows.shape[1])

    send, pick = route(owner_ids, hist_slot, lengths, candidates, cotangent, devices, capacity)
    recv = exchange(send)
    perm = owner_order(width)
    enc, slope, slope_t, v, q, k, q_t, attn_t, grad, normed, nu, gi, xt, mt = layer_forward(
        histories, weight_in, weight_out, perm
    )
    state = (normed, nu, gi, v, k, q_t, attn_t, grad, slope, slope_t)
    d_query, d_enc, dpre, dk, keep, send = owner_backward(recv, enc, weight_out, state, mt, xt, kept)
    returned = exchange(d_query)
    rows = core_stage(keep, send)
    d_enc, rows = after((d_enc, rows))
    d_inputs = input_backward(d_enc, weight_in, dpre, dk)
    parts = send_blocks(rows, (AXES[0], AXES[3]))
    parts, d_inputs, returned = after((parts, d_inputs, returned))
    total = add_up(send_blocks(add_up(parts).astype(bf16), (AXES[2],)))
    candidate_grad = lax.dot_general(
        pick, returned, (((0,), (0,)), ((), ())), preferred_element_type=f32
    ).astype(bf16)
    return d_inputs, candidate_grad, total[:, width:], total[:, :width]


def solution(mesh):
    n_hash, n_dp = mesh.devices.shape
    fine = jax.sharding.Mesh(mesh.devices.reshape(n_hash // 2, 2, n_dp // 2, 2), AXES)
    return jax.shard_map(
        local,
        mesh=fine,
        in_specs=(
            P(AXES, None, None),
            P(),
            P(),
            P(AXES, None),
            P(AXES, None),
            P(AXES, None),
            P(AXES),
            P(AXES),
        ),
        out_specs=(
            P(AXES, None, None),
            P(AXES, None),
            P(AXES, None),
            P(AXES, None),
        ),
        check_vma=False,
    )
```

time: 114 us -> 105 us (0.921); the launches traced: 112 us -> 105 us
  starting transfers between devices: 28.1 us -> 18 us
  waiting for transfers between devices: 24.6 us -> 33 us
  Pallas kernels: 52.3 us -> 46.6 us
    ppermute x12 -> x6, starting transfers between devices: 16 us -> 7.73 us  [send_blocks(): parts.append(lax.ppermute(rows[d * step:(d + 1) * step], axes, pairs))]
    ppermute x12 -> x6, waiting for transfers between devices: 7.62 us -> 13.7 us  [send_blocks(): parts.append(lax.ppermute(rows[d * step:(d + 1) * step], axes, pairs))]
    pallas_call x2 -> x1, Pallas kernels: 28.4 us -> 22.8 us  [owner_backward(): pl.pallas_call(owner_kernel, grid=(1,), in_specs=[raw] * len(operands), o...]
    all_to_all x2, waiting for transfers between devices: 15.1 us -> 19.1 us  [exchange(): lax.all_to_all(shaped, AXES, split_axis=0, concat_axis=0, tiled=True)]
    ppermute x1, waiting for transfers between devices: 1.97 us -> 0.27 us  [core_stage(): parts.append(lax.ppermute(send[(d - 1) * step:d * step], AXES[1], pairs))]
    all_to_all x2, starting transfers between devices: 11.9 us -> 10.2 us  [exchange(): lax.all_to_all(shaped, AXES, split_axis=0, concat_axis=0, tiled=True)]
  transfers between devices with their start and end apart: 15 -> 9, of which waited for: 6 -> 9; matrix products, arithmetic and copies ran while one was open for 2% -> 4% of each run, Pallas kernels for 34% -> 20%
where the time goes in v1:
time: 105 us
  Pallas kernels  46.6 us (44%)
  waiting for transfers between devices  33 us (31%)
  starting transfers between devices  18 us (17%)
  other arithmetic  2.83 us (3%)
  local copies, waits for them, and re-layouts  2.43 us (2%)
    pallas_call x1, Pallas kernels, owner_backward(): pl.pallas_call(owner_kernel, grid=(1,), in_specs=[raw] * len(operands), o...  22.8 us
    all_to_all x2, waiting for transfers between devices, exchange(): lax.all_to_all(shaped, AXES, split_axis=0, concat_axis=0, tiled=True)  19.1 us
    pallas_call x1, Pallas kernels, layer_forward(): pl.pallas_call(forward_kernel, grid=(hist,), in_specs=[row, whole(w_in.sh...  14.2 us
    ppermute x6, waiting for transfers between devices, send_blocks(): parts.append(lax.ppermute(rows[d * step:(d + 1) * step], axes, pairs))  13.7 us
    all_to_all x2, starting transfers between devices, exchange(): lax.all_to_all(shaped, AXES, split_axis=0, concat_axis=0, tiled=True)  10.2 us
    ppermute x6, starting transfers between devices, send_blocks(): parts.append(lax.ppermute(rows[d * step:(d + 1) * step], axes, pairs))  7.73 us
    pallas_call x1, Pallas kernels, input_backward(): pl.pallas_call(input_kernel, grid=(hist,), in_specs=[block(denc), whole(w...  6.68 us
    pallas_call x1, Pallas kernels, route(): pl.pallas_call(functools.partial(route_kernel, devices, capacity), grid=(...  2.9 us
  transfers between devices with their start and end apart: 9, of which 9 were waited for; matrix products, arithmetic and copies ran while one was open for 4% of the time, Pallas kernels for 20%

profile of v1, /device:TPU:0, one launch (start us, length us, event | category | flops | bytes accessed | tf_op | source)
XLA Modules:
  0.0 104.7 jit_solution(2840253999956486194)
XLA Ops:
  0.6 2.9 %route.1 = (bf16[512,1152]{1,0:T(8,128)(2,1)}, bf16[512,256]{1,0:T(8,128)(2,1)}) custom-call(s32[1,256]{1,0:T(1,128)} %bitcast.13, s32[1,256]{1,0:T(1,128)} %bitcast.14, s32[1,256]{1,0:T(1,128)} %bitcast.15, bf16[256,512]{1,0:T(8,128)(2,1)} %cand_ref.1, bf16[256,512]{1,0:T(8,128)(2,1)} %cot_ref.1), custom_call_target="tpu_custom_call" | custom-call | flops 2000000000 | bytes 2097152 | tf_op jit(solution)/shard_map/route/pallas_call | solution.py:92
  3.5 7.3 %all-to-all-start = ((bf16[32,16,1152]{2,1,0:T(8,128)(2,1)}), bf16[32,16,1152]{2,1,0:T(8,128)(2,1)S(1)}, u32[]{:S(2)}, u32[]{:S(2)}) async-start(bf16[32,16,1152]{2,1,0:T(8,128)(2,1)} %bitcast.11), calls=%async_computation | async-start | bytes 2359296 | tf_op jit(solution)/shard_map/all_to_all | solution.py:504
  10.9 1.0 fusion.perm_ref
  11.8 14.2 %forward.1 = (bf16[4,256,512]{2,1,0:T(8,128)(2,1)}, bf16[4,256,1024]{2,1,0:T(8,128)(2,1)}, bf16[4,512,256]{2,1,0:T(8,128)(2,1)}, bf16[4,256,512]{2,1,0:T(8,128)(...) custom-call(bf16[4,256,512]{2,1,0:T(8,128)(2,1)} %x_ref.1, ...), custom_call_target="tpu_custom_call" | custom-call | flops 17999998976 | bytes 24000000 | tf_op jit(solution)/shard_map/forward/pallas_call | solution.py:180
  26.1 15.2 %all-to-all-done = bf16[32,16,1152]{2,1,0:T(8,128)(2,1)S(1)} async-done(((bf16[32,16,1152]{2,1,0:T(8,128)(2,1)}), bf16[32,16,1152]{2,1,0:T(8,128)(2,1)S(1)}, u32[]{:S(2)}, u32[]{:S(2)}) %all-to-all-start) | async-done | bytes 1179680 | tf_op jit(solution)/shard_map/all_to_all | solution.py:504
  41.2 0.0 copy-start
  41.2 1.0 copy-done
  42.3 22.8 %owner_backward.1 = (bf16[512,512]{1,0:T(8,128)(2,1)}, bf16[4,256,512]{2,1,0:T(8,128)(2,1)}, bf16[1024,1536]{1,0:T(8,128)(2,1)}, bf16[512,1024]{1,0:T(8,128)(2,1...) custom-call(bf16[512,1152]{1,0:T(8,128)(2,1)} %bitcast.10, bf16[4,256,512]{2,1,0:T(8,128)(2,1)} %get-tuple-element.34.refs_1_, ...), custom_call_target="tpu_custom_call" | custom-call | flops 30000001024 | bytes 30000000 | tf_op jit(solution)/shard_map/owner_backward/pallas_call | solution.py:397
  65.0 0.1 collective-permute-start
  65.1 3.0 %all-to-all-start.1 = ((bf16[32,16,512]{2,1,0:T(8,128)(2,1)}), bf16[32,16,512]{2,1,0:T(8,128)(2,1)S(1)}, u32[]{:S(2)}, u32[]{:S(2)}) async-start(bf16[32,16,512]{2,1,0:T(8,128)(2,1)} %bitcast.12), calls=%async_computation.1 | async-start | bytes 1048576 | tf_op jit(solution)/shard_map/all_to_all | solution.py:504
  68.1 0.3 collective-permute-done
  68.3 1.6 %add_convert_fusion = bf16[256,2560]{1,0:T(8,128)(2,1)S(1)} fusion(bf16[256,2560]{1,0:T(8,128)(2,1)S(1)} %collective-permute-done, bf16[256,2560]{1,0:T(8,128)(2,1)} %get-tuple-element.48), kind=kLoop, calls=%fused_computation | loop fusion | flops 2621440 | bytes 3932160 | tf_op jit(solution)/shard_map/convert_element_type | solution.py:474
  70.0 0.1 fusion.31
  70.1 2.5 %collective-permute-start.3 = (bf16[64,2560]{1,0:T(8,128)(2,1)S(1)}, bf16[64,2560]{1,0:T(8,128)(2,1)S(1)}, u32[]{:S(2)}, u32[]{:S(2)}) collective-permute-start(bf16[64,2560]{1,0:T(8,128)(2,1)S(1)} %get-tuple-element.62), channel_id=1, source_target_pairs={{0,17},{1,16},{16,1},{17,0},{2,19},{3,18},{18,3},{19,2},{4,21},{5,... | collective-permute-start | bytes 983048 | tf_op jit(solution)/shard_map/ppermute | solution.py:490
  72.6 0.6 collective-permute-start.2
  73.1 0.7 collective-permute-start.1
  73.9 6.7 %input_backward.1 = bf16[4,256,512]{2,1,0:T(8,128)(2,1)} custom-call(bf16[4,256,512]{2,1,0:T(8,128)(2,1)} %get-tuple-element.51.denc_ref, bf16[512,2048]{1,0:T(8,128)(2,1)} %win_ref.3, bf16[1024,1536]{1,0:T(8,128)(2,1)} %get-tuple-element.52.dpre_ref, bf16[512,1024]{1,0:T(8,128)(2,1)} %get-tuple-element.53.dk_ref), custom_call_target="tpu_custom_call" | custom-call | flops 6000000000 | bytes 8000000 | tf_op jit(solution)/shard_map/input_backward/pallas_call | solution.py:427
  80.5 0.0 copy-start.1
  80.5 3.9 %all-to-all-done.1 = bf16[32,16,512]{2,1,0:T(8,128)(2,1)S(1)} async-done(((bf16[32,16,512]{2,1,0:T(8,128)(2,1)}), bf16[32,16,512]{2,1,0:T(8,128)(2,1)S(1)}, u32[]{:S(2)}, u32[]{:S(2)}) %all-to-all-start.1) | async-done | bytes 524320 | tf_op jit(solution)/shard_map/all_to_all | solution.py:504
  84.5 0.9 collective-permute-done.3
  85.3 6.1 %collective-permute-done.2 = bf16[64,2560]{1,0:T(8,128)(2,1)S(1)} collective-permute-done((bf16[64,2560]{1,0:T(8,128)(2,1)S(1)}, bf16[64,2560]{1,0:T(8,128)(2,1)S(1)}, u32[]{:S(2)}, u32[]{:S(2)}) %collective-permute-start.2) | collective-permute-done | bytes 327712 | tf_op jit(solution)/shard_map/ppermute | solution.py:490
  91.4 0.5 collective-permute-done.1
  91.8 0.2 add_convert_fusion.1
  92.0 1.5 %collective-permute-start.4 = (bf16[16,2560]{1,0:T(8,128)(2,1)S(1)}, bf16[16,2560]{1,0:T(8,128)(2,1)S(1)}, u32[]{:S(2)}, u32[]{:S(2)}) collective-permute-start(bf16[16,2560]{1,0:T(8,128)(2,1)S(1)} %get-tuple-element.66), channel_id=1, source_target_pairs={{0,2},{2,4},{4,6},{6,0},{1,3},{3,5},{5,7},{7,1},{8,10},{10,12},{12... | collective-permute-start | bytes 245768 | tf_op jit(solution)/shard_map/ppermute | solution.py:490
  93.5 2.4 %collective-permute-start.6 = (bf16[16,2560]{1,0:T(8,128)(2,1)S(1)}, bf16[16,2560]{1,0:T(8,128)(2,1)S(1)}, u32[]{:S(2)}, u32[]{:S(2)}) collective-permute-start(bf16[16,2560]{1,0:T(8,128)(2,1)S(1)} %get-tuple-element.67), channel_id=1, source_target_pairs={{0,6},{2,0},{4,2},{6,4},{1,7},{3,1},{5,3},{7,5},{8,14},{10,8},{12,... | collective-permute-start | bytes 245768 | tf_op jit(solution)/shard_map/ppermute | solution.py:490
  95.9 0.1 collective-permute-start.5
  96.0 0.0 copy-done.1
  96.0 1.0 convolution_convert_fusion
  97.0 2.2 %collective-permute-done.4 = bf16[16,2560]{1,0:T(8,128)(2,1)S(1)} collective-permute-done((bf16[16,2560]{1,0:T(8,128)(2,1)S(1)}, bf16[16,2560]{1,0:T(8,128)(2,1)S(1)}, u32[]{:S(2)}, u32[]{:S(2)}) %collective-permute-start.4) | collective-permute-done | bytes 81952 | tf_op jit(solution)/shard_map/ppermute | solution.py:490
  99.2 0.2 collective-permute-done.6
  99.4 4.0 %collective-permute-done.5 = bf16[16,2560]{1,0:T(8,128)(2,1)S(1)} collective-permute-done((bf16[16,2560]{1,0:T(8,128)(2,1)S(1)}, bf16[16,2560]{1,0:T(8,128)(2,1)S(1)}, u32[]{:S(2)}, u32[]{:S(2)}) %collective-permute-start.5) | collective-permute-done | bytes 81952 | tf_op jit(solution)/shard_map/ppermute | solution.py:490
  103.4 0.6 slice.45
  104.0 0.7 slice.44
  (3 shorter events, 0.1 us)
Async XLA Ops:
  3.5 37.7 %all-to-all-start = ((bf16[32,16,1152]{2,1,0:T(8,128)(2,1)}), bf16[32,16,1152]{2,1,0:T(8,128)(2,1)S(1)}, u32[]{:S(2)}, u32[]{:S(2)}) async-start(bf16[32,16,1152]{2,1,0:T(8,128)(2,1)} %bitcast.11), calls=%async_computation | async-start | bytes 2359296 | tf_op jit(solution)/shard_map/all_to_all | solution.py:504
  41.2 1.0 copy-start
  65.0 3.3 %collective-permute-start = (bf16[256,2560]{1,0:T(8,128)(2,1)}, bf16[256,2560]{1,0:T(8,128)(2,1)S(1)}, u32[]{:S(2)}, u32[]{:S(2)}) collective-permute-start(bf16[256,2560]{1,0:T(8,128)(2,1)} %get-tuple-element.49), channel_id=1, source_target_pairs={{0,8},{8,0},{1,9},{9,1},{2,10},{10,2},{3,11},{11,3},{4,12},{12,4},... | collective-permute-start | bytes 3932168 | tf_op jit(solution)/shard_map/ppermute | solution.py:473
  65.1 19.4 %all-to-all-start.1 = ((bf16[32,16,512]{2,1,0:T(8,128)(2,1)}), bf16[32,16,512]{2,1,0:T(8,128)(2,1)S(1)}, u32[]{:S(2)}, u32[]{:S(2)}) async-start(bf16[32,16,512]{2,1,0:T(8,128)(2,1)} %bitcast.12), calls=%async_computation.1 | async-start | bytes 1048576 | tf_op jit(solution)/shard_map/all_to_all | solution.py:504
  70.1 15.3 %collective-permute-start.3 = (bf16[64,2560]{1,0:T(8,128)(2,1)S(1)}, bf16[64,2560]{1,0:T(8,128)(2,1)S(1)}, u32[]{:S(2)}, u32[]{:S(2)}) collective-permute-start(bf16[64,2560]{1,0:T(8,128)(2,1)S(1)} %get-tuple-element.62), channel_id=1, source_target_pairs={{0,17},{1,16},{16,1},{17,0},{2,19},{3,18},{18,3},{19,2},{4,21},{5,... | collective-permute-start | bytes 983048 | tf_op jit(solution)/shard_map/ppermute | solution.py:490
  72.6 18.8 %collective-permute-start.2 = (bf16[64,2560]{1,0:T(8,128)(2,1)S(1)}, bf16[64,2560]{1,0:T(8,128)(2,1)S(1)}, u32[]{:S(2)}, u32[]{:S(2)}) collective-permute-start(bf16[64,2560]{1,0:T(8,128)(2,1)S(1)} %get-tuple-element.63), channel_id=1, source_target_pairs={{0,16},{1,17},{16,0},{17,1},{2,18},{3,19},{18,2},{19,3},{4,20},{5,... | collective-permute-start | bytes 983048 | tf_op jit(solution)/shard_map/ppermute | solution.py:490
  73.1 18.7 %collective-permute-start.1 = (bf16[64,2560]{1,0:T(8,128)(2,1)S(1)}, bf16[64,2560]{1,0:T(8,128)(2,1)S(1)}, u32[]{:S(2)}, u32[]{:S(2)}) collective-permute-start(bf16[64,2560]{1,0:T(8,128)(2,1)S(1)} %get-tuple-element.64), channel_id=1, source_target_pairs={{0,1},{1,0},{16,17},{17,16},{2,3},{3,2},{18,19},{19,18},{4,5},{5,4... | collective-permute-start | bytes 983048 | tf_op jit(solution)/shard_map/ppermute | solution.py:490
  80.5 15.5 %copy-start.1 = (bf16[512,256]{1,0:T(8,128)(2,1)S(1)}, bf16[512,256]{1,0:T(8,128)(2,1)}, u32[]{:S(2)}) copy-start(bf16[512,256]{1,0:T(8,128)(2,1)} %get-tuple-element.56) | copy-start | bytes 786436
  92.0 7.1 %collective-permute-start.4 = (bf16[16,2560]{1,0:T(8,128)(2,1)S(1)}, bf16[16,2560]{1,0:T(8,128)(2,1)S(1)}, u32[]{:S(2)}, u32[]{:S(2)}) collective-permute-start(bf16[16,2560]{1,0:T(8,128)(2,1)S(1)} %get-tuple-element.66), channel_id=1, source_target_pairs={{0,2},{2,4},{4,6},{6,0},{1,3},{3,5},{5,7},{7,1},{8,10},{10,12},{12... | collective-permute-start | bytes 245768 | tf_op jit(solution)/shard_map/ppermute | solution.py:490
  93.5 5.8 %collective-permute-start.6 = (bf16[16,2560]{1,0:T(8,128)(2,1)S(1)}, bf16[16,2560]{1,0:T(8,128)(2,1)S(1)}, u32[]{:S(2)}, u32[]{:S(2)}) collective-permute-start(bf16[16,2560]{1,0:T(8,128)(2,1)S(1)} %get-tuple-element.67), channel_id=1, source_target_pairs={{0,6},{2,0},{4,2},{6,4},{1,7},{3,1},{5,3},{7,5},{8,14},{10,8},{12,... | collective-permute-start | bytes 245768 | tf_op jit(solution)/shard_map/ppermute | solution.py:490
  95.9 7.4 %collective-permute-start.5 = (bf16[16,2560]{1,0:T(8,128)(2,1)S(1)}, bf16[16,2560]{1,0:T(8,128)(2,1)S(1)}, u32[]{:S(2)}, u32[]{:S(2)}) collective-permute-start(bf16[16,2560]{1,0:T(8,128)(2,1)S(1)} %get-tuple-element.68), channel_id=1, source_target_pairs={{0,4},{2,6},{4,0},{6,2},{1,5},{3,7},{5,1},{7,3},{8,12},{10,14},{12... | collective-permute-start | bytes 245768 | tf_op jit(solution)/shard_map/ppermute | solution.py:490

commit v2 on v1

--- a/solution.py
+++ b/solution.py
@@ -263,28 +263,33 @@
         grouped_ref[pl.ds(base, TILE), cols] = (d_q * scale).astype(bf16)
 
 
-def history_backward(
-    at, denc_ref, wout_ref, normed_ref, nu_ref, gi_ref, v_ref, k_ref, q_t_ref, attn_t_ref, grad_ref,
-    slope_ref, slope_t_ref, dmix_ref, dpre_ref, dk_ref,
+def norm_backward(denc_ref, wout_ref, normed_ref, nu_ref, gi_ref, dmix_ref, dpre_ref):
+    hist, seq, width = denc_ref.shape
+    for at in range(hist):
+        here = slice(at * seq, (at + 1) * seq)
+        d_merged = dot_nt(denc_ref[at], wout_ref[...])
+        dpre_ref[here, :width] = (d_merged * nu_ref[at].astype(f32)).astype(bf16)
+        normed = normed_ref[at].astype(f32)
+        d_norm = d_merged * gi_ref[at].astype(f32)
+        d_mix = (
+            d_norm
+            - jnp.mean(d_norm, axis=1, keepdims=True)
+            - normed * jnp.mean(d_norm * normed, axis=1, keepdims=True)
+        )
+        dmix_ref[at] = d_mix.astype(bf16)
+
+
+def attention_backward(
+    at, dmix_ref, v_ref, k_ref, q_t_ref, attn_t_ref, grad_ref, slope_ref, slope_t_ref, dpre_ref, dk_ref
 ):
-    seq, width = denc_ref.shape[1:]
+    seq, width = dmix_ref.shape[1:]
     head = width // HEADS
-    here = pl.ds(pl.multiple_of(at * seq, seq), seq)
-    d_merged = dot_nt(denc_ref[at], wout_ref[...])
-    dpre_ref[here, :width] = (d_merged * nu_ref[at].astype(f32)).astype(bf16)
-    normed = normed_ref[at].astype(f32)
-    d_norm = d_merged * gi_ref[at].astype(f32)
-    d_mix = (
-        d_norm
-        - jnp.mean(d_norm, axis=1, keepdims=True)
-        - normed * jnp.mean(d_norm * normed, axis=1, keepdims=True)
-    )
-    dmix_ref[...] = d_mix.astype(bf16)
+    here = slice(at * seq, (at + 1) * seq)
     masks = lane_masks(2 * head, head)
     scale = 0.5 * head**-0.5 / seq
     for pair in range(HEADS // 2):
         cols = slice(pair * 2 * head, (pair + 1) * 2 * head)
-        d_p = dmix_ref[:, cols]
+        d_p = dmix_ref[at, :, cols]
         d_attn = dot_nt(both_heads(d_p, masks), v_ref[at, :, cols])
         d_s = [
             (d_attn[j * seq : (j + 1) * seq] * grad_ref[at, 2 * pair + j].astype(f32)).astype(bf16)
@@ -316,50 +321,55 @@
     hist, seq, width = enc_ref.shape
     slots, padded = recv_ref.shape[0], grouped_ref.shape[0]
     kept = keep_ref.shape[0]
-    loads = [
-        pltpu.make_async_copy(source, held[i], sem_in.at[i]) for i, source in enumerate(sources)
-    ]
-    for load in loads:
-        load.start()
+
+    def load(i, n, at=None):
+        source, dest = (sources[i], held[i]) if at is None else (sources[i].at[at], held[i].at[at])
+        return pltpu.make_async_copy(source, dest, sem_in.at[n])
+
+    first = [load(i, i) for i in range(6)]
+    by_history = [[load(i, i + 7 * at, at) for i in range(6, 13)] for at in range(hist)]
+    last = [load(i, 7 * hist + i - 7) for i in (13, 14)]
+    for copy in first + sum(by_history, []) + last:
+        copy.start()
     grouped_ref[...] = jnp.zeros_like(grouped_ref)
     turned_ref[...] = jnp.zeros_like(turned_ref)
-    loads[0].wait()
+    first[0].wait()
     dest, dest_row, starts, tiles = group_slots(recv_ref, hist)
-    loads[1].wait()
+    first[1].wait()
 
     def one_tile(tile, carry):
         target_tile(tile, starts, dest_row, recv_ref, enc_ref, grouped_ref, turned_ref)
         return carry
 
     lax.fori_loop(0, tiles, one_tile, 0)
+    for h in range(hist):
+        denc_ref[h] = jnp.transpose(turned_ref[h]).astype(bf16)
     back = (dest == iota((slots, padded), 1)).astype(f32).astype(bf16)
     dq_ref[...] = dot_nn(back, grouped_ref[...]).astype(bf16)
-    for h in range(hist):
-        denc_ref[h] = jnp.transpose(turned_ref[h]).astype(bf16)
-    stores = [
-        pltpu.make_async_copy(dq_ref, dq_hbm, sem_out.at[0]),
-        pltpu.make_async_copy(denc_ref, denc_hbm, sem_out.at[1]),
-    ]
-    for store in stores:
-        store.start()
-    for load in loads[2:]:
-        load.wait()
-
-    def one_history(at, carry):
-        history_backward(
-            at, denc_ref, wout_ref, normed_ref, nu_ref, gi_ref, v_ref, k_ref, q_t_ref, attn_t_ref,
-            grad_ref, slope_ref, slope_t_ref, dmix_ref, dpre_ref, dk_ref,
+    stores = []
+
+    def store(source, dest):
+        copy = pltpu.make_async_copy(source, dest, sem_out.at[len(stores)])
+        copy.start()
+        stores.append(copy)
+
+    store(denc_ref, denc_hbm)
+    store(dq_ref, dq_hbm)
+    for copy in first[2:]:
+        copy.wait()
+    norm_backward(denc_ref, wout_ref, normed_ref, nu_ref, gi_ref, dmix_ref, dpre_ref)
+    for at in range(hist):
+        for copy in by_history[at]:
+            copy.wait()
+        attention_backward(
+            at, dmix_ref, v_ref, k_ref, q_t_ref, attn_t_ref, grad_ref, slope_ref, slope_t_ref,
+            dpre_ref, dk_ref,
         )
-        return carry
-
-    lax.fori_loop(0, hist, one_history, 0)
-    late = [
-        pltpu.make_async_copy(dpre_ref, dpre_hbm, sem_out.at[2]),
-        pltpu.make_async_copy(dk_ref, dk_hbm, sem_out.at[3]),
-    ]
-    for store in late:
-        store.start()
-    stores += late
+        here = pl.ds(at * seq, seq)
+        store(dpre_ref.at[here, :], dpre_hbm.at[here, :])
+        store(dk_ref.at[:, here], dk_hbm.at[:, here])
+    for copy in last:
+        copy.wait()
     for block in range(5):
         cols = slice(block * width, (block + 1) * width)
         if block == 0:
@@ -368,15 +378,12 @@
             part = dot_nt(xt_ref[...], dk_ref[...])
         else:
             part = dot_nn(xt_ref[...], dpre_ref[:, (block - 1) * width : block * width])
-        for half, (ref, hbm) in enumerate(((keep_ref, keep_hbm), (send_ref, send_hbm))):
-            ref[:, cols] = (part[:kept] if half == 0 else part[kept:]).astype(bf16)
-            store = pltpu.make_async_copy(
-                ref.at[:, cols], hbm.at[:, cols], sem_out.at[4 + 2 * block + half]
-            )
-            store.start()
-            stores.append(store)
-    for store in stores:
-        store.wait()
+        keep_ref[:, cols] = part[:kept].astype(bf16)
+        send_ref[:, cols] = part[kept:].astype(bf16)
+        store(keep_ref.at[:, cols], keep_hbm.at[:, cols])
+        store(send_ref.at[:, cols], send_hbm.at[:, cols])
+    for copy in stores:
+        copy.wait()
 
 
 def owner_backward(recv, enc, w_out, state, mt, xt, kept):
@@ -404,10 +411,13 @@
         + [
             pltpu.VMEM((padded, width), bf16),
             pltpu.VMEM((hist, width, seq), f32),
-            pltpu.VMEM((seq, width), bf16),
+            pltpu.VMEM((hist, seq, width), bf16),
         ]
         + [pltpu.VMEM(a.shape, a.dtype) for a in outs]
-        + [pltpu.SemaphoreType.DMA((len(operands),)), pltpu.SemaphoreType.DMA((14,))],
+        + [
+            pltpu.SemaphoreType.DMA((7 * hist + 8,)),
+            pltpu.SemaphoreType.DMA((2 * hist + 12,)),
+        ],
         compiler_params=params(60),
         cost_estimate=cost(30e9, 30e6),
         name="owner_backward",
@@ -518,11 +528,13 @@
     d_inputs = input_backward(d_enc, weight_in, dpre, dk)
     parts = send_blocks(rows, (AXES[0], AXES[3]))
     parts, d_inputs, returned = after((parts, d_inputs, returned))
-    total = add_up(send_blocks(add_up(parts).astype(bf16), (AXES[2],)))
+    parts = send_blocks(add_up(parts).astype(bf16), (AXES[2],))
     candidate_grad = lax.dot_general(
         pick, returned, (((0,), (0,)), ((), ())), preferred_element_type=f32
     ).astype(bf16)
-    return d_inputs, candidate_grad, total[:, width:], total[:, :width]
+    w_in_grad = add_up([p[:, width:] for p in parts])
+    w_out_grad = add_up([p[:, :width] for p in parts])
+    return d_inputs, candidate_grad, w_in_grad, w_out_grad
 
 
 def solution(mesh):

time: 105 us -> 105 us (level)
  starting transfers between devices: 18 us -> 20.1 us
  Pallas kernels: 46.6 us -> 44.9 us
  other arithmetic: 2.83 us -> 4.11 us
  local copies, waits for them, and re-layouts: 2.43 us -> 1.15 us
    all_to_all x2, starting transfers between devices: 10.2 us -> 12.1 us  [exchange(): lax.all_to_all(shaped, AXES, split_axis=0, concat_axis=0, tiled=True)]
    pallas_call x1, Pallas kernels: 22.8 us -> 21.1 us  [owner_backward(): pl.pallas_call(owner_kernel, grid=(1,), in_specs=[raw] * len(operands), o...]
    slice x2 -> x0, local copies, waits for them, and re-layouts: 1.28 us -> none  [local(): return (d_inputs, candidate_grad, total[:, width:], total[:, :width])]
    add x1 -> x2, other arithmetic: 0.04 us -> 1.31 us  [add_up(): total = total + block.astype(f32)]
  transfers between devices with their start and end apart: 9 -> 9, of which waited for: 9 -> 8; matrix products, arithmetic and copies ran while one was open for 4% -> 4% of each run, Pallas kernels for 20% -> 20%
where the time goes in v2:
time: 105 us; the launch traced here: 104 us
  Pallas kernels  44.9 us (43%)
  waiting for transfers between devices  32.5 us (31%)
  starting transfers between devices  20.1 us (19%)
  other arithmetic  4.11 us (4%)
  local copies, waits for them, and re-layouts  1.15 us (1%)
    pallas_call x1, Pallas kernels, owner_backward(): pl.pallas_call(owner_kernel, grid=(1,), in_specs=[raw] * len(operands), o...  21.1 us
    all_to_all x2, waiting for transfers between devices, exchange(): lax.all_to_all(shaped, AXES, split_axis=0, concat_axis=0, tiled=True)  19.5 us
    pallas_call x1, Pallas kernels, layer_forward(): pl.pallas_call(forward_kernel, grid=(hist,), in_specs=[row, whole(w_in.sh...  14.2 us
    ppermute x6, waiting for transfers between devices, send_blocks(): parts.append(lax.ppermute(rows[d * step:(d + 1) * step], axes, pairs))  12.9 us
    all_to_all x2, starting transfers between devices, exchange(): lax.all_to_all(shaped, AXES, split_axis=0, concat_axis=0, tiled=True)  12.1 us
    ppermute x6, starting transfers between devices, send_blocks(): parts.append(lax.ppermute(rows[d * step:(d + 1) * step], axes, pairs))  7.89 us
    pallas_call x1, Pallas kernels, input_backward(): pl.pallas_call(input_kernel, grid=(hist,), in_specs=[block(denc), whole(w...  6.68 us
    pallas_call x1, Pallas kernels, route(): pl.pallas_call(functools.partial(route_kernel, devices, capacity), grid=(...  2.9 us
  transfers between devices with their start and end apart: 9, of which 8 were waited for; matrix products, arithmetic and copies ran while one was open for 4% of the time, Pallas kernels for 20%

profile of v2, /device:TPU:0, one launch (start us, length us, event | category | flops | bytes accessed | tf_op | source)
XLA Modules:
  0.0 104.4 jit_solution(12286147348316458870)
XLA Ops:
  0.6 2.9 %route.1 = (bf16[512,1152]{1,0:T(8,128)(2,1)}, bf16[512,256]{1,0:T(8,128)(2,1)}) custom-call(s32[1,256]{1,0:T(1,128)} %bitcast.13, s32[1,256]{1,0:T(1,128)} %bitcast.14, s32[1,256]{1,0:T(1,128)} %bitcast.15, bf16[256,512]{1,0:T(8,128)(2,1)} %cand_ref.1, bf16[256,512]{1,0:T(8,128)(2,1)} %cot_ref.1), custom_call_target="tpu_custom_call" | custom-call | flops 2000000000 | bytes 2097152 | tf_op jit(solution)/shard_map/route/pallas_call | solution.py:92
  3.5 7.3 %all-to-all-start = ((bf16[32,16,1152]{2,1,0:T(8,128)(2,1)}), bf16[32,16,1152]{2,1,0:T(8,128)(2,1)S(1)}, u32[]{:S(2)}, u32[]{:S(2)}) async-start(bf16[32,16,1152]{2,1,0:T(8,128)(2,1)} %bitcast.11), calls=%async_computation | async-start | bytes 2359296 | tf_op jit(solution)/shard_map/all_to_all | solution.py:514
  10.9 1.0 fusion.perm_ref
  11.9 14.2 %forward.1 = (bf16[4,256,512]{2,1,0:T(8,128)(2,1)}, bf16[4,256,1024]{2,1,0:T(8,128)(2,1)}, bf16[4,512,256]{2,1,0:T(8,128)(2,1)}, bf16[4,256,512]{2,1,0:T(8,128)(...) custom-call(bf16[4,256,512]{2,1,0:T(8,128)(2,1)} %x_ref.1, ...), custom_call_target="tpu_custom_call" | custom-call | flops 17999998976 | bytes 24000000 | tf_op jit(solution)/shard_map/forward/pallas_call | solution.py:180
  26.1 15.2 %all-to-all-done = bf16[32,16,1152]{2,1,0:T(8,128)(2,1)S(1)} async-done(((bf16[32,16,1152]{2,1,0:T(8,128)(2,1)}), bf16[32,16,1152]{2,1,0:T(8,128)(2,1)S(1)}, u32[]{:S(2)}, u32[]{:S(2)}) %all-to-all-start) | async-done | bytes 1179680 | tf_op jit(solution)/shard_map/all_to_all | solution.py:514
  41.2 0.0 copy-start
  41.2 1.0 copy-done
  42.3 21.1 %owner_backward.1 = (bf16[512,512]{1,0:T(8,128)(2,1)}, bf16[4,256,512]{2,1,0:T(8,128)(2,1)}, bf16[1024,1536]{1,0:T(8,128)(2,1)}, bf16[512,1024]{1,0:T(8,128)(2,1...) custom-call(bf16[512,1152]{1,0:T(8,128)(2,1)} %bitcast.10, bf16[4,256,512]{2,1,0:T(8,128)(2,1)} %get-tuple-element.34.refs_1_, ...), custom_call_target="tpu_custom_call" | custom-call | flops 30000001024 | bytes 30000000 | tf_op jit(solution)/shard_map/owner_backward/pallas_call | solution.py:404
  63.4 0.1 collective-permute-start
  63.4 4.8 %all-to-all-start.1 = ((bf16[32,16,512]{2,1,0:T(8,128)(2,1)}), bf16[32,16,512]{2,1,0:T(8,128)(2,1)S(1)}, u32[]{:S(2)}, u32[]{:S(2)}) async-start(bf16[32,16,512]{2,1,0:T(8,128)(2,1)} %bitcast.12), calls=%async_computation.1 | async-start | bytes 1048576 | tf_op jit(solution)/shard_map/all_to_all | solution.py:514
  68.2 0.0 collective-permute-done
  68.3 1.6 %add_convert_fusion = bf16[256,2560]{1,0:T(8,128)(2,1)S(1)} fusion(bf16[256,2560]{1,0:T(8,128)(2,1)S(1)} %collective-permute-done, bf16[256,2560]{1,0:T(8,128)(2,1)} %get-tuple-element.48), kind=kLoop, calls=%fused_computation | loop fusion | flops 2621440 | bytes 3932160 | tf_op jit(solution)/shard_map/convert_element_type | solution.py:484
  69.9 0.1 fusion.31
  70.0 2.7 %collective-permute-start.3 = (bf16[64,2560]{1,0:T(8,128)(2,1)S(1)}, bf16[64,2560]{1,0:T(8,128)(2,1)S(1)}, u32[]{:S(2)}, u32[]{:S(2)}) collective-permute-start(bf16[64,2560]{1,0:T(8,128)(2,1)S(1)} %get-tuple-element.62), channel_id=1, source_target_pairs={{0,17},{1,16},{16,1},{17,0},{2,19},{3,18},{18,3},{19,2},{4,21},{5,... | collective-permute-start | bytes 983048 | tf_op jit(solution)/shard_map/ppermute | solution.py:500
  72.7 0.6 collective-permute-start.2
  73.3 0.3 collective-permute-start.1
  73.6 6.7 %input_backward.1 = bf16[4,256,512]{2,1,0:T(8,128)(2,1)} custom-call(bf16[4,256,512]{2,1,0:T(8,128)(2,1)} %get-tuple-element.51.denc_ref, bf16[512,2048]{1,0:T(8,128)(2,1)} %win_ref.3, bf16[1024,1536]{1,0:T(8,128)(2,1)} %get-tuple-element.52.dpre_ref, bf16[512,1024]{1,0:T(8,128)(2,1)} %get-tuple-element.53.dk_ref), custom_call_target="tpu_custom_call" | custom-call | flops 6000000000 | bytes 8000000 | tf_op jit(solution)/shard_map/input_backward/pallas_call | solution.py:437
  80.2 0.0 copy-start.1
  80.2 4.4 %all-to-all-done.1 = bf16[32,16,512]{2,1,0:T(8,128)(2,1)S(1)} async-done(((bf16[32,16,512]{2,1,0:T(8,128)(2,1)}), bf16[32,16,512]{2,1,0:T(8,128)(2,1)S(1)}, u32[]{:S(2)}, u32[]{:S(2)}) %all-to-all-start.1) | async-done | bytes 524320 | tf_op jit(solution)/shard_map/all_to_all | solution.py:514
  84.6 0.8 collective-permute-done.3
  85.4 6.0 %collective-permute-done.2 = bf16[64,2560]{1,0:T(8,128)(2,1)S(1)} collective-permute-done((bf16[64,2560]{1,0:T(8,128)(2,1)S(1)}, bf16[64,2560]{1,0:T(8,128)(2,1)S(1)}, u32[]{:S(2)}, u32[]{:S(2)}) %collective-permute-start.2) | collective-permute-done | bytes 327712 | tf_op jit(solution)/shard_map/ppermute | solution.py:500
  91.4 0.3 collective-permute-done.1
  91.7 0.2 add_convert_fusion.1
  91.9 1.8 %collective-permute-start.4 = (bf16[16,2560]{1,0:T(8,128)(2,1)S(1)}, bf16[16,2560]{1,0:T(8,128)(2,1)S(1)}, u32[]{:S(2)}, u32[]{:S(2)}) collective-permute-start(bf16[16,2560]{1,0:T(8,128)(2,1)S(1)} %get-tuple-element.66), channel_id=1, source_target_pairs={{0,2},{2,4},{4,6},{6,0},{1,3},{3,5},{5,7},{7,1},{8,10},{10,12},{12... | collective-permute-start | bytes 245768 | tf_op jit(solution)/shard_map/ppermute | solution.py:500
  93.7 2.0 %collective-permute-start.6 = (bf16[16,2560]{1,0:T(8,128)(2,1)S(1)}, bf16[16,2560]{1,0:T(8,128)(2,1)S(1)}, u32[]{:S(2)}, u32[]{:S(2)}) collective-permute-start(bf16[16,2560]{1,0:T(8,128)(2,1)S(1)} %get-tuple-element.67), channel_id=1, source_target_pairs={{0,6},{2,0},{4,2},{6,4},{1,7},{3,1},{5,3},{7,5},{8,14},{10,8},{12,... | collective-permute-start | bytes 245768 | tf_op jit(solution)/shard_map/ppermute | solution.py:500
  95.7 0.5 collective-permute-start.5
  96.2 0.0 copy-done.1
  96.2 1.0 convolution_convert_fusion
  97.2 1.8 %collective-permute-done.4 = bf16[16,2560]{1,0:T(8,128)(2,1)S(1)} collective-permute-done((bf16[16,2560]{1,0:T(8,128)(2,1)S(1)}, bf16[16,2560]{1,0:T(8,128)(2,1)S(1)}, u32[]{:S(2)}, u32[]{:S(2)}) %collective-permute-start.4) | collective-permute-done | bytes 81952 | tf_op jit(solution)/shard_map/ppermute | solution.py:500
  99.0 0.7 collective-permute-done.6
  99.7 3.4 %collective-permute-done.5 = bf16[16,2560]{1,0:T(8,128)(2,1)S(1)} collective-permute-done((bf16[16,2560]{1,0:T(8,128)(2,1)S(1)}, bf16[16,2560]{1,0:T(8,128)(2,1)S(1)}, u32[]{:S(2)}, u32[]{:S(2)}) %collective-permute-start.5) | collective-permute-done | bytes 81952 | tf_op jit(solution)/shard_map/ppermute | solution.py:500
  103.1 0.6 convert_add_fusion.1
  103.8 0.7 convert_add_fusion
  (2 shorter events, 0.1 us)
Async XLA Ops:
  3.5 37.7 %all-to-all-start = ((bf16[32,16,1152]{2,1,0:T(8,128)(2,1)}), bf16[32,16,1152]{2,1,0:T(8,128)(2,1)S(1)}, u32[]{:S(2)}, u32[]{:S(2)}) async-start(bf16[32,16,1152]{2,1,0:T(8,128)(2,1)} %bitcast.11), calls=%async_computation | async-start | bytes 2359296 | tf_op jit(solution)/shard_map/all_to_all | solution.py:514
  41.2 1.0 copy-start
  63.4 4.9 %collective-permute-start = (bf16[256,2560]{1,0:T(8,128)(2,1)}, bf16[256,2560]{1,0:T(8,128)(2,1)S(1)}, u32[]{:S(2)}, u32[]{:S(2)}) collective-permute-start(bf16[256,2560]{1,0:T(8,128)(2,1)} %get-tuple-element.49), channel_id=1, source_target_pairs={{0,8},{8,0},{1,9},{9,1},{2,10},{10,2},{3,11},{11,3},{4,12},{12,4},... | collective-permute-start | bytes 3932168 | tf_op jit(solution)/shard_map/ppermute | solution.py:483
  63.4 21.2 %all-to-all-start.1 = ((bf16[32,16,512]{2,1,0:T(8,128)(2,1)}), bf16[32,16,512]{2,1,0:T(8,128)(2,1)S(1)}, u32[]{:S(2)}, u32[]{:S(2)}) async-start(bf16[32,16,512]{2,1,0:T(8,128)(2,1)} %bitcast.12), calls=%async_computation.1 | async-start | bytes 1048576 | tf_op jit(solution)/shard_map/all_to_all | solution.py:514
  70.0 15.4 %collective-permute-start.3 = (bf16[64,2560]{1,0:T(8,128)(2,1)S(1)}, bf16[64,2560]{1,0:T(8,128)(2,1)S(1)}, u32[]{:S(2)}, u32[]{:S(2)}) collective-permute-start(bf16[64,2560]{1,0:T(8,128)(2,1)S(1)} %get-tuple-element.62), channel_id=1, source_target_pairs={{0,17},{1,16},{16,1},{17,0},{2,19},{3,18},{18,3},{19,2},{4,21},{5,... | collective-permute-start | bytes 983048 | tf_op jit(solution)/shard_map/ppermute | solution.py:500
  72.7 18.7 %collective-permute-start.2 = (bf16[64,2560]{1,0:T(8,128)(2,1)S(1)}, bf16[64,2560]{1,0:T(8,128)(2,1)S(1)}, u32[]{:S(2)}, u32[]{:S(2)}) collective-permute-start(bf16[64,2560]{1,0:T(8,128)(2,1)S(1)} %get-tuple-element.63), channel_id=1, source_target_pairs={{0,16},{1,17},{16,0},{17,1},{2,18},{3,19},{18,2},{19,3},{4,20},{5,... | collective-permute-start | bytes 983048 | tf_op jit(solution)/shard_map/ppermute | solution.py:500
  73.3 18.4 %collective-permute-start.1 = (bf16[64,2560]{1,0:T(8,128)(2,1)S(1)}, bf16[64,2560]{1,0:T(8,128)(2,1)S(1)}, u32[]{:S(2)}, u32[]{:S(2)}) collective-permute-start(bf16[64,2560]{1,0:T(8,128)(2,1)S(1)} %get-tuple-element.64), channel_id=1, source_target_pairs={{0,1},{1,0},{16,17},{17,16},{2,3},{3,2},{18,19},{19,18},{4,5},{5,4... | collective-permute-start | bytes 983048 | tf_op jit(solution)/shard_map/ppermute | solution.py:500
  80.2 16.0 %copy-start.1 = (bf16[512,256]{1,0:T(8,128)(2,1)S(1)}, bf16[512,256]{1,0:T(8,128)(2,1)}, u32[]{:S(2)}) copy-start(bf16[512,256]{1,0:T(8,128)(2,1)} %get-tuple-element.56) | copy-start | bytes 786436
  91.9 7.2 %collective-permute-start.4 = (bf16[16,2560]{1,0:T(8,128)(2,1)S(1)}, bf16[16,2560]{1,0:T(8,128)(2,1)S(1)}, u32[]{:S(2)}, u32[]{:S(2)}) collective-permute-start(bf16[16,2560]{1,0:T(8,128)(2,1)S(1)} %get-tuple-element.66), channel_id=1, source_target_pairs={{0,2},{2,4},{4,6},{6,0},{1,3},{3,5},{5,7},{7,1},{8,10},{10,12},{12... | collective-permute-start | bytes 245768 | tf_op jit(solution)/shard_map/ppermute | solution.py:500
  93.7 6.0 %collective-permute-start.6 = (bf16[16,2560]{1,0:T(8,128)(2,1)S(1)}, bf16[16,2560]{1,0:T(8,128)(2,1)S(1)}, u32[]{:S(2)}, u32[]{:S(2)}) collective-permute-start(bf16[16,2560]{1,0:T(8,128)(2,1)S(1)} %get-tuple-element.67), channel_id=1, source_target_pairs={{0,6},{2,0},{4,2},{6,4},{1,7},{3,1},{5,3},{7,5},{8,14},{10,8},{12,... | collective-permute-start | bytes 245768 | tf_op jit(solution)/shard_map/ppermute | solution.py:500
  95.7 7.4 %collective-permute-start.5 = (bf16[16,2560]{1,0:T(8,128)(2,1)S(1)}, bf16[16,2560]{1,0:T(8,128)(2,1)S(1)}, u32[]{:S(2)}, u32[]{:S(2)}) collective-permute-start(bf16[16,2560]{1,0:T(8,128)(2,1)S(1)} %get-tuple-element.68), channel_id=1, source_target_pairs={{0,4},{2,6},{4,0},{6,2},{1,5},{3,7},{5,1},{7,3},{8,12},{10,14},{12... | collective-permute-start | bytes 245768 | tf_op jit(solution)/shard_map/ppermute | solution.py:500

commit v3 on v2

--- a/solution.py
+++ b/solution.py
@@ -1,4 +1,5 @@
 import functools
+import math
 
 import jax
 import jax.numpy as jnp
@@ -67,7 +68,9 @@
     return pl.CostEstimate(flops=int(flops), bytes_accessed=int(nbytes), transcendentals=int(trans))
 
 
-def route_kernel(devices, capacity, own_ref, slot_ref, len_ref, cand_ref, cot_ref, send_ref, pick_ref):
+def route_kernel(sizes, capacity, me_ref, own_ref, slot_ref, len_ref, cand_ref, cot_ref, send_ref, pick_ref):
+    n_y, n_core, n_z, n_x = sizes
+    devices = n_y * n_core * n_z * n_x
     rows, width = cand_ref.shape
     slots = devices * capacity
     own = own_ref[...]
@@ -77,7 +80,13 @@
     position = jnp.sum(earlier * hot, axis=0, keepdims=True).astype(jnp.int32)
     target = own * capacity + position
     pick = (target == iota((slots, rows), 0)).astype(f32).astype(bf16)
-    pick_ref[...] = pick
+    x, z = own % n_x, own // n_x % n_z
+    core, y = own // (n_x * n_z) % n_core, own // (n_x * n_z * n_core)
+    y, core, z, x = (
+        (me_ref[i] - at + n) % n for i, (at, n) in enumerate(zip((y, core, z, x), sizes))
+    )
+    back = (((y * n_x + x) * n_z + z) * n_core + core) * capacity + position
+    pick_ref[...] = (back == iota((slots, rows), 0)).astype(f32).astype(bf16)
     send_ref[:, :width] = dot_nn(pick, cand_ref[...]).astype(bf16)
     send_ref[:, width : 2 * width] = dot_nn(pick, cot_ref[...]).astype(bf16)
     line = iota((META, rows), 0)
@@ -85,14 +94,16 @@
     send_ref[:, 2 * width :] = dot_nt(pick, meta.astype(f32).astype(bf16)).astype(bf16)
 
 
-def route(own, slot, length, cand, cot, devices, capacity):
+def route(me, own, slot, length, cand, cot, sizes, capacity):
     rows, width = cand.shape
-    slots = devices * capacity
+    slots = math.prod(sizes) * capacity
     line = whole((1, rows))
     return pl.pallas_call(
-        functools.partial(route_kernel, devices, capacity),
+        functools.partial(route_kernel, sizes, capacity),
         grid=(1,),
-        in_specs=[line, line, line, whole(cand.shape), whole(cot.shape)],
+        in_specs=[
+            pl.BlockSpec(memory_space=pltpu.SMEM), line, line, line, whole(cand.shape), whole(cot.shape),
+        ],
         out_specs=[whole((slots, 2 * width + META)), whole((slots, rows))],
         out_shape=(
             jax.ShapeDtypeStruct((slots, 2 * width + META), bf16),
@@ -101,7 +112,7 @@
         compiler_params=params(60),
         cost_estimate=cost(2e9, 4 * rows * width * 4),
         name="route",
-    )(own.reshape(1, rows), slot.reshape(1, rows), length.reshape(1, rows), cand, cot)
+    )(me, own.reshape(1, rows), slot.reshape(1, rows), length.reshape(1, rows), cand, cot)
 
 
 def forward_kernel(
@@ -214,7 +225,7 @@
     dest = jnp.where(valid, begin + rank, -1.0)
     eye = iota((slots, slots), 0) == iota((slots, slots), 1)
     dest_row = jnp.sum(jnp.where(eye, dest, 0.0), axis=0, keepdims=True).astype(jnp.int32)
-    return dest.astype(jnp.int32), dest_row, starts, start
+    return dest_row, starts, start
 
 
 def target_tile(tile, starts, dest_row, recv_ref, enc_ref, grouped_ref, turned_ref):
@@ -230,10 +241,10 @@
     rows = dot_nn(choose, recv_ref[...])
     q_all = rows[:, :width] * scale
     g_all = rows[:, width : 2 * width]
-    q_t = jnp.transpose(q_all).astype(bf16)
-    g_t = jnp.transpose(g_all).astype(bf16)
     q_all = q_all.astype(bf16)
     g_all = g_all.astype(bf16)
+    q_t = jnp.transpose(q_all)
+    g_t = jnp.transpose(g_all)
     length = rows[:, 2 * width + 1 : 2 * width + 2]
     positions = iota((TILE, seq), 1).astype(f32)
     weight = jnp.where(positions < length, 1.0 / jnp.maximum(length, 1.0), 0.0)
@@ -308,7 +319,20 @@
             dk_ref[mine, here] = (d_k * slope_t_ref[at, mine].astype(f32)).astype(bf16)
 
 
-def owner_kernel(*refs):
+def return_order(sizes, capacity, me_ref, dest_row):
+    n_y, n_core, n_z, n_x = sizes
+    slots = dest_row.shape[1]
+    place = iota((slots, 1), 0)
+    inner, block = place % capacity, place // capacity
+    x, y = block % n_x, block // n_x % n_y
+    z, core = block // (n_x * n_y) % n_z, block // (n_x * n_y * n_z)
+    y, core, z, x = ((me_ref[i] + at) % n for i, (at, n) in enumerate(zip((y, core, z, x), sizes)))
+    source = (((y * n_core + core) * n_z + z) * n_x + x) * capacity + inner
+    hit = source == iota((slots, slots), 1)
+    return jnp.sum(jnp.where(hit, dest_row.astype(f32), 0.0), axis=1, keepdims=True).astype(jnp.int32)
+
+
+def owner_kernel(sizes, capacity, me_ref, *refs):
     n_in, n_out = 15, 6
     sources, outs, refs = refs[:n_in], refs[n_in : n_in + n_out], refs[n_in + n_out :]
     held, refs = refs[:n_in], refs[n_in:]
@@ -329,21 +353,25 @@
     first = [load(i, i) for i in range(6)]
     by_history = [[load(i, i + 7 * at, at) for i in range(6, 13)] for at in range(hist)]
     last = [load(i, 7 * hist + i - 7) for i in (13, 14)]
-    for copy in first + sum(by_history, []) + last:
+    for copy in first[:2]:
         copy.start()
     grouped_ref[...] = jnp.zeros_like(grouped_ref)
     turned_ref[...] = jnp.zeros_like(turned_ref)
     first[0].wait()
-    dest, dest_row, starts, tiles = group_slots(recv_ref, hist)
     first[1].wait()
+    for copy in first[2:] + sum(by_history, []) + last:
+        copy.start()
+    dest_row, starts, tiles = group_slots(recv_ref, hist)
 
     def one_tile(tile, carry):
         target_tile(tile, starts, dest_row, recv_ref, enc_ref, grouped_ref, turned_ref)
         return carry
 
     lax.fori_loop(0, tiles, one_tile, 0)
+    unit = (iota((seq, seq), 0) == iota((seq, seq), 1)).astype(f32).astype(bf16)
     for h in range(hist):
-        denc_ref[h] = jnp.transpose(turned_ref[h]).astype(bf16)
+        denc_ref[h] = dot_nt(unit, turned_ref[h].astype(bf16)).astype(bf16)
+    dest = return_order(sizes, capacity, me_ref, dest_row)
     back = (dest == iota((slots, padded), 1)).astype(f32).astype(bf16)
     dq_ref[...] = dot_nn(back, grouped_ref[...]).astype(bf16)
     stores = []
@@ -386,7 +414,7 @@
         copy.wait()
 
 
-def owner_backward(recv, enc, w_out, state, mt, xt, kept):
+def owner_backward(me, sizes, recv, enc, w_out, state, mt, xt, kept):
     hist, seq, width = enc.shape
     slots = recv.shape[0]
     rows = hist * seq
@@ -402,9 +430,9 @@
         jax.ShapeDtypeStruct((width - kept, 5 * width), bf16),
     ]
     return pl.pallas_call(
-        owner_kernel,
+        functools.partial(owner_kernel, sizes, slots // math.prod(sizes)),
         grid=(1,),
-        in_specs=[raw] * len(operands),
+        in_specs=[pl.BlockSpec(memory_space=pltpu.SMEM)] + [raw] * len(operands),
         out_specs=[raw] * len(outs),
         out_shape=outs,
         scratch_shapes=[pltpu.VMEM(a.shape, a.dtype) for a in operands]
@@ -421,7 +449,7 @@
         compiler_params=params(60),
         cost_estimate=cost(30e9, 30e6),
         name="owner_backward",
-    )(*operands)
+    )(me, *operands)
 
 
 def input_kernel(denc_ref, win_ref, dpre_ref, dk_ref, out_ref):
@@ -475,20 +503,13 @@
 
 
 def core_stage(keep, send):
-    n_core = lax.axis_size(AXES[1])
-    step = keep.shape[0]
-    parts = [keep]
-    for d in range(1, n_core):
-        pairs = [(c, (c + d) % n_core) for c in range(n_core)]
-        parts.append(lax.ppermute(send[(d - 1) * step : d * step], AXES[1], pairs))
-    return add_up(parts).astype(bf16)
-
-
-def send_blocks(rows, axes):
-    count = lax.axis_size(axes)
-    step = rows.shape[0] // count
+    return add_up(send_blocks([keep] + cut_rows(send, lax.axis_size(AXES[1]) - 1), AXES[1:2])).astype(bf16)
+
+
+def send_blocks(blocks, axes):
+    count = len(blocks)
     sizes = [lax.axis_size(a) for a in axes]
-    parts = [rows[:step]]
+    parts = [blocks[0]]
     for d in range(1, count):
         pairs = []
         for c in range(count):
@@ -497,8 +518,13 @@
                 there += (rest_c + rest_d) % n * stride
                 stride, rest_c, rest_d = stride * n, rest_c // n, rest_d // n
             pairs.append((c, there))
-        parts.append(lax.ppermute(rows[d * step : (d + 1) * step], axes, pairs))
+        parts.append(lax.ppermute(blocks[d], axes, pairs))
     return parts
+
+
+def cut_rows(rows, count):
+    step = rows.shape[0] // count
+    return [rows[i * step : (i + 1) * step] for i in range(count)]
 
 
 def local(histories, weight_in, weight_out, candidates, cotangent, owner_ids, hist_slot, lengths):
@@ -509,26 +535,36 @@
     kept = width // lax.axis_size(AXES[1])
     after = lax.optimization_barrier
 
-    def exchange(rows):
-        shaped = rows.reshape(devices, capacity, rows.shape[1])
-        moved = lax.all_to_all(shaped, AXES, split_axis=0, concat_axis=0, tiled=True)
-        return moved.reshape(slots, rows.shape[1])
-
-    send, pick = route(owner_ids, hist_slot, lengths, candidates, cotangent, devices, capacity)
-    recv = exchange(send)
+    sizes = n_y, n_core, n_z, n_x = tuple(lax.axis_size(a) for a in AXES)
+    me = jnp.stack([lax.axis_index(a) for a in AXES]).astype(jnp.int32)
+    core, line, plane = AXES[1:2], AXES[2:3], (AXES[0], AXES[3])
+    send, pick = route(me, owner_ids, hist_slot, lengths, candidates, cotangent, sizes, capacity)
+    shaped = send.reshape(devices, capacity, send.shape[1])
+    recv = lax.all_to_all(shaped, AXES, split_axis=0, concat_axis=0, tiled=True)
+    recv = recv.reshape(slots, send.shape[1])
     perm = owner_order(width)
     enc, slope, slope_t, v, q, k, q_t, attn_t, grad, normed, nu, gi, xt, mt = layer_forward(
         histories, weight_in, weight_out, perm
     )
     state = (normed, nu, gi, v, k, q_t, attn_t, grad, slope, slope_t)
-    d_query, d_enc, dpre, dk, keep, send = owner_backward(recv, enc, weight_out, state, mt, xt, kept)
-    returned = exchange(d_query)
+    d_query, d_enc, dpre, dk, keep, send = owner_backward(
+        me, sizes, recv, enc, weight_out, state, mt, xt, kept
+    )
     rows = core_stage(keep, send)
-    d_enc, rows = after((d_enc, rows))
+    back = [cut_rows(b, n_z) for b in send_blocks(cut_rows(d_query, n_core), core)]
+    d_enc, rows, back = after((d_enc, rows, back))
+    back = [jnp.concatenate([b[d] for b in back], axis=0) for d in range(n_z)]
     d_inputs = input_backward(d_enc, weight_in, dpre, dk)
-    parts = send_blocks(rows, (AXES[0], AXES[3]))
-    parts, d_inputs, returned = after((parts, d_inputs, returned))
-    parts = send_blocks(add_up(parts).astype(bf16), (AXES[2],))
+    parts = send_blocks(cut_rows(rows, n_y * n_x), plane)
+    back = send_blocks(back, line)
+    parts, back, d_inputs = after((parts, back, d_inputs))
+    parts = send_blocks(cut_rows(add_up(parts).astype(bf16), n_z), line)
+    back = [b.reshape(n_core, n_y * n_x, capacity, width) for b in back]
+    back = [
+        jnp.concatenate([b[:, i].reshape(n_core * capacity, width) for b in back], axis=0)
+        for i in range(n_y * n_x)
+    ]
+    returned = jnp.concatenate(send_blocks(back, plane), axis=0)
     candidate_grad = lax.dot_general(
         pick, returned, (((0,), (0,)), ((), ())), preferred_element_type=f32
     ).astype(bf16)

time: 105 us -> 108 us (1.029)
  waiting for transfers between devices: 32.5 us -> 28.9 us
  Pallas kernels: 44.9 us -> 48.4 us
  local copies, waits for them, and re-layouts: 1.15 us -> 3.26 us
  starting transfers between devices: 20.1 us -> 21.7 us
    ppermute x7 -> x14, starting transfers between devices: 7.96 us -> 14.4 us  [send_blocks(): parts.append(lax.ppermute(blocks[d], axes, pairs))]
    all_to_all x2 -> x1, starting transfers between devices: 12.1 us -> 7.29 us  [local(): recv = lax.all_to_all(shaped, AXES, split_axis=0, concat_axis=0, tiled=True)]
    all_to_all x2 -> x1, waiting for transfers between devices: 19.5 us -> 15.2 us  [local(): recv = lax.all_to_all(shaped, AXES, split_axis=0, concat_axis=0, tiled=True)]
    pallas_call x2, Pallas kernels: 24 us -> 27.5 us  [the longest x1 24.6 us: owner_backward(): pl.pallas_call(functools.partial(owner_kernel, sizes, slots // math.prod(...]
    slice x2 -> x9, local copies, waits for them, and re-layouts: 0.12 us -> 2.18 us  [the longest x5 2.14 us: cut_rows(): return [rows[i * step:(i + 1) * step] for i in range(count)]]
    convert_element_type x2, other arithmetic: 1.79 us -> 0.48 us  [the longest x1 0.32 us: core_stage(): add_up(send_blocks([keep] + cut_rows(send, lax.axis_size(AXES[1]) - 1), A...]
    ppermute x7 -> x14, waiting for transfers between devices: 12.9 us -> 13.7 us  [send_blocks(): parts.append(lax.ppermute(blocks[d], axes, pairs))]
  transfers between devices with their start and end apart: 9 -> 15, of which waited for: 8 -> 8; matrix products, arithmetic and copies ran while one was open for 4% -> 4% of each run, Pallas kernels for 20% -> 19%
where the time goes in v3:
time: 108 us
  Pallas kernels  48.4 us (45%)
  waiting for transfers between devices  28.9 us (27%)
  starting transfers between devices  21.7 us (20%)
  other arithmetic  3.54 us (3%)
  local copies, waits for them, and re-layouts  3.26 us (3%)
    pallas_call x1, Pallas kernels, owner_backward(): pl.pallas_call(functools.partial(owner_kernel, sizes, slots // math.prod(...  24.6 us
    all_to_all x1, waiting for transfers between devices, local(): recv = lax.all_to_all(shaped, AXES, split_axis=0, concat_axis=0, tiled=True)  15.2 us
    ppermute x14, starting transfers between devices, send_blocks(): parts.append(lax.ppermute(blocks[d], axes, pairs))  14.4 us
    pallas_call x1, Pallas kernels, layer_forward(): pl.pallas_call(forward_kernel, grid=(hist,), in_specs=[row, whole(w_in.sh...  14.2 us
    ppermute x14, waiting for transfers between devices, send_blocks(): parts.append(lax.ppermute(blocks[d], axes, pairs))  13.7 us
    all_to_all x1, starting transfers between devices, local(): recv = lax.all_to_all(shaped, AXES, split_axis=0, concat_axis=0, tiled=True)  7.29 us
    pallas_call x1, Pallas kernels, input_backward(): pl.pallas_call(input_kernel, grid=(hist,), in_specs=[block(denc), whole(w...  6.69 us
    pallas_call x1, Pallas kernels, route(): pl.pallas_call(functools.partial(route_kernel, sizes, capacity), grid=(1,...  2.91 us
  transfers between devices with their start and end apart: 15, of which 8 were waited for; matrix products, arithmetic and copies ran while one was open for 4% of the time, Pallas kernels for 19%

profile of v3, /device:TPU:0, one launch (start us, length us, event | category | flops | bytes accessed | tf_op | source)
XLA Modules:
  0.0 107.7 jit_solution(16366529649568902729)
XLA Ops:
  0.6 0.7 pad_add_fusion.me_ref
  1.3 2.9 %route.1 = (bf16[512,1152]{1,0:T(8,128)(2,1)}, bf16[512,256]{1,0:T(8,128)(2,1)}) custom-call(s32[4]{0:T(128)} %pad_add_fusion.me_ref, s32[1,256]{1,0:T(1,128)} %bitcast.53, s32[1,256]{1,0:T(1,128)} %bitcast.54, s32[1,256]{1,0:T(1,128)} %bitcast.55, bf16[256,512]{1,0:T(8,128)(2,1)} %cand_ref.1, bf16[256,512]{1,0:T(8,128)(2,1)} %cot_ref.1), custom_call_target="tpu_custom_call" | custom-call | flops 2000000000 | bytes 2097152 | tf_op jit(solution)/shard_map/route/pallas_call | solution.py:101
  4.2 7.3 %all-to-all-start = ((bf16[32,16,1152]{2,1,0:T(8,128)(2,1)}), bf16[32,16,1152]{2,1,0:T(8,128)(2,1)S(1)}, u32[]{:S(2)}, u32[]{:S(2)}) async-start(bf16[32,16,1152]{2,1,0:T(8,128)(2,1)} %bitcast.32), calls=%async_computation | async-start | bytes 2359296 | tf_op jit(solution)/shard_map/all_to_all | solution.py:543
  11.6 1.0 fusion.perm_ref
  12.5 14.2 %forward.1 = (bf16[4,256,512]{2,1,0:T(8,128)(2,1)}, bf16[4,256,1024]{2,1,0:T(8,128)(2,1)}, bf16[4,512,256]{2,1,0:T(8,128)(2,1)}, bf16[4,256,512]{2,1,0:T(8,128)(...) custom-call(bf16[4,256,512]{2,1,0:T(8,128)(2,1)} %x_ref.1, ...), custom_call_target="tpu_custom_call" | custom-call | flops 17999998976 | bytes 24000000 | tf_op jit(solution)/shard_map/forward/pallas_call | solution.py:191
  26.8 15.2 %all-to-all-done = bf16[32,16,1152]{2,1,0:T(8,128)(2,1)S(1)} async-done(((bf16[32,16,1152]{2,1,0:T(8,128)(2,1)}), bf16[32,16,1152]{2,1,0:T(8,128)(2,1)S(1)}, u32[]{:S(2)}, u32[]{:S(2)}) %all-to-all-start) | async-done | bytes 1179680 | tf_op jit(solution)/shard_map/all_to_all | solution.py:543
  41.9 0.0 copy-start.1
  41.9 1.0 copy-done.1
  42.9 24.6 %owner_backward.1 = (bf16[512,512]{1,0:T(8,128)(2,1)}, bf16[4,256,512]{2,1,0:T(8,128)(2,1)}, bf16[1024,1536]{1,0:T(8,128)(2,1)}, bf16[512,1024]{1,0:T(8,128)(2,1...) custom-call(s32[4]{0:T(128)} %pad_add_fusion.me_ref, bf16[512,1152]{1,0:T(8,128)(2,1)} %bitcast.31, ...), custom_call_target="tpu_custom_call" | custom-call | flops 30000001024 | bytes 30000000 | tf_op jit(solution)/shard_map/owner_backward/pallas_call | solution.py:432
  67.5 0.0 copy-start
  67.5 0.1 collective-permute-start
  67.6 1.1 slice.132
  68.7 0.5 collective-permute-start.1
  69.1 1.0 fusion.32
  70.1 0.9 collective-permute-done.1
  71.0 0.0 collective-permute-done
  71.0 0.0 copy-done
  71.0 0.3 add_convert_fusion
  71.4 0.1 fusion.31
  71.5 0.1 collective-permute-start.7
  71.6 0.1 collective-permute-start.6
  71.7 2.1 %collective-permute-start.5 = (bf16[128,512]{1,0:T(8,128)(2,1)S(1)}, bf16[128,512]{1,0:T(8,128)(2,1)S(1)}, u32[]{:S(2)}, u32[]{:S(2)}) collective-permute-start(bf16[128,512]{1,0:T(8,128)(2,1)S(1)} %pad_maximum_fusion.1), channel_id=1, source_target_pairs={{0,2},{2,4},{4,6},{6,0},{1,3},{3,5},{5,7},{7,1},{8,10},{10,12},{12... | collective-permute-start | bytes 393224 | tf_op jit(solution)/shard_map/ppermute | solution.py:521
  73.7 3.3 %collective-permute-start.4 = (bf16[64,2560]{1,0:T(8,128)(2,1)S(1)}, bf16[64,2560]{1,0:T(8,128)(2,1)S(1)}, u32[]{:S(2)}, u32[]{:S(2)}) collective-permute-start(bf16[64,2560]{1,0:T(8,128)(2,1)S(1)} %get-tuple-element.84), channel_id=1, source_target_pairs={{0,17},{1,16},{16,1},{17,0},{2,19},{3,18},{18,3},{19,2},{4,21},{5,... | collective-permute-start | bytes 983048 | tf_op jit(solution)/shard_map/ppermute | solution.py:521
  77.0 0.0 collective-permute-start.3
  77.0 1.3 %collective-permute-done.7 = bf16[128,512]{1,0:T(8,128)(2,1)S(1)} collective-permute-done((bf16[128,512]{1,0:T(8,128)(2,1)S(1)}, bf16[128,512]{1,0:T(8,128)(2,1)S(1)}, u32[]{:S(2)}, u32[]{:S(2)}) %collective-permute-start.7) | collective-permute-done | bytes 131104 | tf_op jit(solution)/shard_map/ppermute | solution.py:521
  78.3 0.0 collective-permute-start.2
  78.3 6.7 %input_backward.1 = bf16[4,256,512]{2,1,0:T(8,128)(2,1)} custom-call(bf16[4,256,512]{2,1,0:T(8,128)(2,1)} %get-tuple-element.71.denc_ref, bf16[512,2048]{1,0:T(8,128)(2,1)} %win_ref.3, bf16[1024,1536]{1,0:T(8,128)(2,1)} %get-tuple-element.72.dpre_ref, bf16[512,1024]{1,0:T(8,128)(2,1)} %get-tuple-element.73.dk_ref), custom_call_target="tpu_custom_call" | custom-call | flops 6000000000 | bytes 8000000 | tf_op jit(solution)/shard_map/input_backward/pallas_call | solution.py:465
  85.0 0.0 collective-permute-done.6
  85.0 0.0 collective-permute-done.5
  85.0 0.6 collective-permute-done.4
  85.7 5.5 %collective-permute-done.3 = bf16[64,2560]{1,0:T(8,128)(2,1)S(1)} collective-permute-done((bf16[64,2560]{1,0:T(8,128)(2,1)S(1)}, bf16[64,2560]{1,0:T(8,128)(2,1)S(1)}, u32[]{:S(2)}, u32[]{:S(2)}) %collective-permute-start.3) | collective-permute-done | bytes 327712 | tf_op jit(solution)/shard_map/ppermute | solution.py:521
  91.2 0.0 collective-permute-done.2
  91.3 1.9 %collective-permute-start.8 = (bf16[128,512]{1,0:T(8,128)(2,1)S(1)}, bf16[128,512]{1,0:T(8,128)(2,1)S(1)}, u32[]{:S(2)}, u32[]{:S(2)}) collective-permute-start(bf16[128,512]{1,0:T(8,128)(2,1)S(1)} %pad_maximum_fusion.4), channel_id=1, source_target_pairs={{0,1},{1,0},{16,17},{17,16},{2,3},{3,2},{18,19},{19,18},{4,5},{5,4... | collective-permute-start | bytes 393224 | tf_op jit(solution)/shard_map/ppermute | solution.py:521
  93.1 0.6 collective-permute-start.9
  93.7 0.2 add_convert_fusion.1
  93.9 0.0 copy-start.2
  93.9 1.6 %collective-permute-start.11 = (bf16[16,2560]{1,0:T(8,128)(2,1)S(1)}, bf16[16,2560]{1,0:T(8,128)(2,1)S(1)}, u32[]{:S(2)}, u32[]{:S(2)}) collective-permute-start(bf16[16,2560]{1,0:T(8,128)(2,1)S(1)} %get-tuple-element.92), channel_id=1, source_target_pairs={{0,2},{2,4},{4,6},{6,0},{1,3},{3,5},{5,7},{7,1},{8,10},{10,12},{12... | collective-permute-start | bytes 245768 | tf_op jit(solution)/shard_map/ppermute | solution.py:521
  95.5 2.3 %collective-permute-start.13 = (bf16[16,2560]{1,0:T(8,128)(2,1)S(1)}, bf16[16,2560]{1,0:T(8,128)(2,1)S(1)}, u32[]{:S(2)}, u32[]{:S(2)}) collective-permute-start(bf16[16,2560]{1,0:T(8,128)(2,1)S(1)} %get-tuple-element.93), channel_id=1, source_target_pairs={{0,6},{2,0},{4,2},{6,4},{1,7},{3,1},{5,3},{7,5},{8,14},{10,8},{12,... | collective-permute-start | bytes 245768 | tf_op jit(solution)/shard_map/ppermute | solution.py:521
  97.8 0.4 collective-permute-start.12
  98.3 2.5 %collective-permute-done.11 = bf16[16,2560]{1,0:T(8,128)(2,1)S(1)} collective-permute-done((bf16[16,2560]{1,0:T(8,128)(2,1)S(1)}, bf16[16,2560]{1,0:T(8,128)(2,1)S(1)}, u32[]{:S(2)}, u32[]{:S(2)}) %collective-permute-start.11) | collective-permute-done | bytes 81952 | tf_op jit(solution)/shard_map/ppermute | solution.py:521
  100.8 1.7 %collective-permute-start.10 = (bf16[128,512]{1,0:T(8,128)(2,1)S(1)}, bf16[128,512]{1,0:T(8,128)(2,1)S(1)}, u32[]{:S(2)}, u32[]{:S(2)}) collective-permute-start(bf16[128,512]{1,0:T(8,128)(2,1)S(1)} %pad_maximum_fusion.6), channel_id=1, source_target_pairs={{0,17},{1,16},{16,1},{17,0},{2,19},{3,18},{18,3},{19,2},{4,21},{5,... | collective-permute-start | bytes 393224 | tf_op jit(solution)/shard_map/ppermute | solution.py:521
  102.5 0.0 collective-permute-done.13
  102.5 1.7 %collective-permute-done.12 = bf16[16,2560]{1,0:T(8,128)(2,1)S(1)} collective-permute-done((bf16[16,2560]{1,0:T(8,128)(2,1)S(1)}, bf16[16,2560]{1,0:T(8,128)(2,1)S(1)}, u32[]{:S(2)}, u32[]{:S(2)}) %collective-permute-start.12) | collective-permute-done | bytes 81952 | tf_op jit(solution)/shard_map/ppermute | solution.py:521
  104.1 0.7 convert_add_fusion
  104.8 0.6 convert_add_fusion.1
  105.4 0.0 collective-permute-done.8
  105.5 0.0 collective-permute-done.9
  105.5 1.1 %collective-permute-done.10 = bf16[128,512]{1,0:T(8,128)(2,1)S(1)} collective-permute-done((bf16[128,512]{1,0:T(8,128)(2,1)S(1)}, bf16[128,512]{1,0:T(8,128)(2,1)S(1)}, u32[]{:S(2)}, u32[]{:S(2)}) %collective-permute-start.10) | collective-permute-done | bytes 131104 | tf_op jit(solution)/shard_map/ppermute | solution.py:521
  106.6 0.0 copy-done.2
  106.7 1.0 convolution_convert_fusion
  (21 shorter events, 0.2 us)
Async XLA Ops:
  4.2 37.7 %all-to-all-start = ((bf16[32,16,1152]{2,1,0:T(8,128)(2,1)}), bf16[32,16,1152]{2,1,0:T(8,128)(2,1)S(1)}, u32[]{:S(2)}, u32[]{:S(2)}) async-start(bf16[32,16,1152]{2,1,0:T(8,128)(2,1)} %bitcast.32), calls=%async_computation | async-start | bytes 2359296 | tf_op jit(solution)/shard_map/all_to_all | solution.py:543
  41.9 1.0 copy-start.1
  67.5 3.5 %copy-start = (bf16[256,2560]{1,0:T(8,128)(2,1)S(1)}, bf16[256,2560]{1,0:T(8,128)(2,1)}, u32[]{:S(2)}) copy-start(bf16[256,2560]{1,0:T(8,128)(2,1)} %get-tuple-element.59) | copy-start | bytes 3932164
  67.5 3.5 %collective-permute-start = (bf16[256,2560]{1,0:T(8,128)(2,1)}, bf16[256,2560]{1,0:T(8,128)(2,1)S(1)}, u32[]{:S(2)}, u32[]{:S(2)}) collective-permute-start(bf16[256,2560]{1,0:T(8,128)(2,1)} %get-tuple-element.60), channel_id=1, source_target_pairs={{0,8},{8,0},{1,9},{9,1},{2,10},{10,2},{3,11},{11,3},{4,12},{12,4},... | collective-permute-start | bytes 3932168 | tf_op jit(solution)/shard_map/ppermute | solution.py:521
  68.7 2.3 %collective-permute-start.1 = (bf16[256,512]{1,0:T(8,128)(2,1)S(1)}, bf16[256,512]{1,0:T(8,128)(2,1)S(1)}, u32[]{:S(2)}, u32[]{:S(2)}) collective-permute-start(bf16[256,512]{1,0:T(8,128)(2,1)S(1)} %slice.132), channel_id=1, source_target_pairs={{0,8},{8,0},{1,9},{9,1},{2,10},{10,2},{3,11},{11,3},{4,12},{12,4},... | collective-permute-start | bytes 786440 | tf_op jit(solution)/shard_map/ppermute | solution.py:521
  71.5 6.8 %collective-permute-start.7 = (bf16[128,512]{1,0:T(8,128)(2,1)S(1)}, bf16[128,512]{1,0:T(8,128)(2,1)S(1)}, u32[]{:S(2)}, u32[]{:S(2)}) collective-permute-start(bf16[128,512]{1,0:T(8,128)(2,1)S(1)} %pad_maximum_fusion.3), channel_id=1, source_target_pairs={{0,6},{2,0},{4,2},{6,4},{1,7},{3,1},{5,3},{7,5},{8,14},{10,8},{12,... | collective-permute-start | bytes 393224 | tf_op jit(solution)/shard_map/ppermute | solution.py:521
  71.6 13.5 %collective-permute-start.6 = (bf16[128,512]{1,0:T(8,128)(2,1)S(1)}, bf16[128,512]{1,0:T(8,128)(2,1)S(1)}, u32[]{:S(2)}, u32[]{:S(2)}) collective-permute-start(bf16[128,512]{1,0:T(8,128)(2,1)S(1)} %pad_maximum_fusion.2), channel_id=1, source_target_pairs={{0,4},{2,6},{4,0},{6,2},{1,5},{3,7},{5,1},{7,3},{8,12},{10,14},{12... | collective-permute-start | bytes 393224 | tf_op jit(solution)/shard_map/ppermute | solution.py:521
  71.7 13.4 %collective-permute-start.5 = (bf16[128,512]{1,0:T(8,128)(2,1)S(1)}, bf16[128,512]{1,0:T(8,128)(2,1)S(1)}, u32[]{:S(2)}, u32[]{:S(2)}) collective-permute-start(bf16[128,512]{1,0:T(8,128)(2,1)S(1)} %pad_maximum_fusion.1), channel_id=1, source_target_pairs={{0,2},{2,4},{4,6},{6,0},{1,3},{3,5},{5,7},{7,1},{8,10},{10,12},{12... | collective-permute-start | bytes 393224 | tf_op jit(solution)/shard_map/ppermute | solution.py:521
  73.7 11.9 %collective-permute-start.4 = (bf16[64,2560]{1,0:T(8,128)(2,1)S(1)}, bf16[64,2560]{1,0:T(8,128)(2,1)S(1)}, u32[]{:S(2)}, u32[]{:S(2)}) collective-permute-start(bf16[64,2560]{1,0:T(8,128)(2,1)S(1)} %get-tuple-element.84), channel_id=1, source_target_pairs={{0,17},{1,16},{16,1},{17,0},{2,19},{3,18},{18,3},{19,2},{4,21},{5,... | collective-permute-start | bytes 983048 | tf_op jit(solution)/shard_map/ppermute | solution.py:521
  77.0 14.2 %collective-permute-start.3 = (bf16[64,2560]{1,0:T(8,128)(2,1)S(1)}, bf16[64,2560]{1,0:T(8,128)(2,1)S(1)}, u32[]{:S(2)}, u32[]{:S(2)}) collective-permute-start(bf16[64,2560]{1,0:T(8,128)(2,1)S(1)} %get-tuple-element.85), channel_id=1, source_target_pairs={{0,16},{1,17},{16,0},{17,1},{2,18},{3,19},{18,2},{19,3},{4,20},{5,... | collective-permute-start | bytes 983048 | tf_op jit(solution)/shard_map/ppermute | solution.py:521
  78.3 12.9 %collective-permute-start.2 = (bf16[64,2560]{1,0:T(8,128)(2,1)S(1)}, bf16[64,2560]{1,0:T(8,128)(2,1)S(1)}, u32[]{:S(2)}, u32[]{:S(2)}) collective-permute-start(bf16[64,2560]{1,0:T(8,128)(2,1)S(1)} %get-tuple-element.86), channel_id=1, source_target_pairs={{0,1},{1,0},{16,17},{17,16},{2,3},{3,2},{18,19},{19,18},{4,5},{5,4... | collective-permute-start | bytes 983048 | tf_op jit(solution)/shard_map/ppermute | solution.py:521
  91.3 14.2 %collective-permute-start.8 = (bf16[128,512]{1,0:T(8,128)(2,1)S(1)}, bf16[128,512]{1,0:T(8,128)(2,1)S(1)}, u32[]{:S(2)}, u32[]{:S(2)}) collective-permute-start(bf16[128,512]{1,0:T(8,128)(2,1)S(1)} %pad_maximum_fusion.4), channel_id=1, source_target_pairs={{0,1},{1,0},{16,17},{17,16},{2,3},{3,2},{18,19},{19,18},{4,5},{5,4... | collective-permute-start | bytes 393224 | tf_op jit(solution)/shard_map/ppermute | solution.py:521
  93.1 12.3 %collective-permute-start.9 = (bf16[128,512]{1,0:T(8,128)(2,1)S(1)}, bf16[128,512]{1,0:T(8,128)(2,1)S(1)}, u32[]{:S(2)}, u32[]{:S(2)}) collective-permute-start(bf16[128,512]{1,0:T(8,128)(2,1)S(1)} %pad_maximum_fusion.5), channel_id=1, source_target_pairs={{0,16},{1,17},{16,0},{17,1},{2,18},{3,19},{18,2},{19,3},{4,20},{5,... | collective-permute-start | bytes 393224 | tf_op jit(solution)/shard_map/ppermute | solution.py:521
  93.9 12.7 %copy-start.2 = (bf16[512,256]{1,0:T(8,128)(2,1)S(1)}, bf16[512,256]{1,0:T(8,128)(2,1)}, u32[]{:S(2)}) copy-start(bf16[512,256]{1,0:T(8,128)(2,1)} %get-tuple-element.75) | copy-start | bytes 786436
  93.9 6.8 %collective-permute-start.11 = (bf16[16,2560]{1,0:T(8,128)(2,1)S(1)}, bf16[16,2560]{1,0:T(8,128)(2,1)S(1)}, u32[]{:S(2)}, u32[]{:S(2)}) collective-permute-start(bf16[16,2560]{1,0:T(8,128)(2,1)S(1)} %get-tuple-element.92), channel_id=1, source_target_pairs={{0,2},{2,4},{4,6},{6,0},{1,3},{3,5},{5,7},{7,1},{8,10},{10,12},{12... | collective-permute-start | bytes 245768 | tf_op jit(solution)/shard_map/ppermute | solution.py:521
  95.5 7.0 %collective-permute-start.13 = (bf16[16,2560]{1,0:T(8,128)(2,1)S(1)}, bf16[16,2560]{1,0:T(8,128)(2,1)S(1)}, u32[]{:S(2)}, u32[]{:S(2)}) collective-permute-start(bf16[16,2560]{1,0:T(8,128)(2,1)S(1)} %get-tuple-element.93), channel_id=1, source_target_pairs={{0,6},{2,0},{4,2},{6,4},{1,7},{3,1},{5,3},{7,5},{8,14},{10,8},{12,... | collective-permute-start | bytes 245768 | tf_op jit(solution)/shard_map/ppermute | solution.py:521
  97.8 6.3 %collective-permute-start.12 = (bf16[16,2560]{1,0:T(8,128)(2,1)S(1)}, bf16[16,2560]{1,0:T(8,128)(2,1)S(1)}, u32[]{:S(2)}, u32[]{:S(2)}) collective-permute-start(bf16[16,2560]{1,0:T(8,128)(2,1)S(1)} %get-tuple-element.94), channel_id=1, source_target_pairs={{0,4},{2,6},{4,0},{6,2},{1,5},{3,7},{5,1},{7,3},{8,12},{10,14},{12... | collective-permute-start | bytes 245768 | tf_op jit(solution)/shard_map/ppermute | solution.py:521
  100.8 5.9 %collective-permute-start.10 = (bf16[128,512]{1,0:T(8,128)(2,1)S(1)}, bf16[128,512]{1,0:T(8,128)(2,1)S(1)}, u32[]{:S(2)}, u32[]{:S(2)}) collective-permute-start(bf16[128,512]{1,0:T(8,128)(2,1)S(1)} %pad_maximum_fusion.6), channel_id=1, source_target_pairs={{0,17},{1,16},{16,1},{17,0},{2,19},{3,18},{18,3},{19,2},{4,21},{5,... | collective-permute-start | bytes 393224 | tf_op jit(solution)/shard_map/ppermute | solution.py:521

commit v4 on v3

--- a/solution.py
+++ b/solution.py
@@ -332,16 +332,16 @@
     return jnp.sum(jnp.where(hit, dest_row.astype(f32), 0.0), axis=1, keepdims=True).astype(jnp.int32)
 
 
-def owner_kernel(sizes, capacity, me_ref, *refs):
-    n_in, n_out = 15, 6
+def owner_kernel(sizes, capacity, me_ref, recv_ref, *refs):
+    n_in, n_out = 14, 7
     sources, outs, refs = refs[:n_in], refs[n_in : n_in + n_out], refs[n_in + n_out :]
     held, refs = refs[:n_in], refs[n_in:]
     (
-        recv_ref, enc_ref, wout_ref, normed_ref, nu_ref, gi_ref, v_ref, k_ref, q_t_ref,
+        enc_ref, wout_ref, normed_ref, nu_ref, gi_ref, v_ref, k_ref, q_t_ref,
         attn_t_ref, grad_ref, slope_ref, slope_t_ref, mt_ref, xt_ref,
     ) = held
-    grouped_ref, turned_ref, dmix_ref, dq_ref, denc_ref, dpre_ref, dk_ref, keep_ref, send_ref, sem_in, sem_out = refs
-    dq_hbm, denc_hbm, dpre_hbm, dk_hbm, keep_hbm, send_hbm = outs
+    grouped_ref, turned_ref, dmix_ref, dq_ref, dq_far_ref, denc_ref, dpre_ref, dk_ref, keep_ref, send_ref, sem_in, sem_out = refs
+    dq_hbm, dq_far_hbm, denc_hbm, dpre_hbm, dk_hbm, keep_hbm, send_hbm = outs
     hist, seq, width = enc_ref.shape
     slots, padded = recv_ref.shape[0], grouped_ref.shape[0]
     kept = keep_ref.shape[0]
@@ -350,18 +350,15 @@
         source, dest = (sources[i], held[i]) if at is None else (sources[i].at[at], held[i].at[at])
         return pltpu.make_async_copy(source, dest, sem_in.at[n])
 
-    first = [load(i, i) for i in range(6)]
-    by_history = [[load(i, i + 7 * at, at) for i in range(6, 13)] for at in range(hist)]
-    last = [load(i, 7 * hist + i - 7) for i in (13, 14)]
-    for copy in first[:2]:
+    first = [load(i, i) for i in range(5)]
+    by_history = [[load(i, i + 7 * at, at) for i in range(5, 12)] for at in range(hist)]
+    last = [load(i, 7 * hist + i - 7) for i in (12, 13)]
+    for copy in first + sum(by_history, []) + last:
         copy.start()
     grouped_ref[...] = jnp.zeros_like(grouped_ref)
     turned_ref[...] = jnp.zeros_like(turned_ref)
+    dest_row, starts, tiles = group_slots(recv_ref, hist)
     first[0].wait()
-    first[1].wait()
-    for copy in first[2:] + sum(by_history, []) + last:
-        copy.start()
-    dest_row, starts, tiles = group_slots(recv_ref, hist)
 
     def one_tile(tile, carry):
         target_tile(tile, starts, dest_row, recv_ref, enc_ref, grouped_ref, turned_ref)
@@ -373,7 +370,9 @@
         denc_ref[h] = dot_nt(unit, turned_ref[h].astype(bf16)).astype(bf16)
     dest = return_order(sizes, capacity, me_ref, dest_row)
     back = (dest == iota((slots, padded), 1)).astype(f32).astype(bf16)
-    dq_ref[...] = dot_nn(back, grouped_ref[...]).astype(bf16)
+    near = dq_ref.shape[0]
+    dq_ref[...] = dot_nn(back[:near], grouped_ref[...]).astype(bf16)
+    dq_far_ref[...] = dot_nn(back[near:], grouped_ref[...]).astype(bf16)
     stores = []
 
     def store(source, dest):
@@ -383,7 +382,8 @@
 
     store(denc_ref, denc_hbm)
     store(dq_ref, dq_hbm)
-    for copy in first[2:]:
+    store(dq_far_ref, dq_far_hbm)
+    for copy in first[1:]:
         copy.wait()
     norm_backward(denc_ref, wout_ref, normed_ref, nu_ref, gi_ref, dmix_ref, dpre_ref)
     for at in range(hist):
@@ -419,10 +419,11 @@
     slots = recv.shape[0]
     rows = hist * seq
     padded = ((slots - hist) // TILE + hist) * TILE
-    operands = (recv, enc, w_out) + state + (mt, xt)
+    operands = (enc, w_out) + state + (mt, xt)
     raw = pl.BlockSpec(memory_space=pl.ANY)
     outs = [
-        jax.ShapeDtypeStruct((slots, width), bf16),
+        jax.ShapeDtypeStruct((slots // sizes[1], width), bf16),
+        jax.ShapeDtypeStruct((slots - slots // sizes[1], width), bf16),
         jax.ShapeDtypeStruct(enc.shape, bf16),
         jax.ShapeDtypeStruct((rows, 3 * width), bf16),
         jax.ShapeDtypeStruct((width, rows), bf16),
@@ -432,7 +433,9 @@
     return pl.pallas_call(
         functools.partial(owner_kernel, sizes, slots // math.prod(sizes)),
         grid=(1,),
-        in_specs=[pl.BlockSpec(memory_space=pltpu.SMEM)] + [raw] * len(operands),
+        in_specs=[
+            pl.BlockSpec(memory_space=pltpu.SMEM), pl.BlockSpec(memory_space=pltpu.VMEM),
+        ] + [raw] * len(operands),
         out_specs=[raw] * len(outs),
         out_shape=outs,
         scratch_shapes=[pltpu.VMEM(a.shape, a.dtype) for a in operands]
@@ -444,12 +447,12 @@
         + [pltpu.VMEM(a.shape, a.dtype) for a in outs]
         + [
             pltpu.SemaphoreType.DMA((7 * hist + 8,)),
-            pltpu.SemaphoreType.DMA((2 * hist + 12,)),
+            pltpu.SemaphoreType.DMA((2 * hist + 13,)),
         ],
-        compiler_params=params(60),
+        compiler_params=params(56),
         cost_estimate=cost(30e9, 30e6),
         name="owner_backward",
-    )(me, *operands)
+    )(me, recv, *operands)
 
 
 def input_kernel(denc_ref, win_ref, dpre_ref, dk_ref, out_ref):
@@ -547,17 +550,17 @@
         histories, weight_in, weight_out, perm
     )
     state = (normed, nu, gi, v, k, q_t, attn_t, grad, slope, slope_t)
-    d_query, d_enc, dpre, dk, keep, send = owner_backward(
+    near, far, d_enc, dpre, dk, keep, send = owner_backward(
         me, sizes, recv, enc, weight_out, state, mt, xt, kept
     )
     rows = core_stage(keep, send)
-    back = [cut_rows(b, n_z) for b in send_blocks(cut_rows(d_query, n_core), core)]
-    d_enc, rows, back = after((d_enc, rows, back))
+    d_enc, rows, near, far = after((d_enc, rows, near, far))
+    back = [cut_rows(b, n_z) for b in send_blocks([near] + cut_rows(far, n_core - 1), core)]
     back = [jnp.concatenate([b[d] for b in back], axis=0) for d in range(n_z)]
     d_inputs = input_backward(d_enc, weight_in, dpre, dk)
+    back = send_blocks(back, line)
     parts = send_blocks(cut_rows(rows, n_y * n_x), plane)
-    back = send_blocks(back, line)
-    parts, back, d_inputs = after((parts, back, d_inputs))
+    back, parts, d_inputs = after((back, parts, d_inputs))
     parts = send_blocks(cut_rows(add_up(parts).astype(bf16), n_z), line)
     back = [b.reshape(n_core, n_y * n_x, capacity, width) for b in back]
     back = [

time: 108 us -> 107 us (level)
  starting transfers between devices: 21.7 us -> 24.5 us
  local copies, waits for them, and re-layouts: 3.26 us -> 1.28 us
  Pallas kernels: 48.4 us -> 46.8 us
  other arithmetic: 3.54 us -> 4.91 us
    ppermute x14, starting transfers between devices: 14.4 us -> 17.2 us  [send_blocks(): parts.append(lax.ppermute(blocks[d], axes, pairs))]
    slice x5 -> x4, local copies, waits for them, and re-layouts: 2.14 us -> 0.16 us  [cut_rows(): return [rows[i * step:(i + 1) * step] for i in range(count)]]
    pallas_call x1, Pallas kernels: 24.6 us -> 23 us  [owner_backward(): pl.pallas_call(functools.partial(owner_kernel, sizes, slots // math.prod(...]
    convert_element_type x1, other arithmetic: 0.32 us -> 1.73 us  [core_stage(): add_up(send_blocks([keep] + cut_rows(send, lax.axis_size(AXES[1]) - 1), A...]
  transfers between devices with their start and end apart: 15 -> 15, of which waited for: 8 -> 6; matrix products, arithmetic and copies ran while one was open for 4% -> 3% of each run, Pallas kernels for 19% -> 19%
where the time goes in v4:
time: 107 us; the launch traced here: 108 us
  Pallas kernels  46.8 us (44%)
  waiting for transfers between devices  28.3 us (26%)
  starting transfers between devices  24.5 us (23%)
  other arithmetic  4.91 us (5%)
  local copies, waits for them, and re-layouts  1.28 us (1%)
    pallas_call x1, Pallas kernels, owner_backward(): pl.pallas_call(functools.partial(owner_kernel, sizes, slots // math.prod(...  23 us
    ppermute x14, starting transfers between devices, send_blocks(): parts.append(lax.ppermute(blocks[d], axes, pairs))  17.2 us
    all_to_all x1, waiting for transfers between devices, local(): recv = lax.all_to_all(shaped, AXES, split_axis=0, concat_axis=0, tiled=True)  15.2 us
    pallas_call x1, Pallas kernels, layer_forward(): pl.pallas_call(forward_kernel, grid=(hist,), in_specs=[row, whole(w_in.sh...  14.2 us
    ppermute x14, waiting for transfers between devices, send_blocks(): parts.append(lax.ppermute(blocks[d], axes, pairs))  13.1 us
    all_to_all x1, starting transfers between devices, local(): recv = lax.all_to_all(shaped, AXES, split_axis=0, concat_axis=0, tiled=True)  7.3 us
    pallas_call x1, Pallas kernels, input_backward(): pl.pallas_call(input_kernel, grid=(hist,), in_specs=[block(denc), whole(w...  6.68 us
    pallas_call x1, Pallas kernels, route(): pl.pallas_call(functools.partial(route_kernel, sizes, capacity), grid=(1,...  2.9 us
  transfers between devices with their start and end apart: 15, of which 6 were waited for; matrix products, arithmetic and copies ran while one was open for 3% of the time, Pallas kernels for 19%

profile of v4, /device:TPU:0, one launch (start us, length us, event | category | flops | bytes accessed | tf_op | source)
XLA Modules:
  0.0 107.8 jit_solution(16871462176613125438)
XLA Ops:
  0.6 0.6 pad_add_fusion.me_ref
  1.3 2.9 %route.1 = (bf16[512,1152]{1,0:T(8,128)(2,1)}, bf16[512,256]{1,0:T(8,128)(2,1)}) custom-call(s32[4]{0:T(128)} %pad_add_fusion.me_ref, s32[1,256]{1,0:T(1,128)} %bitcast.53, s32[1,256]{1,0:T(1,128)} %bitcast.54, s32[1,256]{1,0:T(1,128)} %bitcast.55, bf16[256,512]{1,0:T(8,128)(2,1)} %cand_ref.1, bf16[256,512]{1,0:T(8,128)(2,1)} %cot_ref.1), custom_call_target="tpu_custom_call" | custom-call | flops 2000000000 | bytes 2097152 | tf_op jit(solution)/shard_map/route/pallas_call | solution.py:101
  4.2 7.3 %all-to-all-start = ((bf16[32,16,1152]{2,1,0:T(8,128)(2,1)}), bf16[32,16,1152]{2,1,0:T(8,128)(2,1)S(1)}, u32[]{:S(2)}, u32[]{:S(2)}) async-start(bf16[32,16,1152]{2,1,0:T(8,128)(2,1)} %bitcast.32), calls=%async_computation | async-start | bytes 2359296 | tf_op jit(solution)/shard_map/all_to_all | solution.py:546
  11.5 0.9 fusion.perm_ref
  12.5 14.2 %forward.1 = (bf16[4,256,512]{2,1,0:T(8,128)(2,1)}, bf16[4,256,1024]{2,1,0:T(8,128)(2,1)}, bf16[4,512,256]{2,1,0:T(8,128)(2,1)}, bf16[4,256,512]{2,1,0:T(8,128)(...) custom-call(bf16[4,256,512]{2,1,0:T(8,128)(2,1)} %x_ref.1, ...), custom_call_target="tpu_custom_call" | custom-call | flops 17999998976 | bytes 24000000 | tf_op jit(solution)/shard_map/forward/pallas_call | solution.py:191
  26.7 15.2 %all-to-all-done = bf16[32,16,1152]{2,1,0:T(8,128)(2,1)S(1)} async-done(((bf16[32,16,1152]{2,1,0:T(8,128)(2,1)}), bf16[32,16,1152]{2,1,0:T(8,128)(2,1)S(1)}, u32[]{:S(2)}, u32[]{:S(2)}) %all-to-all-start) | async-done | bytes 1179680 | tf_op jit(solution)/shard_map/all_to_all | solution.py:546
  41.9 0.0 copy-start
  41.9 1.0 copy-done
  42.9 23.0 %owner_backward.1 = (bf16[256,512]{1,0:T(8,128)(2,1)}, bf16[256,512]{1,0:T(8,128)(2,1)}, bf16[4,256,512]{2,1,0:T(8,128)(2,1)}, bf16[1024,1536]{1,0:T(8,128)(2,1)...) custom-call(s32[4]{0:T(128)} %pad_add_fusion.me_ref, ...), custom_call_target="tpu_custom_call" | custom-call | flops 30000001024 | bytes 30000000 | tf_op jit(solution)/shard_map/owner_backward/pallas_call | solution.py:433
  65.9 0.1 collective-permute-start
  66.0 3.2 %collective-permute-done = bf16[256,2560]{1,0:T(8,128)(2,1)S(1)} collective-permute-done((bf16[256,2560]{1,0:T(8,128)(2,1)}, bf16[256,2560]{1,0:T(8,128)(2,1)S(1)}, u32[]{:S(2)}, u32[]{:S(2)}) %collective-permute-start) | collective-permute-done | bytes 1310752 | tf_op jit(solution)/shard_map/ppermute | solution.py:524
  69.3 0.0 copy-start.3
  69.3 1.7 %add_convert_fusion = bf16[256,2560]{1,0:T(8,128)(2,1)S(1)} fusion(bf16[256,2560]{1,0:T(8,128)(2,1)S(1)} %collective-permute-done, bf16[256,2560]{1,0:T(8,128)(2,1)} %get-tuple-element.54), kind=kLoop, calls=%fused_computation | loop fusion | flops 2621440 | bytes 3932160 | tf_op jit(solution)/shard_map/convert_element_type | solution.py:509
  71.0 0.0 copy-done.3
  71.0 0.0 copy-start.1
  71.0 0.2 collective-permute-start.1
  71.2 0.1 fusion.31
  71.3 2.5 %collective-permute-start.7 = (bf16[64,2560]{1,0:T(8,128)(2,1)S(1)}, bf16[64,2560]{1,0:T(8,128)(2,1)S(1)}, u32[]{:S(2)}, u32[]{:S(2)}) collective-permute-start(bf16[64,2560]{1,0:T(8,128)(2,1)S(1)} %get-tuple-element.74), channel_id=1, source_target_pairs={{0,17},{1,16},{16,1},{17,0},{2,19},{3,18},{18,3},{19,2},{4,21},{5,... | collective-permute-start | bytes 983048 | tf_op jit(solution)/shard_map/ppermute | solution.py:524
  73.8 0.0 collective-permute-start.6
  73.8 1.1 %collective-permute-start.5 = (bf16[64,2560]{1,0:T(8,128)(2,1)S(1)}, bf16[64,2560]{1,0:T(8,128)(2,1)S(1)}, u32[]{:S(2)}, u32[]{:S(2)}) collective-permute-start(bf16[64,2560]{1,0:T(8,128)(2,1)S(1)} %get-tuple-element.76), channel_id=1, source_target_pairs={{0,1},{1,0},{16,17},{17,16},{2,3},{3,2},{18,19},{19,18},{4,5},{5,4... | collective-permute-start | bytes 983048 | tf_op jit(solution)/shard_map/ppermute | solution.py:524
  74.9 0.0 copy-done.1
  74.9 0.0 collective-permute-done.1
  75.0 2.0 %collective-permute-start.2 = (bf16[128,512]{1,0:T(8,128)(2,1)S(1)}, bf16[128,512]{1,0:T(8,128)(2,1)S(1)}, u32[]{:S(2)}, u32[]{:S(2)}) collective-permute-start(bf16[128,512]{1,0:T(8,128)(2,1)S(1)} %pad_maximum_fusion.1), channel_id=1, source_target_pairs={{0,2},{2,4},{4,6},{6,0},{1,3},{3,5},{5,7},{7,1},{8,10},{10,12},{12... | collective-permute-start | bytes 393224 | tf_op jit(solution)/shard_map/ppermute | solution.py:524
  76.9 1.4 %collective-permute-start.3 = (bf16[128,512]{1,0:T(8,128)(2,1)S(1)}, bf16[128,512]{1,0:T(8,128)(2,1)S(1)}, u32[]{:S(2)}, u32[]{:S(2)}) collective-permute-start(bf16[128,512]{1,0:T(8,128)(2,1)S(1)} %pad_maximum_fusion.2), channel_id=1, source_target_pairs={{0,4},{2,6},{4,0},{6,2},{1,5},{3,7},{5,1},{7,3},{8,12},{10,14},{12... | collective-permute-start | bytes 393224 | tf_op jit(solution)/shard_map/ppermute | solution.py:524
  78.3 4.5 %collective-permute-done.7 = bf16[64,2560]{1,0:T(8,128)(2,1)S(1)} collective-permute-done((bf16[64,2560]{1,0:T(8,128)(2,1)S(1)}, bf16[64,2560]{1,0:T(8,128)(2,1)S(1)}, u32[]{:S(2)}, u32[]{:S(2)}) %collective-permute-start.7) | collective-permute-done | bytes 327712 | tf_op jit(solution)/shard_map/ppermute | solution.py:524
  82.9 2.7 %collective-permute-start.4 = (bf16[128,512]{1,0:T(8,128)(2,1)S(1)}, bf16[128,512]{1,0:T(8,128)(2,1)S(1)}, u32[]{:S(2)}, u32[]{:S(2)}) collective-permute-start(bf16[128,512]{1,0:T(8,128)(2,1)S(1)} %pad_maximum_fusion.3), channel_id=1, source_target_pairs={{0,6},{2,0},{4,2},{6,4},{1,7},{3,1},{5,3},{7,5},{8,14},{10,8},{12,... | collective-permute-start | bytes 393224 | tf_op jit(solution)/shard_map/ppermute | solution.py:524
  85.6 6.7 %input_backward.1 = bf16[4,256,512]{2,1,0:T(8,128)(2,1)} custom-call(bf16[4,256,512]{2,1,0:T(8,128)(2,1)} %get-tuple-element.61.denc_ref, bf16[512,2048]{1,0:T(8,128)(2,1)} %win_ref.3, bf16[1024,1536]{1,0:T(8,128)(2,1)} %get-tuple-element.62.dpre_ref, bf16[512,1024]{1,0:T(8,128)(2,1)} %get-tuple-element.63.dk_ref), custom_call_target="tpu_custom_call" | custom-call | flops 6000000000 | bytes 8000000 | tf_op jit(solution)/shard_map/input_backward/pallas_call | solution.py:468
  92.3 0.0 collective-permute-done.6
  92.3 0.0 collective-permute-done.5
  92.3 0.0 collective-permute-done.2
  92.3 0.0 collective-permute-done.3
  92.3 0.0 collective-permute-done.4
  92.4 0.2 collective-permute-start.8
  92.6 1.5 %collective-permute-start.9 = (bf16[128,512]{1,0:T(8,128)(2,1)S(1)}, bf16[128,512]{1,0:T(8,128)(2,1)S(1)}, u32[]{:S(2)}, u32[]{:S(2)}) collective-permute-start(bf16[128,512]{1,0:T(8,128)(2,1)S(1)} %pad_maximum_fusion.5), channel_id=1, source_target_pairs={{0,16},{1,17},{16,0},{17,1},{2,18},{3,19},{18,2},{19,3},{4,20},{5,... | collective-permute-start | bytes 393224 | tf_op jit(solution)/shard_map/ppermute | solution.py:524
  94.1 0.2 add_convert_fusion.1
  94.3 0.0 copy-start.2
  94.3 0.8 collective-permute-start.11
  95.1 3.1 %collective-permute-start.13 = (bf16[16,2560]{1,0:T(8,128)(2,1)S(1)}, bf16[16,2560]{1,0:T(8,128)(2,1)S(1)}, u32[]{:S(2)}, u32[]{:S(2)}) collective-permute-start(bf16[16,2560]{1,0:T(8,128)(2,1)S(1)} %get-tuple-element.79), channel_id=1, source_target_pairs={{0,6},{2,0},{4,2},{6,4},{1,7},{3,1},{5,3},{7,5},{8,14},{10,8},{12,... | collective-permute-start | bytes 245768 | tf_op jit(solution)/shard_map/ppermute | solution.py:524
  98.2 0.0 collective-permute-start.12
  98.3 2.6 %collective-permute-done.11 = bf16[16,2560]{1,0:T(8,128)(2,1)S(1)} collective-permute-done((bf16[16,2560]{1,0:T(8,128)(2,1)S(1)}, bf16[16,2560]{1,0:T(8,128)(2,1)S(1)}, u32[]{:S(2)}, u32[]{:S(2)}) %collective-permute-start.11) | collective-permute-done | bytes 81952 | tf_op jit(solution)/shard_map/ppermute | solution.py:524
  100.8 1.7 %collective-permute-start.10 = (bf16[128,512]{1,0:T(8,128)(2,1)S(1)}, bf16[128,512]{1,0:T(8,128)(2,1)S(1)}, u32[]{:S(2)}, u32[]{:S(2)}) collective-permute-start(bf16[128,512]{1,0:T(8,128)(2,1)S(1)} %pad_maximum_fusion.6), channel_id=1, source_target_pairs={{0,17},{1,16},{16,1},{17,0},{2,19},{3,18},{18,3},{19,2},{4,21},{5,... | collective-permute-start | bytes 393224 | tf_op jit(solution)/shard_map/ppermute | solution.py:524
  102.5 0.0 collective-permute-done.13
  102.5 1.7 %collective-permute-done.12 = bf16[16,2560]{1,0:T(8,128)(2,1)S(1)} collective-permute-done((bf16[16,2560]{1,0:T(8,128)(2,1)S(1)}, bf16[16,2560]{1,0:T(8,128)(2,1)S(1)}, u32[]{:S(2)}, u32[]{:S(2)}) %collective-permute-start.12) | collective-permute-done | bytes 81952 | tf_op jit(solution)/shard_map/ppermute | solution.py:524
  104.3 0.7 convert_add_fusion
  104.9 0.6 convert_add_fusion.1
  105.6 0.0 collective-permute-done.8
  105.6 0.0 collective-permute-done.9
  105.6 1.1 %collective-permute-done.10 = bf16[128,512]{1,0:T(8,128)(2,1)S(1)} collective-permute-done((bf16[128,512]{1,0:T(8,128)(2,1)S(1)}, bf16[128,512]{1,0:T(8,128)(2,1)S(1)}, u32[]{:S(2)}, u32[]{:S(2)}) %collective-permute-start.10) | collective-permute-done | bytes 131104 | tf_op jit(solution)/shard_map/ppermute | solution.py:524
  106.7 0.0 copy-done.2
  106.7 1.0 convolution_convert_fusion
  (22 shorter events, 0.3 us)
Async XLA Ops:
  4.2 37.7 %all-to-all-start = ((bf16[32,16,1152]{2,1,0:T(8,128)(2,1)}), bf16[32,16,1152]{2,1,0:T(8,128)(2,1)S(1)}, u32[]{:S(2)}, u32[]{:S(2)}) async-start(bf16[32,16,1152]{2,1,0:T(8,128)(2,1)} %bitcast.32), calls=%async_computation | async-start | bytes 2359296 | tf_op jit(solution)/shard_map/all_to_all | solution.py:546
  41.9 1.0 copy-start
  65.9 3.3 %collective-permute-start = (bf16[256,2560]{1,0:T(8,128)(2,1)}, bf16[256,2560]{1,0:T(8,128)(2,1)S(1)}, u32[]{:S(2)}, u32[]{:S(2)}) collective-permute-start(bf16[256,2560]{1,0:T(8,128)(2,1)} %get-tuple-element.55), channel_id=1, source_target_pairs={{0,8},{8,0},{1,9},{9,1},{2,10},{10,2},{3,11},{11,3},{4,12},{12,4},... | collective-permute-start | bytes 3932168 | tf_op jit(solution)/shard_map/ppermute | solution.py:524
  69.3 1.7 %copy-start.3 = (bf16[256,512]{1,0:T(8,128)(2,1)S(1)}, bf16[256,512]{1,0:T(8,128)(2,1)}, u32[]{:S(2)}) copy-start(bf16[256,512]{1,0:T(8,128)(2,1)} %get-tuple-element.59) | copy-start | bytes 786436
  71.0 3.9 %copy-start.1 = (bf16[256,512]{1,0:T(8,128)(2,1)S(1)}, bf16[256,512]{1,0:T(8,128)(2,1)}, u32[]{:S(2)}) copy-start(bf16[256,512]{1,0:T(8,128)(2,1)} %get-tuple-element.58) | copy-start | bytes 786436
  71.0 3.9 %collective-permute-start.1 = (bf16[256,512]{1,0:T(8,128)(2,1)S(1)}, bf16[256,512]{1,0:T(8,128)(2,1)S(1)}, u32[]{:S(2)}, u32[]{:S(2)}) collective-permute-start(bf16[256,512]{1,0:T(8,128)(2,1)S(1)} %copy-done.3), channel_id=1, source_target_pairs={{0,8},{8,0},{1,9},{9,1},{2,10},{10,2},{3,11},{11,3},{4,12},{12,4},... | collective-permute-start | bytes 786440 | tf_op jit(solution)/shard_map/ppermute | solution.py:524
  71.3 11.6 %collective-permute-start.7 = (bf16[64,2560]{1,0:T(8,128)(2,1)S(1)}, bf16[64,2560]{1,0:T(8,128)(2,1)S(1)}, u32[]{:S(2)}, u32[]{:S(2)}) collective-permute-start(bf16[64,2560]{1,0:T(8,128)(2,1)S(1)} %get-tuple-element.74), channel_id=1, source_target_pairs={{0,17},{1,16},{16,1},{17,0},{2,19},{3,18},{18,3},{19,2},{4,21},{5,... | collective-permute-start | bytes 983048 | tf_op jit(solution)/shard_map/ppermute | solution.py:524
  73.8 18.5 %collective-permute-start.6 = (bf16[64,2560]{1,0:T(8,128)(2,1)S(1)}, bf16[64,2560]{1,0:T(8,128)(2,1)S(1)}, u32[]{:S(2)}, u32[]{:S(2)}) collective-permute-start(bf16[64,2560]{1,0:T(8,128)(2,1)S(1)} %get-tuple-element.75), channel_id=1, source_target_pairs={{0,16},{1,17},{16,0},{17,1},{2,18},{3,19},{18,2},{19,3},{4,20},{5,... | collective-permute-start | bytes 983048 | tf_op jit(solution)/shard_map/ppermute | solution.py:524
  73.8 18.5 %collective-permute-start.5 = (bf16[64,2560]{1,0:T(8,128)(2,1)S(1)}, bf16[64,2560]{1,0:T(8,128)(2,1)S(1)}, u32[]{:S(2)}, u32[]{:S(2)}) collective-permute-start(bf16[64,2560]{1,0:T(8,128)(2,1)S(1)} %get-tuple-element.76), channel_id=1, source_target_pairs={{0,1},{1,0},{16,17},{17,16},{2,3},{3,2},{18,19},{19,18},{4,5},{5,4... | collective-permute-start | bytes 983048 | tf_op jit(solution)/shard_map/ppermute | solution.py:524
  75.0 17.3 %collective-permute-start.2 = (bf16[128,512]{1,0:T(8,128)(2,1)S(1)}, bf16[128,512]{1,0:T(8,128)(2,1)S(1)}, u32[]{:S(2)}, u32[]{:S(2)}) collective-permute-start(bf16[128,512]{1,0:T(8,128)(2,1)S(1)} %pad_maximum_fusion.1), channel_id=1, source_target_pairs={{0,2},{2,4},{4,6},{6,0},{1,3},{3,5},{5,7},{7,1},{8,10},{10,12},{12... | collective-permute-start | bytes 393224 | tf_op jit(solution)/shard_map/ppermute | solution.py:524
  76.9 15.4 %collective-permute-start.3 = (bf16[128,512]{1,0:T(8,128)(2,1)S(1)}, bf16[128,512]{1,0:T(8,128)(2,1)S(1)}, u32[]{:S(2)}, u32[]{:S(2)}) collective-permute-start(bf16[128,512]{1,0:T(8,128)(2,1)S(1)} %pad_maximum_fusion.2), channel_id=1, source_target_pairs={{0,4},{2,6},{4,0},{6,2},{1,5},{3,7},{5,1},{7,3},{8,12},{10,14},{12... | collective-permute-start | bytes 393224 | tf_op jit(solution)/shard_map/ppermute | solution.py:524
  82.9 9.4 %collective-permute-start.4 = (bf16[128,512]{1,0:T(8,128)(2,1)S(1)}, bf16[128,512]{1,0:T(8,128)(2,1)S(1)}, u32[]{:S(2)}, u32[]{:S(2)}) collective-permute-start(bf16[128,512]{1,0:T(8,128)(2,1)S(1)} %pad_maximum_fusion.3), channel_id=1, source_target_pairs={{0,6},{2,0},{4,2},{6,4},{1,7},{3,1},{5,3},{7,5},{8,14},{10,8},{12,... | collective-permute-start | bytes 393224 | tf_op jit(solution)/shard_map/ppermute | solution.py:524
  92.4 13.2 %collective-permute-start.8 = (bf16[128,512]{1,0:T(8,128)(2,1)S(1)}, bf16[128,512]{1,0:T(8,128)(2,1)S(1)}, u32[]{:S(2)}, u32[]{:S(2)}) collective-permute-start(bf16[128,512]{1,0:T(8,128)(2,1)S(1)} %pad_maximum_fusion.4), channel_id=1, source_target_pairs={{0,1},{1,0},{16,17},{17,16},{2,3},{3,2},{18,19},{19,18},{4,5},{5,4... | collective-permute-start | bytes 393224 | tf_op jit(solution)/shard_map/ppermute | solution.py:524
  92.6 13.0 %collective-permute-start.9 = (bf16[128,512]{1,0:T(8,128)(2,1)S(1)}, bf16[128,512]{1,0:T(8,128)(2,1)S(1)}, u32[]{:S(2)}, u32[]{:S(2)}) collective-permute-start(bf16[128,512]{1,0:T(8,128)(2,1)S(1)} %pad_maximum_fusion.5), channel_id=1, source_target_pairs={{0,16},{1,17},{16,0},{17,1},{2,18},{3,19},{18,2},{19,3},{4,20},{5,... | collective-permute-start | bytes 393224 | tf_op jit(solution)/shard_map/ppermute | solution.py:524
  94.3 12.4 %copy-start.2 = (bf16[512,256]{1,0:T(8,128)(2,1)S(1)}, bf16[512,256]{1,0:T(8,128)(2,1)}, u32[]{:S(2)}) copy-start(bf16[512,256]{1,0:T(8,128)(2,1)} %get-tuple-element.65) | copy-start | bytes 786436
  94.3 6.5 %collective-permute-start.11 = (bf16[16,2560]{1,0:T(8,128)(2,1)S(1)}, bf16[16,2560]{1,0:T(8,128)(2,1)S(1)}, u32[]{:S(2)}, u32[]{:S(2)}) collective-permute-start(bf16[16,2560]{1,0:T(8,128)(2,1)S(1)} %get-tuple-element.78), channel_id=1, source_target_pairs={{0,2},{2,4},{4,6},{6,0},{1,3},{3,5},{5,7},{7,1},{8,10},{10,12},{12... | collective-permute-start | bytes 245768 | tf_op jit(solution)/shard_map/ppermute | solution.py:524
  95.1 7.4 %collective-permute-start.13 = (bf16[16,2560]{1,0:T(8,128)(2,1)S(1)}, bf16[16,2560]{1,0:T(8,128)(2,1)S(1)}, u32[]{:S(2)}, u32[]{:S(2)}) collective-permute-start(bf16[16,2560]{1,0:T(8,128)(2,1)S(1)} %get-tuple-element.79), channel_id=1, source_target_pairs={{0,6},{2,0},{4,2},{6,4},{1,7},{3,1},{5,3},{7,5},{8,14},{10,8},{12,... | collective-permute-start | bytes 245768 | tf_op jit(solution)/shard_map/ppermute | solution.py:524
  98.2 6.0 %collective-permute-start.12 = (bf16[16,2560]{1,0:T(8,128)(2,1)S(1)}, bf16[16,2560]{1,0:T(8,128)(2,1)S(1)}, u32[]{:S(2)}, u32[]{:S(2)}) collective-permute-start(bf16[16,2560]{1,0:T(8,128)(2,1)S(1)} %get-tuple-element.80), channel_id=1, source_target_pairs={{0,4},{2,6},{4,0},{6,2},{1,5},{3,7},{5,1},{7,3},{8,12},{10,14},{12... | collective-permute-start | bytes 245768 | tf_op jit(solution)/shard_map/ppermute | solution.py:524
  100.8 5.9 %collective-permute-start.10 = (bf16[128,512]{1,0:T(8,128)(2,1)S(1)}, bf16[128,512]{1,0:T(8,128)(2,1)S(1)}, u32[]{:S(2)}, u32[]{:S(2)}) collective-permute-start(bf16[128,512]{1,0:T(8,128)(2,1)S(1)} %pad_maximum_fusion.6), channel_id=1, source_target_pairs={{0,17},{1,16},{16,1},{17,0},{2,19},{3,18},{18,3},{19,2},{4,21},{5,... | collective-permute-start | bytes 393224 | tf_op jit(solution)/shard_map/ppermute | solution.py:524

commit v5 on v2

--- a/solution.py
+++ b/solution.py
@@ -308,16 +308,16 @@
             dk_ref[mine, here] = (d_k * slope_t_ref[at, mine].astype(f32)).astype(bf16)
 
 
-def owner_kernel(*refs):
-    n_in, n_out = 15, 6
+def owner_kernel(recv_ref, *refs):
+    n_in, n_out = 15, 7
     sources, outs, refs = refs[:n_in], refs[n_in : n_in + n_out], refs[n_in + n_out :]
     held, refs = refs[:n_in], refs[n_in:]
     (
-        recv_ref, enc_ref, wout_ref, normed_ref, nu_ref, gi_ref, v_ref, k_ref, q_t_ref,
+        enc_ref, order_ref, wout_ref, normed_ref, nu_ref, gi_ref, v_ref, k_ref, q_t_ref,
         attn_t_ref, grad_ref, slope_ref, slope_t_ref, mt_ref, xt_ref,
     ) = held
-    grouped_ref, turned_ref, dmix_ref, dq_ref, denc_ref, dpre_ref, dk_ref, keep_ref, send_ref, sem_in, sem_out = refs
-    dq_hbm, denc_hbm, dpre_hbm, dk_hbm, keep_hbm, send_hbm = outs
+    grouped_ref, turned_ref, dmix_ref, dq_ref, dq_far_ref, denc_ref, dpre_ref, dk_ref, keep_ref, send_ref, sem_in, sem_out = refs
+    dq_hbm, dq_far_hbm, denc_hbm, dpre_hbm, dk_hbm, keep_hbm, send_hbm = outs
     hist, seq, width = enc_ref.shape
     slots, padded = recv_ref.shape[0], grouped_ref.shape[0]
     kept = keep_ref.shape[0]
@@ -333,9 +333,8 @@
         copy.start()
     grouped_ref[...] = jnp.zeros_like(grouped_ref)
     turned_ref[...] = jnp.zeros_like(turned_ref)
+    dest, dest_row, starts, tiles = group_slots(recv_ref, hist)
     first[0].wait()
-    dest, dest_row, starts, tiles = group_slots(recv_ref, hist)
-    first[1].wait()
 
     def one_tile(tile, carry):
         target_tile(tile, starts, dest_row, recv_ref, enc_ref, grouped_ref, turned_ref)
@@ -345,7 +344,11 @@
     for h in range(hist):
         denc_ref[h] = jnp.transpose(turned_ref[h]).astype(bf16)
     back = (dest == iota((slots, padded), 1)).astype(f32).astype(bf16)
-    dq_ref[...] = dot_nn(back, grouped_ref[...]).astype(bf16)
+    d_query = dot_nn(back, grouped_ref[...]).astype(bf16)
+    near = dq_ref.shape[0]
+    first[1].wait()
+    dq_ref[...] = dot_nn(order_ref[:near], d_query).astype(bf16)
+    dq_far_ref[...] = dot_nn(order_ref[near:], d_query).astype(bf16)
     stores = []
 
     def store(source, dest):
@@ -355,6 +358,7 @@
 
     store(denc_ref, denc_hbm)
     store(dq_ref, dq_hbm)
+    store(dq_far_ref, dq_far_hbm)
     for copy in first[2:]:
         copy.wait()
     norm_backward(denc_ref, wout_ref, normed_ref, nu_ref, gi_ref, dmix_ref, dpre_ref)
@@ -386,15 +390,16 @@
         copy.wait()
 
 
-def owner_backward(recv, enc, w_out, state, mt, xt, kept):
+def owner_backward(order, recv, enc, w_out, state, mt, xt, kept):
     hist, seq, width = enc.shape
     slots = recv.shape[0]
     rows = hist * seq
     padded = ((slots - hist) // TILE + hist) * TILE
-    operands = (recv, enc, w_out) + state + (mt, xt)
+    operands = (enc, order, w_out) + state + (mt, xt)
     raw = pl.BlockSpec(memory_space=pl.ANY)
     outs = [
-        jax.ShapeDtypeStruct((slots, width), bf16),
+        jax.ShapeDtypeStruct((slots // 2, width), bf16),
+        jax.ShapeDtypeStruct((slots - slots // 2, width), bf16),
         jax.ShapeDtypeStruct(enc.shape, bf16),
         jax.ShapeDtypeStruct((rows, 3 * width), bf16),
         jax.ShapeDtypeStruct((width, rows), bf16),
@@ -404,7 +409,7 @@
     return pl.pallas_call(
         owner_kernel,
         grid=(1,),
-        in_specs=[raw] * len(operands),
+        in_specs=[pl.BlockSpec(memory_space=pltpu.VMEM)] + [raw] * len(operands),
         out_specs=[raw] * len(outs),
         out_shape=outs,
         scratch_shapes=[pltpu.VMEM(a.shape, a.dtype) for a in operands]
@@ -416,12 +421,12 @@
         + [pltpu.VMEM(a.shape, a.dtype) for a in outs]
         + [
             pltpu.SemaphoreType.DMA((7 * hist + 8,)),
-            pltpu.SemaphoreType.DMA((2 * hist + 12,)),
+            pltpu.SemaphoreType.DMA((2 * hist + 13,)),
         ],
-        compiler_params=params(60),
+        compiler_params=params(44),
         cost_estimate=cost(30e9, 30e6),
         name="owner_backward",
-    )(*operands)
+    )(recv, *operands)
 
 
 def input_kernel(denc_ref, win_ref, dpre_ref, dk_ref, out_ref):
@@ -467,6 +472,26 @@
     return (source[:, None] == jnp.arange(width, dtype=jnp.int32)[None, :]).astype(bf16)
 
 
+def return_orders(capacity):
+    sizes = n_y, n_core, n_z, n_x = tuple(lax.axis_size(a) for a in AXES)
+    slots = n_y * n_core * n_z * n_x * capacity
+    place = jnp.arange(slots, dtype=jnp.int32)
+    inner, block = place % capacity, place // capacity
+    plane = n_y * n_x
+    orders = []
+    for sign, (d_core, d_z, d_plane) in (
+        (1, (block // (plane * n_z), block // plane % n_z, block % plane)),
+        (-1, (block % n_core, block // n_core % n_z, block // (n_core * n_z))),
+    ):
+        y, core, z, x = (
+            (lax.axis_index(a) + sign * d + n) % n
+            for a, d, n in zip(AXES, (d_plane // n_x, d_core, d_z, d_plane % n_x), sizes)
+        )
+        source = (((y * n_core + core) * n_z + z) * n_x + x) * capacity + inner
+        orders.append((source[:, None] == place[None, :]).astype(bf16))
+    return orders
+
+
 def add_up(blocks):
     total = blocks[0].astype(f32)
     for block in blocks[1:]:
@@ -475,20 +500,13 @@
 
 
 def core_stage(keep, send):
-    n_core = lax.axis_size(AXES[1])
-    step = keep.shape[0]
-    parts = [keep]
-    for d in range(1, n_core):
-        pairs = [(c, (c + d) % n_core) for c in range(n_core)]
-        parts.append(lax.ppermute(send[(d - 1) * step : d * step], AXES[1], pairs))
-    return add_up(parts).astype(bf16)
-
-
-def send_blocks(rows, axes):
-    count = lax.axis_size(axes)
-    step = rows.shape[0] // count
+    return add_up(send_blocks([keep] + cut_rows(send, lax.axis_size(AXES[1]) - 1), AXES[1:2])).astype(bf16)
+
+
+def send_blocks(blocks, axes):
+    count = len(blocks)
     sizes = [lax.axis_size(a) for a in axes]
-    parts = [rows[:step]]
+    parts = [blocks[0]]
     for d in range(1, count):
         pairs = []
         for c in range(count):
@@ -497,8 +515,13 @@
                 there += (rest_c + rest_d) % n * stride
                 stride, rest_c, rest_d = stride * n, rest_c // n, rest_d // n
             pairs.append((c, there))
-        parts.append(lax.ppermute(rows[d * step : (d + 1) * step], axes, pairs))
+        parts.append(lax.ppermute(blocks[d], axes, pairs))
     return parts
+
+
+def cut_rows(rows, count):
+    step = rows.shape[0] // count
+    return [rows[i * step : (i + 1) * step] for i in range(count)]
 
 
 def local(histories, weight_in, weight_out, candidates, cotangent, owner_ids, hist_slot, lengths):
@@ -509,26 +532,37 @@
     kept = width // lax.axis_size(AXES[1])
     after = lax.optimization_barrier
 
-    def exchange(rows):
-        shaped = rows.reshape(devices, capacity, rows.shape[1])
-        moved = lax.all_to_all(shaped, AXES, split_axis=0, concat_axis=0, tiled=True)
-        return moved.reshape(slots, rows.shape[1])
-
+    sizes = n_y, n_core, n_z, n_x = tuple(lax.axis_size(a) for a in AXES)
+    core, line, plane = AXES[1:2], AXES[2:3], (AXES[0], AXES[3])
     send, pick = route(owner_ids, hist_slot, lengths, candidates, cotangent, devices, capacity)
-    recv = exchange(send)
+    shaped = send.reshape(devices, capacity, send.shape[1])
+    recv = lax.all_to_all(shaped, AXES, split_axis=0, concat_axis=0, tiled=True)
+    recv = recv.reshape(slots, send.shape[1])
     perm = owner_order(width)
+    leaving, arriving = return_orders(capacity)
+    pick = dot_nn(arriving, pick).astype(bf16)
     enc, slope, slope_t, v, q, k, q_t, attn_t, grad, normed, nu, gi, xt, mt = layer_forward(
         histories, weight_in, weight_out, perm
     )
     state = (normed, nu, gi, v, k, q_t, attn_t, grad, slope, slope_t)
-    d_query, d_enc, dpre, dk, keep, send = owner_backward(recv, enc, weight_out, state, mt, xt, kept)
-    returned = exchange(d_query)
+    near, far, d_enc, dpre, dk, keep, send = owner_backward(
+        leaving, recv, enc, weight_out, state, mt, xt, kept
+    )
     rows = core_stage(keep, send)
-    d_enc, rows = after((d_enc, rows))
+    d_enc, rows, near, far = after((d_enc, rows, near, far))
+    back = [cut_rows(b, n_z) for b in send_blocks([near] + cut_rows(far, n_core - 1), core)]
+    back = [jnp.concatenate([b[d] for b in back], axis=0) for d in range(n_z)]
     d_inputs = input_backward(d_enc, weight_in, dpre, dk)
-    parts = send_blocks(rows, (AXES[0], AXES[3]))
-    parts, d_inputs, returned = after((parts, d_inputs, returned))
-    parts = send_blocks(add_up(parts).astype(bf16), (AXES[2],))
+    back = send_blocks(back, line)
+    parts = send_blocks(cut_rows(rows, n_y * n_x), plane)
+    back, parts, d_inputs = after((back, parts, d_inputs))
+    parts = send_blocks(cut_rows(add_up(parts).astype(bf16), n_z), line)
+    back = [b.reshape(n_core, n_y * n_x, capacity, width) for b in back]
+    back = [
+        jnp.concatenate([b[:, i].reshape(n_core * capacity, width) for b in back], axis=0)
+        for i in range(n_y * n_x)
+    ]
+    returned = jnp.concatenate(send_blocks(back, plane), axis=0)
     candidate_grad = lax.dot_general(
         pick, returned, (((0,), (0,)), ((), ())), preferred_element_type=f32
     ).astype(bf16)

time: 105 us -> 115 us (1.095)
  local copies, waits for them, and re-layouts: 1.15 us -> 8.67 us
  Pallas kernels: 44.9 us -> 46.1 us
    unnamed x4 -> x28, local copies, waits for them, and re-layouts: 1.03 us -> 8.46 us
    ppermute x7 -> x14, starting transfers between devices: 7.96 us -> 13.8 us  [send_blocks(): parts.append(lax.ppermute(blocks[d], axes, pairs))]
    all_to_all x2 -> x1, starting transfers between devices: 12.1 us -> 7.3 us  [local(): recv = lax.all_to_all(shaped, AXES, split_axis=0, concat_axis=0, tiled=True)]
    all_to_all x2 -> x1, waiting for transfers between devices: 19.5 us -> 14.9 us  [local(): recv = lax.all_to_all(shaped, AXES, split_axis=0, concat_axis=0, tiled=True)]
    ppermute x7 -> x14, waiting for transfers between devices: 12.9 us -> 16.6 us  [send_blocks(): parts.append(lax.ppermute(blocks[d], axes, pairs))]
    pallas_call x1, Pallas kernels: 21.1 us -> 22.3 us  [owner_backward(): pl.pallas_call(owner_kernel, grid=(1,), in_specs=[pl.BlockSpec(memory_spa...]
  transfers between devices with their start and end apart: 9 -> 15, of which waited for: 8 -> 6; matrix products, arithmetic and copies ran while one was open for 4% -> 3% of each run, Pallas kernels for 20% -> 18%
where the time goes in v5:
time: 115 us; the launch traced here: 114 us
  Pallas kernels  46.1 us (40%)
  waiting for transfers between devices  31.5 us (27%)
  starting transfers between devices  21.1 us (18%)
  local copies, waits for them, and re-layouts  8.67 us (8%)
  other arithmetic  4.44 us (4%)
  matrix products  1.52 us (1%)
    pallas_call x1, Pallas kernels, owner_backward(): pl.pallas_call(owner_kernel, grid=(1,), in_specs=[pl.BlockSpec(memory_spa...  22.3 us
    ppermute x14, waiting for transfers between devices, send_blocks(): parts.append(lax.ppermute(blocks[d], axes, pairs))  16.6 us
    all_to_all x1, waiting for transfers between devices, local(): recv = lax.all_to_all(shaped, AXES, split_axis=0, concat_axis=0, tiled=True)  14.9 us
    pallas_call x1, Pallas kernels, layer_forward(): pl.pallas_call(forward_kernel, grid=(hist,), in_specs=[row, whole(w_in.sh...  14.3 us
    ppermute x14, starting transfers between devices, send_blocks(): parts.append(lax.ppermute(blocks[d], axes, pairs))  13.8 us
    unnamed x28, local copies, waits for them, and re-layouts  8.46 us
    all_to_all x1, starting transfers between devices, local(): recv = lax.all_to_all(shaped, AXES, split_axis=0, concat_axis=0, tiled=True)  7.3 us
    pallas_call x1, Pallas kernels, input_backward(): pl.pallas_call(input_kernel, grid=(hist,), in_specs=[block(denc), whole(w...  6.69 us
  transfers between devices with their start and end apart: 15, of which 6 were waited for; matrix products, arithmetic and copies ran while one was open for 3% of the time, Pallas kernels for 18%

profile of v5, /device:TPU:0, one launch (start us, length us, event | category | flops | bytes accessed | tf_op | source)
XLA Modules:
  0.0 114.4 jit_solution(14734760307072987461)
XLA Ops:
  0.6 2.8 %route.1 = (bf16[512,1152]{1,0:T(8,128)(2,1)}, bf16[512,256]{1,0:T(8,128)(2,1)}) custom-call(s32[1,256]{1,0:T(1,128)} %bitcast.49, s32[1,256]{1,0:T(1,128)} %bitcast.50, s32[1,256]{1,0:T(1,128)} %bitcast.51, bf16[256,512]{1,0:T(8,128)(2,1)} %cand_ref.1, bf16[256,512]{1,0:T(8,128)(2,1)} %cot_ref.1), custom_call_target="tpu_custom_call" | custom-call | flops 2000000000 | bytes 2097152 | tf_op jit(solution)/shard_map/route/pallas_call | solution.py:92
  3.5 7.3 %all-to-all-start = ((bf16[32,16,1152]{2,1,0:T(8,128)(2,1)}), bf16[32,16,1152]{2,1,0:T(8,128)(2,1)S(1)}, u32[]{:S(2)}, u32[]{:S(2)}) async-start(bf16[32,16,1152]{2,1,0:T(8,128)(2,1)} %bitcast.28), calls=%async_computation | async-start | bytes 2359296 | tf_op jit(solution)/shard_map/all_to_all | solution.py:539
  10.9 1.0 fusion.perm_ref
  11.8 0.1 fusion.1.refs_1_
  12.0 0.0 copy-start
  12.0 14.3 %forward.1 = (bf16[4,256,512]{2,1,0:T(8,128)(2,1)}, bf16[4,256,1024]{2,1,0:T(8,128)(2,1)}, bf16[4,512,256]{2,1,0:T(8,128)(2,1)}, bf16[4,256,512]{2,1,0:T(8,128)(...) custom-call(bf16[4,256,512]{2,1,0:T(8,128)(2,1)} %x_ref.1, ...), custom_call_target="tpu_custom_call" | custom-call | flops 17999998976 | bytes 24000000 | tf_op jit(solution)/shard_map/forward/pallas_call | solution.py:180
  26.2 14.9 %all-to-all-done = bf16[32,16,1152]{2,1,0:T(8,128)(2,1)S(1)} async-done(((bf16[32,16,1152]{2,1,0:T(8,128)(2,1)}), bf16[32,16,1152]{2,1,0:T(8,128)(2,1)S(1)}, u32[]{:S(2)}, u32[]{:S(2)}) %all-to-all-start) | async-done | bytes 1179680 | tf_op jit(solution)/shard_map/all_to_all | solution.py:539
  41.2 0.0 copy-start.9
  41.2 1.1 copy-done.9
  42.2 0.0 copy-done
  42.2 0.0 copy-start.3
  42.2 1.2 %copy-done.3 = bf16[4,256,512]{2,1,0:T(8,128)(2,1)S(1)} copy-done((bf16[4,256,512]{2,1,0:T(8,128)(2,1)S(1)}, bf16[4,256,512]{2,1,0:T(8,128)(2,1)}, u32[]{:S(2)}) %copy-start.3) | copy-done | bytes 1048600
  43.5 0.0 copy-start.4
  43.5 1.2 %copy-done.4 = bf16[4,256,512]{2,1,0:T(8,128)(2,1)S(1)} copy-done((bf16[4,256,512]{2,1,0:T(8,128)(2,1)S(1)}, bf16[4,256,512]{2,1,0:T(8,128)(2,1)}, u32[]{:S(2)}) %copy-start.4) | copy-done | bytes 1048600
  44.7 0.0 copy-start.5
  44.7 1.2 %copy-done.5 = bf16[4,256,512]{2,1,0:T(8,128)(2,1)S(1)} copy-done((bf16[4,256,512]{2,1,0:T(8,128)(2,1)S(1)}, bf16[4,256,512]{2,1,0:T(8,128)(2,1)}, u32[]{:S(2)}) %copy-start.5) | copy-done | bytes 1048600
  45.9 0.0 copy-start.6
  45.9 1.2 %copy-done.6 = bf16[4,256,512]{2,1,0:T(8,128)(2,1)S(1)} copy-done((bf16[4,256,512]{2,1,0:T(8,128)(2,1)S(1)}, bf16[4,256,512]{2,1,0:T(8,128)(2,1)}, u32[]{:S(2)}) %copy-start.6) | copy-done | bytes 1048600
  47.1 0.0 copy-start.7
  47.1 1.2 %copy-done.7 = bf16[4,256,512]{2,1,0:T(8,128)(2,1)S(1)} copy-done((bf16[4,256,512]{2,1,0:T(8,128)(2,1)S(1)}, bf16[4,256,512]{2,1,0:T(8,128)(2,1)}, u32[]{:S(2)}) %copy-start.7) | copy-done | bytes 1048600
  48.4 0.0 copy-start.8
  48.4 1.2 %copy-done.8 = bf16[4,256,512]{2,1,0:T(8,128)(2,1)S(1)} copy-done((bf16[4,256,512]{2,1,0:T(8,128)(2,1)S(1)}, bf16[4,256,512]{2,1,0:T(8,128)(2,1)}, u32[]{:S(2)}) %copy-start.8) | copy-done | bytes 1048600
  49.6 22.3 %owner_backward.1 = (bf16[256,512]{1,0:T(8,128)(2,1)S(1)}, bf16[256,512]{1,0:T(8,128)(2,1)S(1)}, bf16[4,256,512]{2,1,0:T(8,128)(2,1)S(1)}, bf16[1024,1536]{1,0:T...) custom-call(bf16[512,1152]{1,0:T(8,128)(2,1)} %bitcast.27, ...), custom_call_target="tpu_custom_call" | custom-call | flops 30000001024 | bytes 30000000 | tf_op jit(solution)/shard_map/owner_backward/pallas_call | solution.py:409
  71.9 0.0 copy-start.1
  71.9 0.0 copy-start.2
  72.0 3.2 %collective-permute-start = (bf16[256,2560]{1,0:T(8,128)(2,1)}, bf16[256,2560]{1,0:T(8,128)(2,1)S(1)}, u32[]{:S(2)}, u32[]{:S(2)}) collective-permute-start(bf16[256,2560]{1,0:T(8,128)(2,1)} %get-tuple-element.55), channel_id=1, source_target_pairs={{0,8},{8,0},{1,9},{9,1},{2,10},{10,2},{3,11},{11,3},{4,12},{12,4},... | collective-permute-start | bytes 3932168 | tf_op jit(solution)/shard_map/ppermute | solution.py:518
  75.2 2.8 %collective-permute-done = bf16[256,2560]{1,0:T(8,128)(2,1)S(1)} collective-permute-done((bf16[256,2560]{1,0:T(8,128)(2,1)}, bf16[256,2560]{1,0:T(8,128)(2,1)S(1)}, u32[]{:S(2)}, u32[]{:S(2)}) %collective-permute-start) | collective-permute-done | bytes 1310752 | tf_op jit(solution)/shard_map/ppermute | solution.py:518
  78.0 1.7 %add_convert_fusion = bf16[256,2560]{1,0:T(8,128)(2,1)S(1)} fusion(bf16[256,2560]{1,0:T(8,128)(2,1)S(1)} %collective-permute-done, bf16[256,2560]{1,0:T(8,128)(2,1)} %get-tuple-element.54), kind=kLoop, calls=%fused_computation | loop fusion | flops 2621440 | bytes 3932160 | tf_op jit(solution)/shard_map/convert_element_type | solution.py:503
  79.7 0.0 copy-done.1
  79.7 0.0 copy-done.2
  79.7 0.4 collective-permute-start.1
  80.2 0.1 fusion.83
  80.3 0.1 collective-permute-start.7
  80.4 0.1 collective-permute-start.6
  80.5 3.4 %collective-permute-start.5 = (bf16[64,2560]{1,0:T(8,128)(2,1)S(1)}, bf16[64,2560]{1,0:T(8,128)(2,1)S(1)}, u32[]{:S(2)}, u32[]{:S(2)}) collective-permute-start(bf16[64,2560]{1,0:T(8,128)(2,1)S(1)} %get-tuple-element.76), channel_id=1, source_target_pairs={{0,1},{1,0},{16,17},{17,16},{2,3},{3,2},{18,19},{19,18},{4,5},{5,4... | collective-permute-start | bytes 983048 | tf_op jit(solution)/shard_map/ppermute | solution.py:518
  83.9 0.0 collective-permute-done.1
  83.9 0.1 collective-permute-start.2
  84.0 0.1 collective-permute-start.3
  84.1 7.7 %collective-permute-done.7 = bf16[64,2560]{1,0:T(8,128)(2,1)S(1)} collective-permute-done((bf16[64,2560]{1,0:T(8,128)(2,1)S(1)}, bf16[64,2560]{1,0:T(8,128)(2,1)S(1)}, u32[]{:S(2)}, u32[]{:S(2)}) %collective-permute-start.7) | collective-permute-done | bytes 327712 | tf_op jit(solution)/shard_map/ppermute | solution.py:518
  91.9 0.0 collective-permute-start.4
  91.9 6.7 %input_backward.1 = bf16[4,256,512]{2,1,0:T(8,128)(2,1)} custom-call(bf16[4,256,512]{2,1,0:T(8,128)(2,1)} %copy-done.1, bf16[512,2048]{1,0:T(8,128)(2,1)} %win_ref.3, bf16[1024,1536]{1,0:T(8,128)(2,1)} %get-tuple-element.62.dpre_ref, bf16[512,1024]{1,0:T(8,128)(2,1)} %copy-done.2), custom_call_target="tpu_custom_call" | custom-call | flops 6000000000 | bytes 8000000 | tf_op jit(solution)/shard_map/input_backward/pallas_call | solution.py:442
  98.6 0.0 collective-permute-done.6
  98.6 0.0 collective-permute-done.5
  98.6 0.0 collective-permute-done.2
  98.6 0.0 collective-permute-done.3
  98.6 0.0 collective-permute-done.4
  98.7 0.1 collective-permute-start.8
  98.8 0.6 collective-permute-start.9
  99.4 0.2 add_convert_fusion.1
  99.6 0.0 copy-start.10
  99.6 2.1 %collective-permute-start.11 = (bf16[16,2560]{1,0:T(8,128)(2,1)S(1)}, bf16[16,2560]{1,0:T(8,128)(2,1)S(1)}, u32[]{:S(2)}, u32[]{:S(2)}) collective-permute-start(bf16[16,2560]{1,0:T(8,128)(2,1)S(1)} %get-tuple-element.78), channel_id=1, source_target_pairs={{0,2},{2,4},{4,6},{6,0},{1,3},{3,5},{5,7},{7,1},{8,10},{10,12},{12... | collective-permute-start | bytes 245768 | tf_op jit(solution)/shard_map/ppermute | solution.py:518
  101.7 1.8 %collective-permute-start.13 = (bf16[16,2560]{1,0:T(8,128)(2,1)S(1)}, bf16[16,2560]{1,0:T(8,128)(2,1)S(1)}, u32[]{:S(2)}, u32[]{:S(2)}) collective-permute-start(bf16[16,2560]{1,0:T(8,128)(2,1)S(1)} %get-tuple-element.79), channel_id=1, source_target_pairs={{0,6},{2,0},{4,2},{6,4},{1,7},{3,1},{5,3},{7,5},{8,14},{10,8},{12,... | collective-permute-start | bytes 245768 | tf_op jit(solution)/shard_map/ppermute | solution.py:518
  103.5 0.0 collective-permute-start.12
  103.5 3.4 %collective-permute-done.11 = bf16[16,2560]{1,0:T(8,128)(2,1)S(1)} collective-permute-done((bf16[16,2560]{1,0:T(8,128)(2,1)S(1)}, bf16[16,2560]{1,0:T(8,128)(2,1)S(1)}, u32[]{:S(2)}, u32[]{:S(2)}) %collective-permute-start.11) | collective-permute-done | bytes 81952 | tf_op jit(solution)/shard_map/ppermute | solution.py:518
  107.0 2.0 %collective-permute-start.10 = (bf16[128,512]{1,0:T(8,128)(2,1)S(1)}, bf16[128,512]{1,0:T(8,128)(2,1)S(1)}, u32[]{:S(2)}, u32[]{:S(2)}) collective-permute-start(bf16[128,512]{1,0:T(8,128)(2,1)S(1)} %pad_maximum_fusion.6), channel_id=1, source_target_pairs={{0,17},{1,16},{16,1},{17,0},{2,19},{3,18},{18,3},{19,2},{4,21},{5,... | collective-permute-start | bytes 393224 | tf_op jit(solution)/shard_map/ppermute | solution.py:518
  108.9 0.0 collective-permute-done.13
  108.9 1.1 collective-permute-done.12
  110.0 0.7 convert_add_fusion
  110.7 0.6 convert_add_fusion.1
  111.3 0.0 collective-permute-done.8
  111.3 0.0 collective-permute-done.9
  111.4 1.5 %collective-permute-done.10 = bf16[128,512]{1,0:T(8,128)(2,1)S(1)} collective-permute-done((bf16[128,512]{1,0:T(8,128)(2,1)S(1)}, bf16[128,512]{1,0:T(8,128)(2,1)S(1)}, u32[]{:S(2)}, u32[]{:S(2)}) %collective-permute-start.10) | collective-permute-done | bytes 131104 | tf_op jit(solution)/shard_map/ppermute | solution.py:518
  112.8 0.0 copy-done.10
  112.8 1.5 %convolution_convert_fusion = bf16[256,512]{1,0:T(8,128)(2,1)} fusion(bf16[512,512]{1,0:T(8,128)(2,1)S(1)} %constant_dynamic-update-slice_fusion, bf16[512,256]{1,0:T(8,128)(2,1)S(1)} %copy-done.10, s32[512]{0:T(512)S(1)} %fusion.56), kind=kOutput, calls=%fused_computation.1 | convolution fusion | flops 268959744 | bytes 1050624 | tf_op jit(solution)/shard_map/dot_general | solution.py:566
  (24 shorter events, 0.3 us)
Async XLA Ops:
  3.5 37.7 %all-to-all-start = ((bf16[32,16,1152]{2,1,0:T(8,128)(2,1)}), bf16[32,16,1152]{2,1,0:T(8,128)(2,1)S(1)}, u32[]{:S(2)}, u32[]{:S(2)}) async-start(bf16[32,16,1152]{2,1,0:T(8,128)(2,1)} %bitcast.28), calls=%async_computation | async-start | bytes 2359296 | tf_op jit(solution)/shard_map/all_to_all | solution.py:539
  12.0 30.3 %copy-start = (bf16[512,512]{1,0:T(8,128)(2,1)S(1)}, bf16[512,512]{1,0:T(8,128)(2,1)}, u32[]{:S(2)}) copy-start(bf16[512,512]{1,0:T(8,128)(2,1)} %refs_2_.1) | copy-start | bytes 1572868
  41.2 1.1 copy-start.9
  42.2 1.2 %copy-start.3 = (bf16[4,256,512]{2,1,0:T(8,128)(2,1)S(1)}, bf16[4,256,512]{2,1,0:T(8,128)(2,1)}, u32[]{:S(2)}) copy-start(bf16[4,256,512]{2,1,0:T(8,128)(2,1)} %get-tuple-element.40.refs_0_) | copy-start | bytes 3145732
  43.5 1.2 %copy-start.4 = (bf16[4,256,512]{2,1,0:T(8,128)(2,1)S(1)}, bf16[4,256,512]{2,1,0:T(8,128)(2,1)}, u32[]{:S(2)}) copy-start(bf16[4,256,512]{2,1,0:T(8,128)(2,1)} %get-tuple-element.44.refs_6_) | copy-start | bytes 3145732
  44.7 1.2 %copy-start.5 = (bf16[4,256,512]{2,1,0:T(8,128)(2,1)S(1)}, bf16[4,256,512]{2,1,0:T(8,128)(2,1)}, u32[]{:S(2)}) copy-start(bf16[4,256,512]{2,1,0:T(8,128)(2,1)} %get-tuple-element.45.refs_7_) | copy-start | bytes 3145732
  45.9 1.2 %copy-start.6 = (bf16[4,256,512]{2,1,0:T(8,128)(2,1)S(1)}, bf16[4,256,512]{2,1,0:T(8,128)(2,1)}, u32[]{:S(2)}) copy-start(bf16[4,256,512]{2,1,0:T(8,128)(2,1)} %get-tuple-element.41.refs_3_) | copy-start | bytes 3145732
  47.1 1.2 %copy-start.7 = (bf16[4,256,512]{2,1,0:T(8,128)(2,1)S(1)}, bf16[4,256,512]{2,1,0:T(8,128)(2,1)}, u32[]{:S(2)}) copy-start(bf16[4,256,512]{2,1,0:T(8,128)(2,1)} %get-tuple-element.42.refs_4_) | copy-start | bytes 3145732
  48.4 1.2 %copy-start.8 = (bf16[4,256,512]{2,1,0:T(8,128)(2,1)S(1)}, bf16[4,256,512]{2,1,0:T(8,128)(2,1)}, u32[]{:S(2)}) copy-start(bf16[4,256,512]{2,1,0:T(8,128)(2,1)} %get-tuple-element.43.refs_5_) | copy-start | bytes 3145732
  71.9 7.8 %copy-start.1 = (bf16[4,256,512]{2,1,0:T(8,128)(2,1)}, bf16[4,256,512]{2,1,0:T(8,128)(2,1)S(1)}, u32[]{:S(2)}) copy-start(bf16[4,256,512]{2,1,0:T(8,128)(2,1)S(1)} %get-tuple-element.61.denc_ref) | copy-start | bytes 3145732
  71.9 7.8 %copy-start.2 = (bf16[512,1024]{1,0:T(8,128)(2,1)}, bf16[512,1024]{1,0:T(8,128)(2,1)S(1)}, u32[]{:S(2)}) copy-start(bf16[512,1024]{1,0:T(8,128)(2,1)S(1)} %get-tuple-element.63.dk_ref) | copy-start | bytes 3145732
  72.0 6.1 %collective-permute-start = (bf16[256,2560]{1,0:T(8,128)(2,1)}, bf16[256,2560]{1,0:T(8,128)(2,1)S(1)}, u32[]{:S(2)}, u32[]{:S(2)}) collective-permute-start(bf16[256,2560]{1,0:T(8,128)(2,1)} %get-tuple-element.55), channel_id=1, source_target_pairs={{0,8},{8,0},{1,9},{9,1},{2,10},{10,2},{3,11},{11,3},{4,12},{12,4},... | collective-permute-start | bytes 3932168 | tf_op jit(solution)/shard_map/ppermute | solution.py:518
  79.7 4.1 %collective-permute-start.1 = (bf16[256,512]{1,0:T(8,128)(2,1)S(1)}, bf16[256,512]{1,0:T(8,128)(2,1)S(1)}, u32[]{:S(2)}, u32[]{:S(2)}) collective-permute-start(bf16[256,512]{1,0:T(8,128)(2,1)S(1)} %get-tuple-element.59), channel_id=1, source_target_pairs={{0,8},{8,0},{1,9},{9,1},{2,10},{10,2},{3,11},{11,3},{4,12},{12,4},... | collective-permute-start | bytes 786440 | tf_op jit(solution)/shard_map/ppermute | solution.py:518
  80.3 11.6 %collective-permute-start.7 = (bf16[64,2560]{1,0:T(8,128)(2,1)S(1)}, bf16[64,2560]{1,0:T(8,128)(2,1)S(1)}, u32[]{:S(2)}, u32[]{:S(2)}) collective-permute-start(bf16[64,2560]{1,0:T(8,128)(2,1)S(1)} %get-tuple-element.74), channel_id=1, source_target_pairs={{0,17},{1,16},{16,1},{17,0},{2,19},{3,18},{18,3},{19,2},{4,21},{5,... | collective-permute-start | bytes 983048 | tf_op jit(solution)/shard_map/ppermute | solution.py:518
  80.4 18.2 %collective-permute-start.6 = (bf16[64,2560]{1,0:T(8,128)(2,1)S(1)}, bf16[64,2560]{1,0:T(8,128)(2,1)S(1)}, u32[]{:S(2)}, u32[]{:S(2)}) collective-permute-start(bf16[64,2560]{1,0:T(8,128)(2,1)S(1)} %get-tuple-element.75), channel_id=1, source_target_pairs={{0,16},{1,17},{16,0},{17,1},{2,18},{3,19},{18,2},{19,3},{4,20},{5,... | collective-permute-start | bytes 983048 | tf_op jit(solution)/shard_map/ppermute | solution.py:518
  80.5 18.1 %collective-permute-start.5 = (bf16[64,2560]{1,0:T(8,128)(2,1)S(1)}, bf16[64,2560]{1,0:T(8,128)(2,1)S(1)}, u32[]{:S(2)}, u32[]{:S(2)}) collective-permute-start(bf16[64,2560]{1,0:T(8,128)(2,1)S(1)} %get-tuple-element.76), channel_id=1, source_target_pairs={{0,1},{1,0},{16,17},{17,16},{2,3},{3,2},{18,19},{19,18},{4,5},{5,4... | collective-permute-start | bytes 983048 | tf_op jit(solution)/shard_map/ppermute | solution.py:518
  83.9 14.7 %collective-permute-start.2 = (bf16[128,512]{1,0:T(8,128)(2,1)S(1)}, bf16[128,512]{1,0:T(8,128)(2,1)S(1)}, u32[]{:S(2)}, u32[]{:S(2)}) collective-permute-start(bf16[128,512]{1,0:T(8,128)(2,1)S(1)} %pad_maximum_fusion.1), channel_id=1, source_target_pairs={{0,2},{2,4},{4,6},{6,0},{1,3},{3,5},{5,7},{7,1},{8,10},{10,12},{12... | collective-permute-start | bytes 393224 | tf_op jit(solution)/shard_map/ppermute | solution.py:518
  84.0 14.6 %collective-permute-start.3 = (bf16[128,512]{1,0:T(8,128)(2,1)S(1)}, bf16[128,512]{1,0:T(8,128)(2,1)S(1)}, u32[]{:S(2)}, u32[]{:S(2)}) collective-permute-start(bf16[128,512]{1,0:T(8,128)(2,1)S(1)} %pad_maximum_fusion.2), channel_id=1, source_target_pairs={{0,4},{2,6},{4,0},{6,2},{1,5},{3,7},{5,1},{7,3},{8,12},{10,14},{12... | collective-permute-start | bytes 393224 | tf_op jit(solution)/shard_map/ppermute | solution.py:518
  91.9 6.7 %collective-permute-start.4 = (bf16[128,512]{1,0:T(8,128)(2,1)S(1)}, bf16[128,512]{1,0:T(8,128)(2,1)S(1)}, u32[]{:S(2)}, u32[]{:S(2)}) collective-permute-start(bf16[128,512]{1,0:T(8,128)(2,1)S(1)} %pad_maximum_fusion.3), channel_id=1, source_target_pairs={{0,6},{2,0},{4,2},{6,4},{1,7},{3,1},{5,3},{7,5},{8,14},{10,8},{12,... | collective-permute-start | bytes 393224 | tf_op jit(solution)/shard_map/ppermute | solution.py:518
  98.7 12.6 %collective-permute-start.8 = (bf16[128,512]{1,0:T(8,128)(2,1)S(1)}, bf16[128,512]{1,0:T(8,128)(2,1)S(1)}, u32[]{:S(2)}, u32[]{:S(2)}) collective-permute-start(bf16[128,512]{1,0:T(8,128)(2,1)S(1)} %pad_maximum_fusion.4), channel_id=1, source_target_pairs={{0,1},{1,0},{16,17},{17,16},{2,3},{3,2},{18,19},{19,18},{4,5},{5,4... | collective-permute-start | bytes 393224 | tf_op jit(solution)/shard_map/ppermute | solution.py:518
  98.8 12.5 %collective-permute-start.9 = (bf16[128,512]{1,0:T(8,128)(2,1)S(1)}, bf16[128,512]{1,0:T(8,128)(2,1)S(1)}, u32[]{:S(2)}, u32[]{:S(2)}) collective-permute-start(bf16[128,512]{1,0:T(8,128)(2,1)S(1)} %pad_maximum_fusion.5), channel_id=1, source_target_pairs={{0,16},{1,17},{16,0},{17,1},{2,18},{3,19},{18,2},{19,3},{4,20},{5,... | collective-permute-start | bytes 393224 | tf_op jit(solution)/shard_map/ppermute | solution.py:518
  99.6 13.3 %copy-start.10 = (bf16[512,256]{1,0:T(8,128)(2,1)S(1)}, bf16[512,256]{1,0:T(8,128)(2,1)}, u32[]{:S(2)}) copy-start(bf16[512,256]{1,0:T(8,128)(2,1)} %get-tuple-element.65) | copy-start | bytes 786436
  99.6 7.4 %collective-permute-start.11 = (bf16[16,2560]{1,0:T(8,128)(2,1)S(1)}, bf16[16,2560]{1,0:T(8,128)(2,1)S(1)}, u32[]{:S(2)}, u32[]{:S(2)}) collective-permute-start(bf16[16,2560]{1,0:T(8,128)(2,1)S(1)} %get-tuple-element.78), channel_id=1, source_target_pairs={{0,2},{2,4},{4,6},{6,0},{1,3},{3,5},{5,7},{7,1},{8,10},{10,12},{12... | collective-permute-start | bytes 245768 | tf_op jit(solution)/shard_map/ppermute | solution.py:518
  101.7 7.3 %collective-permute-start.13 = (bf16[16,2560]{1,0:T(8,128)(2,1)S(1)}, bf16[16,2560]{1,0:T(8,128)(2,1)S(1)}, u32[]{:S(2)}, u32[]{:S(2)}) collective-permute-start(bf16[16,2560]{1,0:T(8,128)(2,1)S(1)} %get-tuple-element.79), channel_id=1, source_target_pairs={{0,6},{2,0},{4,2},{6,4},{1,7},{3,1},{5,3},{7,5},{8,14},{10,8},{12,... | collective-permute-start | bytes 245768 | tf_op jit(solution)/shard_map/ppermute | solution.py:518
  103.5 6.5 %collective-permute-start.12 = (bf16[16,2560]{1,0:T(8,128)(2,1)S(1)}, bf16[16,2560]{1,0:T(8,128)(2,1)S(1)}, u32[]{:S(2)}, u32[]{:S(2)}) collective-permute-start(bf16[16,2560]{1,0:T(8,128)(2,1)S(1)} %get-tuple-element.80), channel_id=1, source_target_pairs={{0,4},{2,6},{4,0},{6,2},{1,5},{3,7},{5,1},{7,3},{8,12},{10,14},{12... | collective-permute-start | bytes 245768 | tf_op jit(solution)/shard_map/ppermute | solution.py:518
  107.0 5.9 %collective-permute-start.10 = (bf16[128,512]{1,0:T(8,128)(2,1)S(1)}, bf16[128,512]{1,0:T(8,128)(2,1)S(1)}, u32[]{:S(2)}, u32[]{:S(2)}) collective-permute-start(bf16[128,512]{1,0:T(8,128)(2,1)S(1)} %pad_maximum_fusion.6), channel_id=1, source_target_pairs={{0,17},{1,16},{16,1},{17,0},{2,19},{3,18},{18,3},{19,2},{4,21},{5,... | collective-permute-start | bytes 393224 | tf_op jit(solution)/shard_map/ppermute | solution.py:518

commit v6 on v5

--- a/solution.py
+++ b/solution.py
@@ -308,16 +308,16 @@
             dk_ref[mine, here] = (d_k * slope_t_ref[at, mine].astype(f32)).astype(bf16)
 
 
-def owner_kernel(recv_ref, *refs):
-    n_in, n_out = 15, 7
+def owner_kernel(*refs):
+    n_in, n_out = 15, 6
     sources, outs, refs = refs[:n_in], refs[n_in : n_in + n_out], refs[n_in + n_out :]
     held, refs = refs[:n_in], refs[n_in:]
     (
-        enc_ref, order_ref, wout_ref, normed_ref, nu_ref, gi_ref, v_ref, k_ref, q_t_ref,
+        recv_ref, enc_ref, wout_ref, normed_ref, nu_ref, gi_ref, v_ref, k_ref, q_t_ref,
         attn_t_ref, grad_ref, slope_ref, slope_t_ref, mt_ref, xt_ref,
     ) = held
-    grouped_ref, turned_ref, dmix_ref, dq_ref, dq_far_ref, denc_ref, dpre_ref, dk_ref, keep_ref, send_ref, sem_in, sem_out = refs
-    dq_hbm, dq_far_hbm, denc_hbm, dpre_hbm, dk_hbm, keep_hbm, send_hbm = outs
+    grouped_ref, turned_ref, dmix_ref, dq_ref, denc_ref, dpre_ref, dk_ref, keep_ref, send_ref, sem_in, sem_out = refs
+    dq_hbm, denc_hbm, dpre_hbm, dk_hbm, keep_hbm, send_hbm = outs
     hist, seq, width = enc_ref.shape
     slots, padded = recv_ref.shape[0], grouped_ref.shape[0]
     kept = keep_ref.shape[0]
@@ -333,8 +333,9 @@
         copy.start()
     grouped_ref[...] = jnp.zeros_like(grouped_ref)
     turned_ref[...] = jnp.zeros_like(turned_ref)
+    first[0].wait()
     dest, dest_row, starts, tiles = group_slots(recv_ref, hist)
-    first[0].wait()
+    first[1].wait()
 
     def one_tile(tile, carry):
         target_tile(tile, starts, dest_row, recv_ref, enc_ref, grouped_ref, turned_ref)
@@ -344,11 +345,7 @@
     for h in range(hist):
         denc_ref[h] = jnp.transpose(turned_ref[h]).astype(bf16)
     back = (dest == iota((slots, padded), 1)).astype(f32).astype(bf16)
-    d_query = dot_nn(back, grouped_ref[...]).astype(bf16)
-    near = dq_ref.shape[0]
-    first[1].wait()
-    dq_ref[...] = dot_nn(order_ref[:near], d_query).astype(bf16)
-    dq_far_ref[...] = dot_nn(order_ref[near:], d_query).astype(bf16)
+    dq_ref[...] = dot_nn(back, grouped_ref[...]).astype(bf16)
     stores = []
 
     def store(source, dest):
@@ -358,7 +355,6 @@
 
     store(denc_ref, denc_hbm)
     store(dq_ref, dq_hbm)
-    store(dq_far_ref, dq_far_hbm)
     for copy in first[2:]:
         copy.wait()
     norm_backward(denc_ref, wout_ref, normed_ref, nu_ref, gi_ref, dmix_ref, dpre_ref)
@@ -390,16 +386,15 @@
         copy.wait()
 
 
-def owner_backward(order, recv, enc, w_out, state, mt, xt, kept):
+def owner_backward(recv, enc, w_out, state, mt, xt, kept):
     hist, seq, width = enc.shape
     slots = recv.shape[0]
     rows = hist * seq
     padded = ((slots - hist) // TILE + hist) * TILE
-    operands = (enc, order, w_out) + state + (mt, xt)
+    operands = (recv, enc, w_out) + state + (mt, xt)
     raw = pl.BlockSpec(memory_space=pl.ANY)
     outs = [
-        jax.ShapeDtypeStruct((slots // 2, width), bf16),
-        jax.ShapeDtypeStruct((slots - slots // 2, width), bf16),
+        jax.ShapeDtypeStruct((slots, width), bf16),
         jax.ShapeDtypeStruct(enc.shape, bf16),
         jax.ShapeDtypeStruct((rows, 3 * width), bf16),
         jax.ShapeDtypeStruct((width, rows), bf16),
@@ -409,7 +404,7 @@
     return pl.pallas_call(
         owner_kernel,
         grid=(1,),
-        in_specs=[pl.BlockSpec(memory_space=pltpu.VMEM)] + [raw] * len(operands),
+        in_specs=[raw] * len(operands),
         out_specs=[raw] * len(outs),
         out_shape=outs,
         scratch_shapes=[pltpu.VMEM(a.shape, a.dtype) for a in operands]
@@ -421,12 +416,12 @@
         + [pltpu.VMEM(a.shape, a.dtype) for a in outs]
         + [
             pltpu.SemaphoreType.DMA((7 * hist + 8,)),
-            pltpu.SemaphoreType.DMA((2 * hist + 13,)),
+            pltpu.SemaphoreType.DMA((2 * hist + 12,)),
         ],
-        compiler_params=params(44),
+        compiler_params=params(60),
         cost_estimate=cost(30e9, 30e6),
         name="owner_backward",
-    )(recv, *operands)
+    )(*operands)
 
 
 def input_kernel(denc_ref, win_ref, dpre_ref, dk_ref, out_ref):
@@ -532,7 +527,7 @@
     kept = width // lax.axis_size(AXES[1])
     after = lax.optimization_barrier
 
-    sizes = n_y, n_core, n_z, n_x = tuple(lax.axis_size(a) for a in AXES)
+    n_y, n_core, n_z, n_x = (lax.axis_size(a) for a in AXES)
     core, line, plane = AXES[1:2], AXES[2:3], (AXES[0], AXES[3])
     send, pick = route(owner_ids, hist_slot, lengths, candidates, cotangent, devices, capacity)
     shaped = send.reshape(devices, capacity, send.shape[1])
@@ -545,12 +540,11 @@
         histories, weight_in, weight_out, perm
     )
     state = (normed, nu, gi, v, k, q_t, attn_t, grad, slope, slope_t)
-    near, far, d_enc, dpre, dk, keep, send = owner_backward(
-        leaving, recv, enc, weight_out, state, mt, xt, kept
-    )
+    d_query, d_enc, dpre, dk, keep, send = owner_backward(recv, enc, weight_out, state, mt, xt, kept)
+    d_query = dot_nn(leaving, d_query).astype(bf16)
     rows = core_stage(keep, send)
-    d_enc, rows, near, far = after((d_enc, rows, near, far))
-    back = [cut_rows(b, n_z) for b in send_blocks([near] + cut_rows(far, n_core - 1), core)]
+    d_enc, rows, d_query = after((d_enc, rows, d_query))
+    back = [cut_rows(b, n_z) for b in send_blocks(cut_rows(d_query, n_core), core)]
     back = [jnp.concatenate([b[d] for b in back], axis=0) for d in range(n_z)]
     d_inputs = input_backward(d_enc, weight_in, dpre, dk)
     back = send_blocks(back, line)

time: 115 us -> 102 us (0.89)
  local copies, waits for them, and re-layouts: 8.67 us -> 1.29 us
  waiting for transfers between devices: 31.5 us -> 25.2 us
  starting transfers between devices: 21.1 us -> 23.2 us
  other arithmetic: 4.44 us -> 2.92 us
  matrix products: 1.52 us -> 3.04 us
  Pallas kernels: 46.1 us -> 44.8 us
    unnamed x28 -> x12, local copies, waits for them, and re-layouts: 8.46 us -> 1.06 us
    ppermute x14, waiting for transfers between devices: 16.6 us -> 10 us  [send_blocks(): parts.append(lax.ppermute(blocks[d], axes, pairs))]
    ppermute x14, starting transfers between devices: 13.8 us -> 15.9 us  [send_blocks(): parts.append(lax.ppermute(blocks[d], axes, pairs))]
    dot_general x0 -> x1, matrix products: none -> 1.52 us  [dot_nn(): lax.dot_general(a, b, (((1,), (0,)), ((), ())), preferred_element_type=f32)]
    convert_element_type x1, other arithmetic: 1.68 us -> 0.32 us  [core_stage(): add_up(send_blocks([keep] + cut_rows(send, lax.axis_size(AXES[1]) - 1), A...]
    pallas_call x1, Pallas kernels: 22.3 us -> 21.1 us  [owner_backward(): pl.pallas_call(owner_kernel, grid=(1,), in_specs=[raw] * len(operands), o...]
  transfers between devices with their start and end apart: 15 -> 15, of which waited for: 6 -> 7; matrix products, arithmetic and copies ran while one was open for 3% -> 4% of each run, Pallas kernels for 18% -> 21%
where the time goes in v6:
time: 102 us; the launch traced here: 101 us
  Pallas kernels  44.8 us (44%)
  waiting for transfers between devices  25.2 us (25%)
  starting transfers between devices  23.2 us (23%)
  matrix products  3.04 us (3%)
  other arithmetic  2.92 us (3%)
  local copies, waits for them, and re-layouts  1.29 us (1%)
    pallas_call x1, Pallas kernels, owner_backward(): pl.pallas_call(owner_kernel, grid=(1,), in_specs=[raw] * len(operands), o...  21.1 us
    ppermute x14, starting transfers between devices, send_blocks(): parts.append(lax.ppermute(blocks[d], axes, pairs))  15.9 us
    all_to_all x1, waiting for transfers between devices, local(): recv = lax.all_to_all(shaped, AXES, split_axis=0, concat_axis=0, tiled=True)  15.2 us
    pallas_call x1, Pallas kernels, layer_forward(): pl.pallas_call(forward_kernel, grid=(hist,), in_specs=[row, whole(w_in.sh...  14.2 us
    ppermute x14, waiting for transfers between devices, send_blocks(): parts.append(lax.ppermute(blocks[d], axes, pairs))  10 us
    all_to_all x1, starting transfers between devices, local(): recv = lax.all_to_all(shaped, AXES, split_axis=0, concat_axis=0, tiled=True)  7.3 us
    pallas_call x1, Pallas kernels, input_backward(): pl.pallas_call(input_kernel, grid=(hist,), in_specs=[block(denc), whole(w...  6.69 us
    pallas_call x1, Pallas kernels, route(): pl.pallas_call(functools.partial(route_kernel, devices, capacity), grid=(...  2.86 us
  transfers between devices with their start and end apart: 15, of which 7 were waited for; matrix products, arithmetic and copies ran while one was open for 4% of the time, Pallas kernels for 21%

profile of v6, /device:TPU:0, one launch (start us, length us, event | category | flops | bytes accessed | tf_op | source)
XLA Modules:
  0.0 101.4 jit_solution(2710913079048824814)
XLA Ops:
  0.6 2.9 %route.1 = (bf16[512,1152]{1,0:T(8,128)(2,1)}, bf16[512,256]{1,0:T(8,128)(2,1)}) custom-call(s32[1,256]{1,0:T(1,128)} %bitcast.50, s32[1,256]{1,0:T(1,128)} %bitcast.51, s32[1,256]{1,0:T(1,128)} %bitcast.52, bf16[256,512]{1,0:T(8,128)(2,1)} %cand_ref.1, bf16[256,512]{1,0:T(8,128)(2,1)} %cot_ref.1), custom_call_target="tpu_custom_call" | custom-call | flops 2000000000 | bytes 2097152 | tf_op jit(solution)/shard_map/route/pallas_call | solution.py:92
  3.5 7.3 %all-to-all-start = ((bf16[32,16,1152]{2,1,0:T(8,128)(2,1)}), bf16[32,16,1152]{2,1,0:T(8,128)(2,1)S(1)}, u32[]{:S(2)}, u32[]{:S(2)}) async-start(bf16[32,16,1152]{2,1,0:T(8,128)(2,1)} %bitcast.29), calls=%async_computation | async-start | bytes 2359296 | tf_op jit(solution)/shard_map/all_to_all | solution.py:534
  10.8 1.0 fusion.perm_ref
  11.8 14.2 %forward.1 = (bf16[4,256,512]{2,1,0:T(8,128)(2,1)}, bf16[4,256,1024]{2,1,0:T(8,128)(2,1)}, bf16[4,512,256]{2,1,0:T(8,128)(2,1)}, bf16[4,256,512]{2,1,0:T(8,128)(...) custom-call(bf16[4,256,512]{2,1,0:T(8,128)(2,1)} %x_ref.1, ...), custom_call_target="tpu_custom_call" | custom-call | flops 17999998976 | bytes 24000000 | tf_op jit(solution)/shard_map/forward/pallas_call | solution.py:180
  26.0 15.2 %all-to-all-done = bf16[32,16,1152]{2,1,0:T(8,128)(2,1)S(1)} async-done(((bf16[32,16,1152]{2,1,0:T(8,128)(2,1)}), bf16[32,16,1152]{2,1,0:T(8,128)(2,1)S(1)}, u32[]{:S(2)}, u32[]{:S(2)}) %all-to-all-start) | async-done | bytes 1179680 | tf_op jit(solution)/shard_map/all_to_all | solution.py:534
  41.2 0.0 copy-start.1
  41.2 1.0 %copy-done.1 = bf16[32,16,1152]{2,1,0:T(8,128)(2,1)} copy-done((bf16[32,16,1152]{2,1,0:T(8,128)(2,1)}, bf16[32,16,1152]{2,1,0:T(8,128)(2,1)S(1)}, u32[]{:S(2)}) %copy-start.1) | copy-done | bytes 1179672
  42.2 21.1 %owner_backward.1 = (bf16[512,512]{1,0:T(8,128)(2,1)}, bf16[4,256,512]{2,1,0:T(8,128)(2,1)}, bf16[1024,1536]{1,0:T(8,128)(2,1)}, bf16[512,1024]{1,0:T(8,128)(2,1...) custom-call(bf16[512,1152]{1,0:T(8,128)(2,1)} %bitcast.28, bf16[4,256,512]{2,1,0:T(8,128)(2,1)} %get-tuple-element.38.refs_1_, ...), custom_call_target="tpu_custom_call" | custom-call | flops 30000001024 | bytes 30000000 | tf_op jit(solution)/shard_map/owner_backward/pallas_call | solution.py:404
  63.3 0.0 copy-start
  63.3 3.2 %collective-permute-start = (bf16[256,2560]{1,0:T(8,128)(2,1)}, bf16[256,2560]{1,0:T(8,128)(2,1)S(1)}, u32[]{:S(2)}, u32[]{:S(2)}) collective-permute-start(bf16[256,2560]{1,0:T(8,128)(2,1)} %get-tuple-element.53), channel_id=1, source_target_pairs={{0,8},{8,0},{1,9},{9,1},{2,10},{10,2},{3,11},{11,3},{4,12},{12,4},... | collective-permute-start | bytes 3932168 | tf_op jit(solution)/shard_map/ppermute | solution.py:513
  66.6 1.5 %convolution_convert_fusion = bf16[512,512]{1,0:T(8,128)(2,1)S(1)} fusion(bf16[512,512]{1,0:T(8,128)(2,1)} %get-tuple-element.54, s32[512]{0:T(512)S(1)} %fusion.33), kind=kOutput, calls=%fused_computation.1 | convolution fusion | flops 268959744 | bytes 1050624 | tf_op jit(solution)/shard_map/dot_general | solution.py:21
  68.1 1.3 %collective-permute-done = bf16[256,2560]{1,0:T(8,128)(2,1)S(1)} collective-permute-done((bf16[256,2560]{1,0:T(8,128)(2,1)}, bf16[256,2560]{1,0:T(8,128)(2,1)S(1)}, u32[]{:S(2)}, u32[]{:S(2)}) %collective-permute-start) | collective-permute-done | bytes 1310752 | tf_op jit(solution)/shard_map/ppermute | solution.py:513
  69.4 0.0 copy-done
  69.4 0.3 add_convert_fusion
  69.7 0.4 collective-permute-start.1
  70.2 0.1 fusion.83
  70.3 0.1 collective-permute-start.5
  70.4 0.1 collective-permute-start.6
  70.4 3.4 %collective-permute-start.7 = (bf16[64,2560]{1,0:T(8,128)(2,1)S(1)}, bf16[64,2560]{1,0:T(8,128)(2,1)S(1)}, u32[]{:S(2)}, u32[]{:S(2)}) collective-permute-start(bf16[64,2560]{1,0:T(8,128)(2,1)S(1)} %get-tuple-element.70), channel_id=1, source_target_pairs={{0,17},{1,16},{16,1},{17,0},{2,19},{3,18},{18,3},{19,2},{4,21},{5,... | collective-permute-start | bytes 983048 | tf_op jit(solution)/shard_map/ppermute | solution.py:513
  73.9 0.0 collective-permute-done.1
  73.9 0.1 collective-permute-start.4
  74.0 0.6 collective-permute-start.3
  74.6 6.3 %collective-permute-done.5 = bf16[64,2560]{1,0:T(8,128)(2,1)S(1)} collective-permute-done((bf16[64,2560]{1,0:T(8,128)(2,1)S(1)}, bf16[64,2560]{1,0:T(8,128)(2,1)S(1)}, u32[]{:S(2)}, u32[]{:S(2)}) %collective-permute-start.5) | collective-permute-done | bytes 327712 | tf_op jit(solution)/shard_map/ppermute | solution.py:513
  80.9 0.0 collective-permute-start.2
  80.9 6.7 %input_backward.1 = bf16[4,256,512]{2,1,0:T(8,128)(2,1)} custom-call(bf16[4,256,512]{2,1,0:T(8,128)(2,1)} %get-tuple-element.57.denc_ref, bf16[512,2048]{1,0:T(8,128)(2,1)} %win_ref.3, bf16[1024,1536]{1,0:T(8,128)(2,1)} %get-tuple-element.58.dpre_ref, bf16[512,1024]{1,0:T(8,128)(2,1)} %get-tuple-element.59.dk_ref), custom_call_target="tpu_custom_call" | custom-call | flops 6000000000 | bytes 8000000 | tf_op jit(solution)/shard_map/input_backward/pallas_call | solution.py:437
  87.6 0.0 collective-permute-done.6
  87.6 0.0 collective-permute-done.7
  87.6 0.0 collective-permute-done.4
  87.6 0.0 collective-permute-done.3
  87.6 0.0 collective-permute-done.2
  87.7 0.2 add_convert_fusion.1
  87.9 0.1 collective-permute-start.11
  87.9 4.4 %collective-permute-start.12 = (bf16[16,2560]{1,0:T(8,128)(2,1)S(1)}, bf16[16,2560]{1,0:T(8,128)(2,1)S(1)}, u32[]{:S(2)}, u32[]{:S(2)}) collective-permute-start(bf16[16,2560]{1,0:T(8,128)(2,1)S(1)} %get-tuple-element.80), channel_id=1, source_target_pairs={{0,4},{2,6},{4,0},{6,2},{1,5},{3,7},{5,1},{7,3},{8,12},{10,14},{12... | collective-permute-start | bytes 245768 | tf_op jit(solution)/shard_map/ppermute | solution.py:513
  92.3 0.0 collective-permute-start.13
  92.3 0.0 copy-start.2
  92.4 0.7 collective-permute-start.10
  93.1 1.6 %collective-permute-start.9 = (bf16[128,512]{1,0:T(8,128)(2,1)S(1)}, bf16[128,512]{1,0:T(8,128)(2,1)S(1)}, u32[]{:S(2)}, u32[]{:S(2)}) collective-permute-start(bf16[128,512]{1,0:T(8,128)(2,1)S(1)} %pad_maximum_fusion.5), channel_id=1, source_target_pairs={{0,16},{1,17},{16,0},{17,1},{2,18},{3,19},{18,2},{19,3},{4,20},{5,... | collective-permute-start | bytes 393224 | tf_op jit(solution)/shard_map/ppermute | solution.py:513
  94.7 0.1 collective-permute-done.11
  94.8 1.4 %collective-permute-start.8 = (bf16[128,512]{1,0:T(8,128)(2,1)S(1)}, bf16[128,512]{1,0:T(8,128)(2,1)S(1)}, u32[]{:S(2)}, u32[]{:S(2)}) collective-permute-start(bf16[128,512]{1,0:T(8,128)(2,1)S(1)} %pad_maximum_fusion.4), channel_id=1, source_target_pairs={{0,1},{1,0},{16,17},{17,16},{2,3},{3,2},{18,19},{19,18},{4,5},{5,4... | collective-permute-start | bytes 393224 | tf_op jit(solution)/shard_map/ppermute | solution.py:513
  96.1 1.1 %collective-permute-done.12 = bf16[16,2560]{1,0:T(8,128)(2,1)S(1)} collective-permute-done((bf16[16,2560]{1,0:T(8,128)(2,1)S(1)}, bf16[16,2560]{1,0:T(8,128)(2,1)S(1)}, u32[]{:S(2)}, u32[]{:S(2)}) %collective-permute-start.12) | collective-permute-done | bytes 81952 | tf_op jit(solution)/shard_map/ppermute | solution.py:513
  97.2 0.2 collective-permute-done.13
  97.4 0.7 convert_add_fusion
  98.1 0.6 convert_add_fusion.1
  98.7 1.0 %collective-permute-done.8 = bf16[128,512]{1,0:T(8,128)(2,1)S(1)} collective-permute-done((bf16[128,512]{1,0:T(8,128)(2,1)S(1)}, bf16[128,512]{1,0:T(8,128)(2,1)S(1)}, u32[]{:S(2)}, u32[]{:S(2)}) %collective-permute-start.8) | collective-permute-done | bytes 131104 | tf_op jit(solution)/shard_map/ppermute | solution.py:513
  99.8 0.0 collective-permute-done.9
  99.8 0.0 collective-permute-done.10
  99.8 0.0 copy-done.2
  99.8 1.5 %convolution_convert_fusion.1 = bf16[256,512]{1,0:T(8,128)(2,1)} fusion(bf16[512,512]{1,0:T(8,128)(2,1)S(1)} %constant_dynamic-update-slice_fusion, bf16[512,256]{1,0:T(8,128)(2,1)S(1)} %copy-done.2, s32[512]{0:T(512)S(1)} %fusion.56), kind=kOutput, calls=%fused_computation.2 | convolution fusion | flops 268959744 | bytes 1050624 | tf_op jit(solution)/shard_map/dot_general | solution.py:560
  (25 shorter events, 0.3 us)
Async XLA Ops:
  3.5 37.7 %all-to-all-start = ((bf16[32,16,1152]{2,1,0:T(8,128)(2,1)}), bf16[32,16,1152]{2,1,0:T(8,128)(2,1)S(1)}, u32[]{:S(2)}, u32[]{:S(2)}) async-start(bf16[32,16,1152]{2,1,0:T(8,128)(2,1)} %bitcast.29), calls=%async_computation | async-start | bytes 2359296 | tf_op jit(solution)/shard_map/all_to_all | solution.py:534
  41.2 1.0 %copy-start.1 = (bf16[32,16,1152]{2,1,0:T(8,128)(2,1)}, bf16[32,16,1152]{2,1,0:T(8,128)(2,1)S(1)}, u32[]{:S(2)}) copy-start(bf16[32,16,1152]{2,1,0:T(8,128)(2,1)S(1)} %all-to-all-done) | copy-start | bytes 3538948
  63.3 6.1 %copy-start = (bf16[256,2560]{1,0:T(8,128)(2,1)S(1)}, bf16[256,2560]{1,0:T(8,128)(2,1)}, u32[]{:S(2)}) copy-start(bf16[256,2560]{1,0:T(8,128)(2,1)} %get-tuple-element.52) | copy-start | bytes 3932164
  63.3 6.1 %collective-permute-start = (bf16[256,2560]{1,0:T(8,128)(2,1)}, bf16[256,2560]{1,0:T(8,128)(2,1)S(1)}, u32[]{:S(2)}, u32[]{:S(2)}) collective-permute-start(bf16[256,2560]{1,0:T(8,128)(2,1)} %get-tuple-element.53), channel_id=1, source_target_pairs={{0,8},{8,0},{1,9},{9,1},{2,10},{10,2},{3,11},{11,3},{4,12},{12,4},... | collective-permute-start | bytes 3932168 | tf_op jit(solution)/shard_map/ppermute | solution.py:513
  69.7 4.1 %collective-permute-start.1 = (bf16[256,512]{1,0:T(8,128)(2,1)S(1)}, bf16[256,512]{1,0:T(8,128)(2,1)S(1)}, u32[]{:S(2)}, u32[]{:S(2)}) collective-permute-start(bf16[256,512]{1,0:T(8,128)(2,1)S(1)} %slice.129), channel_id=1, source_target_pairs={{0,8},{8,0},{1,9},{9,1},{2,10},{10,2},{3,11},{11,3},{4,12},{12,4},... | collective-permute-start | bytes 786440 | tf_op jit(solution)/shard_map/ppermute | solution.py:513
  70.3 10.6 %collective-permute-start.5 = (bf16[64,2560]{1,0:T(8,128)(2,1)S(1)}, bf16[64,2560]{1,0:T(8,128)(2,1)S(1)}, u32[]{:S(2)}, u32[]{:S(2)}) collective-permute-start(bf16[64,2560]{1,0:T(8,128)(2,1)S(1)} %get-tuple-element.72), channel_id=1, source_target_pairs={{0,1},{1,0},{16,17},{17,16},{2,3},{3,2},{18,19},{19,18},{4,5},{5,4... | collective-permute-start | bytes 983048 | tf_op jit(solution)/shard_map/ppermute | solution.py:513
  70.4 17.2 %collective-permute-start.6 = (bf16[64,2560]{1,0:T(8,128)(2,1)S(1)}, bf16[64,2560]{1,0:T(8,128)(2,1)S(1)}, u32[]{:S(2)}, u32[]{:S(2)}) collective-permute-start(bf16[64,2560]{1,0:T(8,128)(2,1)S(1)} %get-tuple-element.71), channel_id=1, source_target_pairs={{0,16},{1,17},{16,0},{17,1},{2,18},{3,19},{18,2},{19,3},{4,20},{5,... | collective-permute-start | bytes 983048 | tf_op jit(solution)/shard_map/ppermute | solution.py:513
  70.4 17.2 %collective-permute-start.7 = (bf16[64,2560]{1,0:T(8,128)(2,1)S(1)}, bf16[64,2560]{1,0:T(8,128)(2,1)S(1)}, u32[]{:S(2)}, u32[]{:S(2)}) collective-permute-start(bf16[64,2560]{1,0:T(8,128)(2,1)S(1)} %get-tuple-element.70), channel_id=1, source_target_pairs={{0,17},{1,16},{16,1},{17,0},{2,19},{3,18},{18,3},{19,2},{4,21},{5,... | collective-permute-start | bytes 983048 | tf_op jit(solution)/shard_map/ppermute | solution.py:513
  73.9 13.7 %collective-permute-start.4 = (bf16[128,512]{1,0:T(8,128)(2,1)S(1)}, bf16[128,512]{1,0:T(8,128)(2,1)S(1)}, u32[]{:S(2)}, u32[]{:S(2)}) collective-permute-start(bf16[128,512]{1,0:T(8,128)(2,1)S(1)} %pad_maximum_fusion.3), channel_id=1, source_target_pairs={{0,6},{2,0},{4,2},{6,4},{1,7},{3,1},{5,3},{7,5},{8,14},{10,8},{12,... | collective-permute-start | bytes 393224 | tf_op jit(solution)/shard_map/ppermute | solution.py:513
  74.0 13.6 %collective-permute-start.3 = (bf16[128,512]{1,0:T(8,128)(2,1)S(1)}, bf16[128,512]{1,0:T(8,128)(2,1)S(1)}, u32[]{:S(2)}, u32[]{:S(2)}) collective-permute-start(bf16[128,512]{1,0:T(8,128)(2,1)S(1)} %pad_maximum_fusion.2), channel_id=1, source_target_pairs={{0,4},{2,6},{4,0},{6,2},{1,5},{3,7},{5,1},{7,3},{8,12},{10,14},{12... | collective-permute-start | bytes 393224 | tf_op jit(solution)/shard_map/ppermute | solution.py:513
  80.9 6.8 %collective-permute-start.2 = (bf16[128,512]{1,0:T(8,128)(2,1)S(1)}, bf16[128,512]{1,0:T(8,128)(2,1)S(1)}, u32[]{:S(2)}, u32[]{:S(2)}) collective-permute-start(bf16[128,512]{1,0:T(8,128)(2,1)S(1)} %pad_maximum_fusion.1), channel_id=1, source_target_pairs={{0,2},{2,4},{4,6},{6,0},{1,3},{3,5},{5,7},{7,1},{8,10},{10,12},{12... | collective-permute-start | bytes 393224 | tf_op jit(solution)/shard_map/ppermute | solution.py:513
  87.9 6.9 %collective-permute-start.11 = (bf16[16,2560]{1,0:T(8,128)(2,1)S(1)}, bf16[16,2560]{1,0:T(8,128)(2,1)S(1)}, u32[]{:S(2)}, u32[]{:S(2)}) collective-permute-start(bf16[16,2560]{1,0:T(8,128)(2,1)S(1)} %get-tuple-element.78), channel_id=1, source_target_pairs={{0,2},{2,4},{4,6},{6,0},{1,3},{3,5},{5,7},{7,1},{8,10},{10,12},{12... | collective-permute-start | bytes 245768 | tf_op jit(solution)/shard_map/ppermute | solution.py:513
  87.9 9.3 %collective-permute-start.12 = (bf16[16,2560]{1,0:T(8,128)(2,1)S(1)}, bf16[16,2560]{1,0:T(8,128)(2,1)S(1)}, u32[]{:S(2)}, u32[]{:S(2)}) collective-permute-start(bf16[16,2560]{1,0:T(8,128)(2,1)S(1)} %get-tuple-element.80), channel_id=1, source_target_pairs={{0,4},{2,6},{4,0},{6,2},{1,5},{3,7},{5,1},{7,3},{8,12},{10,14},{12... | collective-permute-start | bytes 245768 | tf_op jit(solution)/shard_map/ppermute | solution.py:513
  92.3 5.1 %collective-permute-start.13 = (bf16[16,2560]{1,0:T(8,128)(2,1)S(1)}, bf16[16,2560]{1,0:T(8,128)(2,1)S(1)}, u32[]{:S(2)}, u32[]{:S(2)}) collective-permute-start(bf16[16,2560]{1,0:T(8,128)(2,1)S(1)} %get-tuple-element.79), channel_id=1, source_target_pairs={{0,6},{2,0},{4,2},{6,4},{1,7},{3,1},{5,3},{7,5},{8,14},{10,8},{12,... | collective-permute-start | bytes 245768 | tf_op jit(solution)/shard_map/ppermute | solution.py:513
  92.3 7.5 %copy-start.2 = (bf16[512,256]{1,0:T(8,128)(2,1)S(1)}, bf16[512,256]{1,0:T(8,128)(2,1)}, u32[]{:S(2)}) copy-start(bf16[512,256]{1,0:T(8,128)(2,1)} %get-tuple-element.61) | copy-start | bytes 786436
  92.4 7.4 %collective-permute-start.10 = (bf16[128,512]{1,0:T(8,128)(2,1)S(1)}, bf16[128,512]{1,0:T(8,128)(2,1)S(1)}, u32[]{:S(2)}, u32[]{:S(2)}) collective-permute-start(bf16[128,512]{1,0:T(8,128)(2,1)S(1)} %pad_maximum_fusion.6), channel_id=1, source_target_pairs={{0,17},{1,16},{16,1},{17,0},{2,19},{3,18},{18,3},{19,2},{4,21},{5,... | collective-permute-start | bytes 393224 | tf_op jit(solution)/shard_map/ppermute | solution.py:513
  93.1 6.7 %collective-permute-start.9 = (bf16[128,512]{1,0:T(8,128)(2,1)S(1)}, bf16[128,512]{1,0:T(8,128)(2,1)S(1)}, u32[]{:S(2)}, u32[]{:S(2)}) collective-permute-start(bf16[128,512]{1,0:T(8,128)(2,1)S(1)} %pad_maximum_fusion.5), channel_id=1, source_target_pairs={{0,16},{1,17},{16,0},{17,1},{2,18},{3,19},{18,2},{19,3},{4,20},{5,... | collective-permute-start | bytes 393224 | tf_op jit(solution)/shard_map/ppermute | solution.py:513
  94.8 5.0 %collective-permute-start.8 = (bf16[128,512]{1,0:T(8,128)(2,1)S(1)}, bf16[128,512]{1,0:T(8,128)(2,1)S(1)}, u32[]{:S(2)}, u32[]{:S(2)}) collective-permute-start(bf16[128,512]{1,0:T(8,128)(2,1)S(1)} %pad_maximum_fusion.4), channel_id=1, source_target_pairs={{0,1},{1,0},{16,17},{17,16},{2,3},{3,2},{18,19},{19,18},{4,5},{5,4... | collective-permute-start | bytes 393224 | tf_op jit(solution)/shard_map/ppermute | solution.py:513

commit v7 on v6

--- a/solution.py
+++ b/solution.py
@@ -424,31 +424,37 @@
     )(*operands)
 
 
-def input_kernel(denc_ref, win_ref, dpre_ref, dk_ref, out_ref):
+def input_kernel(denc_ref, win_ref, dpre_ref, dk_ref, *refs):
+    out_ref = refs[-1]
     width = denc_ref.shape[2]
     total = denc_ref[0].astype(f32) + dot_nt(dpre_ref[...], win_ref[:, : 3 * width])
     total = total + dot_nt(jnp.transpose(dk_ref[...]), win_ref[:, 3 * width :])
     out_ref[0] = total.astype(bf16)
 
 
-def input_backward(denc, w_in, dpre, dk):
+def input_backward(denc, w_in, dpre, dk, part, parts, earlier=None):
     hist, seq, width = denc.shape
-    block = lambda a: pl.BlockSpec((1,) + a.shape[1:], lambda i: (i, 0, 0))
+    count = hist // parts
+    begin = part * count
+    block = pl.BlockSpec((1, seq, width), lambda i: (i + begin, 0, 0))
+    held = [] if earlier is None else [earlier]
     return pl.pallas_call(
         input_kernel,
-        grid=(hist,),
+        grid=(count,),
         in_specs=[
-            block(denc),
+            block,
             whole(w_in.shape),
-            pl.BlockSpec((seq, 3 * width), lambda i: (i, 0)),
-            pl.BlockSpec((width, seq), lambda i: (0, i)),
-        ],
-        out_specs=block(denc),
+            pl.BlockSpec((seq, 3 * width), lambda i: (i + begin, 0)),
+            pl.BlockSpec((width, seq), lambda i: (0, i + begin)),
+        ]
+        + [pl.BlockSpec(memory_space=pl.ANY)] * len(held),
+        out_specs=block,
         out_shape=jax.ShapeDtypeStruct(denc.shape, bf16),
+        input_output_aliases={4: 0} if held else {},
         compiler_params=params(60),
-        cost_estimate=cost(6e9, 8e6),
+        cost_estimate=cost(6e9 / parts, 8e6 / parts),
         name="input_backward",
-    )(denc, w_in, dpre, dk)
+    )(denc, w_in, dpre, dk, *held)
 
 
 def owner_order(width):
@@ -546,11 +552,13 @@
     d_enc, rows, d_query = after((d_enc, rows, d_query))
     back = [cut_rows(b, n_z) for b in send_blocks(cut_rows(d_query, n_core), core)]
     back = [jnp.concatenate([b[d] for b in back], axis=0) for d in range(n_z)]
-    d_inputs = input_backward(d_enc, weight_in, dpre, dk)
+    d_inputs = input_backward(d_enc, weight_in, dpre, dk, 0, 2)
     back = send_blocks(back, line)
     parts = send_blocks(cut_rows(rows, n_y * n_x), plane)
     back, parts, d_inputs = after((back, parts, d_inputs))
     parts = send_blocks(cut_rows(add_up(parts).astype(bf16), n_z), line)
+    parts, d_inputs = after((parts, d_inputs))
+    d_inputs = input_backward(d_enc, weight_in, dpre, dk, 1, 2, d_inputs)
     back = [b.reshape(n_core, n_y * n_x, capacity, width) for b in back]
     back = [
         jnp.concatenate([b[:, i].reshape(n_core * capacity, width) for b in back], axis=0)

time: 102 us -> 105 us (1.029); the launches traced: 101 us -> 103 us
  Pallas kernels: 44.8 us -> 47.1 us
  starting transfers between devices: 23.2 us -> 21.1 us
  waiting for transfers between devices: 25.2 us -> 26.8 us
    pallas_call x1 -> x2, Pallas kernels: 6.69 us -> 8.98 us  [input_backward(): pl.pallas_call(input_kernel, grid=(count,), in_specs=[block, whole(w_in.s...]
    ppermute x14, starting transfers between devices: 15.9 us -> 13.8 us  [send_blocks(): parts.append(lax.ppermute(blocks[d], axes, pairs))]
    ppermute x14, waiting for transfers between devices: 10 us -> 11.6 us  [send_blocks(): parts.append(lax.ppermute(blocks[d], axes, pairs))]
  transfers between devices with their start and end apart: 15 -> 15, of which waited for: 7 -> 8; matrix products, arithmetic and copies ran while one was open for 4% -> 4% of each run, Pallas kernels for 21% -> 22%
where the time goes in v7:
time: 105 us; the launch traced here: 103 us
  Pallas kernels  47.1 us (45%)
  waiting for transfers between devices  26.8 us (26%)
  starting transfers between devices  21.1 us (20%)
  matrix products  3.04 us (3%)
  other arithmetic  2.92 us (3%)
  local copies, waits for them, and re-layouts  1.29 us (1%)
    pallas_call x1, Pallas kernels, owner_backward(): pl.pallas_call(owner_kernel, grid=(1,), in_specs=[raw] * len(operands), o...  21.1 us
    all_to_all x1, waiting for transfers between devices, local(): recv = lax.all_to_all(shaped, AXES, split_axis=0, concat_axis=0, tiled=True)  15.2 us
    pallas_call x1, Pallas kernels, layer_forward(): pl.pallas_call(forward_kernel, grid=(hist,), in_specs=[row, whole(w_in.sh...  14.2 us
    ppermute x14, starting transfers between devices, send_blocks(): parts.append(lax.ppermute(blocks[d], axes, pairs))  13.8 us
    ppermute x14, waiting for transfers between devices, send_blocks(): parts.append(lax.ppermute(blocks[d], axes, pairs))  11.6 us
    pallas_call x2, Pallas kernels, input_backward(): pl.pallas_call(input_kernel, grid=(count,), in_specs=[block, whole(w_in.s...  8.98 us
    all_to_all x1, starting transfers between devices, local(): recv = lax.all_to_all(shaped, AXES, split_axis=0, concat_axis=0, tiled=True)  7.3 us
    pallas_call x1, Pallas kernels, route(): pl.pallas_call(functools.partial(route_kernel, devices, capacity), grid=(...  2.86 us
  transfers between devices with their start and end apart: 15, of which 8 were waited for; matrix products, arithmetic and copies ran while one was open for 4% of the time, Pallas kernels for 22%

profile of v7, /device:TPU:0, one launch (start us, length us, event | category | flops | bytes accessed | tf_op | source)
XLA Modules:
  0.0 103.2 jit_solution(4896856641404088175)
XLA Ops:
  0.6 2.9 %route.1 = (bf16[512,1152]{1,0:T(8,128)(2,1)}, bf16[512,256]{1,0:T(8,128)(2,1)}) custom-call(s32[1,256]{1,0:T(1,128)} %bitcast.50, s32[1,256]{1,0:T(1,128)} %bitcast.51, s32[1,256]{1,0:T(1,128)} %bitcast.52, bf16[256,512]{1,0:T(8,128)(2,1)} %cand_ref.1, bf16[256,512]{1,0:T(8,128)(2,1)} %cot_ref.1), custom_call_target="tpu_custom_call" | custom-call | flops 2000000000 | bytes 2097152 | tf_op jit(solution)/shard_map/route/pallas_call | solution.py:92
  3.5 7.3 %all-to-all-start = ((bf16[32,16,1152]{2,1,0:T(8,128)(2,1)}), bf16[32,16,1152]{2,1,0:T(8,128)(2,1)S(1)}, u32[]{:S(2)}, u32[]{:S(2)}) async-start(bf16[32,16,1152]{2,1,0:T(8,128)(2,1)} %bitcast.29), calls=%async_computation | async-start | bytes 2359296 | tf_op jit(solution)/shard_map/all_to_all | solution.py:540
  10.8 1.0 fusion.perm_ref
  11.8 14.2 %forward.1 = (bf16[4,256,512]{2,1,0:T(8,128)(2,1)}, bf16[4,256,1024]{2,1,0:T(8,128)(2,1)}, bf16[4,512,256]{2,1,0:T(8,128)(2,1)}, bf16[4,256,512]{2,1,0:T(8,128)(...) custom-call(bf16[4,256,512]{2,1,0:T(8,128)(2,1)} %x_ref.1, ...), custom_call_target="tpu_custom_call" | custom-call | flops 17999998976 | bytes 24000000 | tf_op jit(solution)/shard_map/forward/pallas_call | solution.py:180
  26.0 15.2 %all-to-all-done = bf16[32,16,1152]{2,1,0:T(8,128)(2,1)S(1)} async-done(((bf16[32,16,1152]{2,1,0:T(8,128)(2,1)}), bf16[32,16,1152]{2,1,0:T(8,128)(2,1)S(1)}, u32[]{:S(2)}, u32[]{:S(2)}) %all-to-all-start) | async-done | bytes 1179680 | tf_op jit(solution)/shard_map/all_to_all | solution.py:540
  41.2 0.0 copy-start.1
  41.2 1.0 copy-done.1
  42.2 21.1 %owner_backward.1 = (bf16[512,512]{1,0:T(8,128)(2,1)}, bf16[4,256,512]{2,1,0:T(8,128)(2,1)}, bf16[1024,1536]{1,0:T(8,128)(2,1)}, bf16[512,1024]{1,0:T(8,128)(2,1...) custom-call(bf16[512,1152]{1,0:T(8,128)(2,1)} %bitcast.28, bf16[4,256,512]{2,1,0:T(8,128)(2,1)} %get-tuple-element.43.refs_1_, ...), custom_call_target="tpu_custom_call" | custom-call | flops 30000001024 | bytes 30000000 | tf_op jit(solution)/shard_map/owner_backward/pallas_call | solution.py:404
  63.3 0.0 copy-start
  63.3 1.5 %collective-permute-start = (bf16[256,2560]{1,0:T(8,128)(2,1)}, bf16[256,2560]{1,0:T(8,128)(2,1)S(1)}, u32[]{:S(2)}, u32[]{:S(2)}) collective-permute-start(bf16[256,2560]{1,0:T(8,128)(2,1)} %get-tuple-element.58), channel_id=1, source_target_pairs={{0,8},{8,0},{1,9},{9,1},{2,10},{10,2},{3,11},{11,3},{4,12},{12,4},... | collective-permute-start | bytes 3932168 | tf_op jit(solution)/shard_map/ppermute | solution.py:519
  64.8 1.5 %convolution_convert_fusion = bf16[512,512]{1,0:T(8,128)(2,1)S(1)} fusion(bf16[512,512]{1,0:T(8,128)(2,1)} %get-tuple-element.59, s32[512]{0:T(512)S(1)} %fusion.33), kind=kOutput, calls=%fused_computation.1 | convolution fusion | flops 268959744 | bytes 1050624 | tf_op jit(solution)/shard_map/dot_general | solution.py:21
  66.4 1.3 %collective-permute-done = bf16[256,2560]{1,0:T(8,128)(2,1)S(1)} collective-permute-done((bf16[256,2560]{1,0:T(8,128)(2,1)}, bf16[256,2560]{1,0:T(8,128)(2,1)S(1)}, u32[]{:S(2)}, u32[]{:S(2)}) %collective-permute-start) | collective-permute-done | bytes 1310752 | tf_op jit(solution)/shard_map/ppermute | solution.py:519
  67.6 0.0 copy-done
  67.6 0.3 add_convert_fusion
  68.0 0.4 collective-permute-start.1
  68.4 0.1 fusion.83
  68.5 0.1 collective-permute-start.5
  68.6 0.1 collective-permute-start.6
  68.7 3.4 %collective-permute-start.7 = (bf16[64,2560]{1,0:T(8,128)(2,1)S(1)}, bf16[64,2560]{1,0:T(8,128)(2,1)S(1)}, u32[]{:S(2)}, u32[]{:S(2)}) collective-permute-start(bf16[64,2560]{1,0:T(8,128)(2,1)S(1)} %get-tuple-element.80), channel_id=1, source_target_pairs={{0,17},{1,16},{16,1},{17,0},{2,19},{3,18},{18,3},{19,2},{4,21},{5,... | collective-permute-start | bytes 983048 | tf_op jit(solution)/shard_map/ppermute | solution.py:519
  72.1 0.0 collective-permute-done.1
  72.2 1.6 %collective-permute-start.4 = (bf16[128,512]{1,0:T(8,128)(2,1)S(1)}, bf16[128,512]{1,0:T(8,128)(2,1)S(1)}, u32[]{:S(2)}, u32[]{:S(2)}) collective-permute-start(bf16[128,512]{1,0:T(8,128)(2,1)S(1)} %pad_maximum_fusion.3), channel_id=1, source_target_pairs={{0,6},{2,0},{4,2},{6,4},{1,7},{3,1},{5,3},{7,5},{8,14},{10,8},{12,... | collective-permute-start | bytes 393224 | tf_op jit(solution)/shard_map/ppermute | solution.py:519
  73.8 0.1 collective-permute-start.3
  73.9 5.3 %collective-permute-done.5 = bf16[64,2560]{1,0:T(8,128)(2,1)S(1)} collective-permute-done((bf16[64,2560]{1,0:T(8,128)(2,1)S(1)}, bf16[64,2560]{1,0:T(8,128)(2,1)S(1)}, u32[]{:S(2)}, u32[]{:S(2)}) %collective-permute-start.5) | collective-permute-done | bytes 327712 | tf_op jit(solution)/shard_map/ppermute | solution.py:519
  79.1 0.0 collective-permute-start.2
  79.1 4.5 %input_backward.2.refs_0_ = bf16[4,256,512]{2,1,0:T(8,128)(2,1)} custom-call(bf16[4,256,512]{2,1,0:T(8,128)(2,1)} %get-tuple-element.60.denc_ref, bf16[512,2048]{1,0:T(8,128)(2,1)} %win_ref.5, bf16[1024,1536]{1,0:T(8,128)(2,1)} %get-tuple-element.61.dpre_ref, bf16[512,1024]{1,0:T(8,128)(2,1)} %get-tuple-element.62.dk_ref), custom_call_target="tpu_custom_call" | custom-call | flops 3000000000 | bytes 4000000 | tf_op jit(solution)/shard_map/input_backward/pallas_call | solution.py:441
  83.6 1.8 %collective-permute-done.6 = bf16[64,2560]{1,0:T(8,128)(2,1)S(1)} collective-permute-done((bf16[64,2560]{1,0:T(8,128)(2,1)S(1)}, bf16[64,2560]{1,0:T(8,128)(2,1)S(1)}, u32[]{:S(2)}, u32[]{:S(2)}) %collective-permute-start.6) | collective-permute-done | bytes 327712 | tf_op jit(solution)/shard_map/ppermute | solution.py:519
  85.4 0.0 collective-permute-done.7
  85.4 0.0 collective-permute-done.4
  85.5 0.0 collective-permute-done.3
  85.5 0.5 collective-permute-done.2
  85.9 0.2 add_convert_fusion.1
  86.1 1.7 %collective-permute-start.10 = (bf16[16,2560]{1,0:T(8,128)(2,1)S(1)}, bf16[16,2560]{1,0:T(8,128)(2,1)S(1)}, u32[]{:S(2)}, u32[]{:S(2)}) collective-permute-start(bf16[16,2560]{1,0:T(8,128)(2,1)S(1)} %get-tuple-element.88), channel_id=1, source_target_pairs={{0,6},{2,0},{4,2},{6,4},{1,7},{3,1},{5,3},{7,5},{8,14},{10,8},{12,... | collective-permute-start | bytes 245768 | tf_op jit(solution)/shard_map/ppermute | solution.py:519
  87.8 0.4 collective-permute-start.8
  88.2 1.3 %collective-permute-start.9 = (bf16[16,2560]{1,0:T(8,128)(2,1)S(1)}, bf16[16,2560]{1,0:T(8,128)(2,1)S(1)}, u32[]{:S(2)}, u32[]{:S(2)}) collective-permute-start(bf16[16,2560]{1,0:T(8,128)(2,1)S(1)} %get-tuple-element.89), channel_id=1, source_target_pairs={{0,4},{2,6},{4,0},{6,2},{1,5},{3,7},{5,1},{7,3},{8,12},{10,14},{12... | collective-permute-start | bytes 245768 | tf_op jit(solution)/shard_map/ppermute | solution.py:519
  89.6 0.3 collective-permute-start.13
  89.9 1.7 %collective-permute-start.12 = (bf16[128,512]{1,0:T(8,128)(2,1)S(1)}, bf16[128,512]{1,0:T(8,128)(2,1)S(1)}, u32[]{:S(2)}, u32[]{:S(2)}) collective-permute-start(bf16[128,512]{1,0:T(8,128)(2,1)S(1)} %pad_maximum_fusion.5), channel_id=1, source_target_pairs={{0,16},{1,17},{16,0},{17,1},{2,18},{3,19},{18,2},{19,3},{4,20},{5,... | collective-permute-start | bytes 393224 | tf_op jit(solution)/shard_map/ppermute | solution.py:519
  91.7 0.7 collective-permute-done.10
  92.4 1.2 %collective-permute-start.11 = (bf16[128,512]{1,0:T(8,128)(2,1)S(1)}, bf16[128,512]{1,0:T(8,128)(2,1)S(1)}, u32[]{:S(2)}, u32[]{:S(2)}) collective-permute-start(bf16[128,512]{1,0:T(8,128)(2,1)S(1)} %pad_maximum_fusion.4), channel_id=1, source_target_pairs={{0,1},{1,0},{16,17},{17,16},{2,3},{3,2},{18,19},{19,18},{4,5},{5,4... | collective-permute-start | bytes 393224 | tf_op jit(solution)/shard_map/ppermute | solution.py:519
  93.6 0.5 collective-permute-done.8
  94.1 1.7 %collective-permute-done.9 = bf16[16,2560]{1,0:T(8,128)(2,1)S(1)} collective-permute-done((bf16[16,2560]{1,0:T(8,128)(2,1)S(1)}, bf16[16,2560]{1,0:T(8,128)(2,1)S(1)}, u32[]{:S(2)}, u32[]{:S(2)}) %collective-permute-start.9) | collective-permute-done | bytes 81952 | tf_op jit(solution)/shard_map/ppermute | solution.py:519
  95.7 0.0 copy-start.2
  95.7 4.5 %input_backward.3 = bf16[4,256,512]{2,1,0:T(8,128)(2,1)} custom-call(bf16[4,256,512]{2,1,0:T(8,128)(2,1)} %get-tuple-element.60.denc_ref, bf16[512,2048]{1,0:T(8,128)(2,1)} %win_ref.5, bf16[1024,1536]{1,0:T(8,128)(2,1)} %get-tuple-element.61.dpre_ref, bf16[512,1024]{1,0:T(8,128)(2,1)} %get-tuple-element.62.dk_ref, ...), custom_call_target="tpu_custom_call", output_to_operand_aliasing={{}: (4, {})} | custom-call | flops 3000000000 | bytes 4000000 | tf_op jit(solution)/shard_map/input_backward/pallas_call | solution.py:441
  100.2 0.7 convert_add_fusion
  100.9 0.6 convert_add_fusion.1
  101.5 0.0 collective-permute-done.11
  101.6 0.0 collective-permute-done.12
  101.6 0.0 collective-permute-done.13
  101.6 0.0 copy-done.2
  101.6 1.5 %convolution_convert_fusion.1 = bf16[256,512]{1,0:T(8,128)(2,1)} fusion(bf16[512,512]{1,0:T(8,128)(2,1)S(1)} %constant_dynamic-update-slice_fusion, bf16[512,256]{1,0:T(8,128)(2,1)S(1)} %copy-done.2, s32[512]{0:T(512)S(1)} %fusion.56), kind=kOutput, calls=%fused_computation.2 | convolution fusion | flops 268959744 | bytes 1050624 | tf_op jit(solution)/shard_map/dot_general | solution.py:568
  (25 shorter events, 0.3 us)
Async XLA Ops:
  3.5 37.7 %all-to-all-start = ((bf16[32,16,1152]{2,1,0:T(8,128)(2,1)}), bf16[32,16,1152]{2,1,0:T(8,128)(2,1)S(1)}, u32[]{:S(2)}, u32[]{:S(2)}) async-start(bf16[32,16,1152]{2,1,0:T(8,128)(2,1)} %bitcast.29), calls=%async_computation | async-start | bytes 2359296 | tf_op jit(solution)/shard_map/all_to_all | solution.py:540
  41.2 1.0 copy-start.1
  63.3 4.3 %copy-start = (bf16[256,2560]{1,0:T(8,128)(2,1)S(1)}, bf16[256,2560]{1,0:T(8,128)(2,1)}, u32[]{:S(2)}) copy-start(bf16[256,2560]{1,0:T(8,128)(2,1)} %get-tuple-element.57) | copy-start | bytes 3932164
  63.3 4.3 %collective-permute-start = (bf16[256,2560]{1,0:T(8,128)(2,1)}, bf16[256,2560]{1,0:T(8,128)(2,1)S(1)}, u32[]{:S(2)}, u32[]{:S(2)}) collective-permute-start(bf16[256,2560]{1,0:T(8,128)(2,1)} %get-tuple-element.58), channel_id=1, source_target_pairs={{0,8},{8,0},{1,9},{9,1},{2,10},{10,2},{3,11},{11,3},{4,12},{12,4},... | collective-permute-start | bytes 3932168 | tf_op jit(solution)/shard_map/ppermute | solution.py:519
  68.0 4.1 %collective-permute-start.1 = (bf16[256,512]{1,0:T(8,128)(2,1)S(1)}, bf16[256,512]{1,0:T(8,128)(2,1)S(1)}, u32[]{:S(2)}, u32[]{:S(2)}) collective-permute-start(bf16[256,512]{1,0:T(8,128)(2,1)S(1)} %slice.129), channel_id=1, source_target_pairs={{0,8},{8,0},{1,9},{9,1},{2,10},{10,2},{3,11},{11,3},{4,12},{12,4},... | collective-permute-start | bytes 786440 | tf_op jit(solution)/shard_map/ppermute | solution.py:519
  68.5 10.6 %collective-permute-start.5 = (bf16[64,2560]{1,0:T(8,128)(2,1)S(1)}, bf16[64,2560]{1,0:T(8,128)(2,1)S(1)}, u32[]{:S(2)}, u32[]{:S(2)}) collective-permute-start(bf16[64,2560]{1,0:T(8,128)(2,1)S(1)} %get-tuple-element.82), channel_id=1, source_target_pairs={{0,1},{1,0},{16,17},{17,16},{2,3},{3,2},{18,19},{19,18},{4,5},{5,4... | collective-permute-start | bytes 983048 | tf_op jit(solution)/shard_map/ppermute | solution.py:519
  68.6 16.8 %collective-permute-start.6 = (bf16[64,2560]{1,0:T(8,128)(2,1)S(1)}, bf16[64,2560]{1,0:T(8,128)(2,1)S(1)}, u32[]{:S(2)}, u32[]{:S(2)}) collective-permute-start(bf16[64,2560]{1,0:T(8,128)(2,1)S(1)} %get-tuple-element.81), channel_id=1, source_target_pairs={{0,16},{1,17},{16,0},{17,1},{2,18},{3,19},{18,2},{19,3},{4,20},{5,... | collective-permute-start | bytes 983048 | tf_op jit(solution)/shard_map/ppermute | solution.py:519
  68.7 16.8 %collective-permute-start.7 = (bf16[64,2560]{1,0:T(8,128)(2,1)S(1)}, bf16[64,2560]{1,0:T(8,128)(2,1)S(1)}, u32[]{:S(2)}, u32[]{:S(2)}) collective-permute-start(bf16[64,2560]{1,0:T(8,128)(2,1)S(1)} %get-tuple-element.80), channel_id=1, source_target_pairs={{0,17},{1,16},{16,1},{17,0},{2,19},{3,18},{18,3},{19,2},{4,21},{5,... | collective-permute-start | bytes 983048 | tf_op jit(solution)/shard_map/ppermute | solution.py:519
  72.2 13.3 %collective-permute-start.4 = (bf16[128,512]{1,0:T(8,128)(2,1)S(1)}, bf16[128,512]{1,0:T(8,128)(2,1)S(1)}, u32[]{:S(2)}, u32[]{:S(2)}) collective-permute-start(bf16[128,512]{1,0:T(8,128)(2,1)S(1)} %pad_maximum_fusion.3), channel_id=1, source_target_pairs={{0,6},{2,0},{4,2},{6,4},{1,7},{3,1},{5,3},{7,5},{8,14},{10,8},{12,... | collective-permute-start | bytes 393224 | tf_op jit(solution)/shard_map/ppermute | solution.py:519
  73.8 11.7 %collective-permute-start.3 = (bf16[128,512]{1,0:T(8,128)(2,1)S(1)}, bf16[128,512]{1,0:T(8,128)(2,1)S(1)}, u32[]{:S(2)}, u32[]{:S(2)}) collective-permute-start(bf16[128,512]{1,0:T(8,128)(2,1)S(1)} %pad_maximum_fusion.2), channel_id=1, source_target_pairs={{0,4},{2,6},{4,0},{6,2},{1,5},{3,7},{5,1},{7,3},{8,12},{10,14},{12... | collective-permute-start | bytes 393224 | tf_op jit(solution)/shard_map/ppermute | solution.py:519
  79.1 6.8 %collective-permute-start.2 = (bf16[128,512]{1,0:T(8,128)(2,1)S(1)}, bf16[128,512]{1,0:T(8,128)(2,1)S(1)}, u32[]{:S(2)}, u32[]{:S(2)}) collective-permute-start(bf16[128,512]{1,0:T(8,128)(2,1)S(1)} %pad_maximum_fusion.1), channel_id=1, source_target_pairs={{0,2},{2,4},{4,6},{6,0},{1,3},{3,5},{5,7},{7,1},{8,10},{10,12},{12... | collective-permute-start | bytes 393224 | tf_op jit(solution)/shard_map/ppermute | solution.py:519
  86.1 6.2 %collective-permute-start.10 = (bf16[16,2560]{1,0:T(8,128)(2,1)S(1)}, bf16[16,2560]{1,0:T(8,128)(2,1)S(1)}, u32[]{:S(2)}, u32[]{:S(2)}) collective-permute-start(bf16[16,2560]{1,0:T(8,128)(2,1)S(1)} %get-tuple-element.88), channel_id=1, source_target_pairs={{0,6},{2,0},{4,2},{6,4},{1,7},{3,1},{5,3},{7,5},{8,14},{10,8},{12,... | collective-permute-start | bytes 245768 | tf_op jit(solution)/shard_map/ppermute | solution.py:519
  87.8 6.3 %collective-permute-start.8 = (bf16[16,2560]{1,0:T(8,128)(2,1)S(1)}, bf16[16,2560]{1,0:T(8,128)(2,1)S(1)}, u32[]{:S(2)}, u32[]{:S(2)}) collective-permute-start(bf16[16,2560]{1,0:T(8,128)(2,1)S(1)} %get-tuple-element.90), channel_id=1, source_target_pairs={{0,2},{2,4},{4,6},{6,0},{1,3},{3,5},{5,7},{7,1},{8,10},{10,12},{12... | collective-permute-start | bytes 245768 | tf_op jit(solution)/shard_map/ppermute | solution.py:519
  88.2 7.5 %collective-permute-start.9 = (bf16[16,2560]{1,0:T(8,128)(2,1)S(1)}, bf16[16,2560]{1,0:T(8,128)(2,1)S(1)}, u32[]{:S(2)}, u32[]{:S(2)}) collective-permute-start(bf16[16,2560]{1,0:T(8,128)(2,1)S(1)} %get-tuple-element.89), channel_id=1, source_target_pairs={{0,4},{2,6},{4,0},{6,2},{1,5},{3,7},{5,1},{7,3},{8,12},{10,14},{12... | collective-permute-start | bytes 245768 | tf_op jit(solution)/shard_map/ppermute | solution.py:519
  89.6 12.0 %collective-permute-start.13 = (bf16[128,512]{1,0:T(8,128)(2,1)S(1)}, bf16[128,512]{1,0:T(8,128)(2,1)S(1)}, u32[]{:S(2)}, u32[]{:S(2)}) collective-permute-start(bf16[128,512]{1,0:T(8,128)(2,1)S(1)} %pad_maximum_fusion.6), channel_id=1, source_target_pairs={{0,17},{1,16},{16,1},{17,0},{2,19},{3,18},{18,3},{19,2},{4,21},{5,... | collective-permute-start | bytes 393224 | tf_op jit(solution)/shard_map/ppermute | solution.py:519
  89.9 11.6 %collective-permute-start.12 = (bf16[128,512]{1,0:T(8,128)(2,1)S(1)}, bf16[128,512]{1,0:T(8,128)(2,1)S(1)}, u32[]{:S(2)}, u32[]{:S(2)}) collective-permute-start(bf16[128,512]{1,0:T(8,128)(2,1)S(1)} %pad_maximum_fusion.5), channel_id=1, source_target_pairs={{0,16},{1,17},{16,0},{17,1},{2,18},{3,19},{18,2},{19,3},{4,20},{5,... | collective-permute-start | bytes 393224 | tf_op jit(solution)/shard_map/ppermute | solution.py:519
  92.4 9.2 %collective-permute-start.11 = (bf16[128,512]{1,0:T(8,128)(2,1)S(1)}, bf16[128,512]{1,0:T(8,128)(2,1)S(1)}, u32[]{:S(2)}, u32[]{:S(2)}) collective-permute-start(bf16[128,512]{1,0:T(8,128)(2,1)S(1)} %pad_maximum_fusion.4), channel_id=1, source_target_pairs={{0,1},{1,0},{16,17},{17,16},{2,3},{3,2},{18,19},{19,18},{4,5},{5,4... | collective-permute-start | bytes 393224 | tf_op jit(solution)/shard_map/ppermute | solution.py:519
  95.7 5.9 %copy-start.2 = (bf16[512,256]{1,0:T(8,128)(2,1)S(1)}, bf16[512,256]{1,0:T(8,128)(2,1)}, u32[]{:S(2)}) copy-start(bf16[512,256]{1,0:T(8,128)(2,1)} %get-tuple-element.71) | copy-start | bytes 786436

commit v8 on v6

--- a/solution.py
+++ b/solution.py
@@ -265,9 +265,10 @@
 
 def norm_backward(denc_ref, wout_ref, normed_ref, nu_ref, gi_ref, dmix_ref, dpre_ref):
     hist, seq, width = denc_ref.shape
+    d_merged_all = dot_nt(denc_ref[...].reshape(hist * seq, width), wout_ref[...])
     for at in range(hist):
         here = slice(at * seq, (at + 1) * seq)
-        d_merged = dot_nt(denc_ref[at], wout_ref[...])
+        d_merged = d_merged_all[here]
         dpre_ref[here, :width] = (d_merged * nu_ref[at].astype(f32)).astype(bf16)
         normed = normed_ref[at].astype(f32)
         d_norm = d_merged * gi_ref[at].astype(f32)
@@ -284,17 +285,24 @@
 ):
     seq, width = dmix_ref.shape[1:]
     head = width // HEADS
+    half_seq = seq // 2
+    zero = jnp.zeros((half_seq, half_seq), bf16)
     here = slice(at * seq, (at + 1) * seq)
     masks = lane_masks(2 * head, head)
     scale = 0.5 * head**-0.5 / seq
     for pair in range(HEADS // 2):
         cols = slice(pair * 2 * head, (pair + 1) * 2 * head)
         d_p = dmix_ref[at, :, cols]
-        d_attn = dot_nt(both_heads(d_p, masks), v_ref[at, :, cols])
-        d_s = [
-            (d_attn[j * seq : (j + 1) * seq] * grad_ref[at, 2 * pair + j].astype(f32)).astype(bf16)
-            for j in range(2)
-        ]
+        v_p = v_ref[at, :, cols]
+        top = dot_nt(both_heads(d_p[:half_seq], masks), v_p[:half_seq])
+        bot = dot_nt(both_heads(d_p[half_seq:], masks), v_p)
+        d_s = []
+        for j in range(2):
+            part = slice(j * half_seq, (j + 1) * half_seq)
+            grad = grad_ref[at, 2 * pair + j]
+            d_top = (top[part] * grad[:half_seq, :half_seq].astype(f32)).astype(bf16)
+            d_bot = (bot[part] * grad[half_seq:].astype(f32)).astype(bf16)
+            d_s.append(jnp.concatenate([jnp.concatenate([d_top, zero], axis=1), d_bot], axis=0))
         attn_t = jnp.concatenate([attn_t_ref[at, 2 * pair], attn_t_ref[at, 2 * pair + 1]], axis=0)
         d_v = pick_lanes(dot_nn(attn_t, d_p), head) * (1.0 / seq)
         d_q = pick_lanes(dot_nn(jnp.concatenate(d_s, axis=0), k_ref[at, :, cols]), head) * scale

time: 102 us -> 102 us (level)
  transfers between devices with their start and end apart: 15 -> 15, of which waited for: 7 -> 6; matrix products, arithmetic and copies ran while one was open for 4% -> 4% of each run, Pallas kernels for 21% -> 21%
where the time goes in v8:
time: 102 us; the launch traced here: 101 us
  Pallas kernels  44.5 us (44%)
  waiting for transfers between devices  26 us (25%)
  starting transfers between devices  22.7 us (22%)
  matrix products  3.13 us (3%)
  other arithmetic  2.93 us (3%)
  local copies, waits for them, and re-layouts  1.29 us (1%)
    pallas_call x1, Pallas kernels, owner_backward(): pl.pallas_call(owner_kernel, grid=(1,), in_specs=[raw] * len(operands), o...  20.7 us
    ppermute x14, starting transfers between devices, send_blocks(): parts.append(lax.ppermute(blocks[d], axes, pairs))  15.4 us
    all_to_all x1, waiting for transfers between devices, local(): recv = lax.all_to_all(shaped, AXES, split_axis=0, concat_axis=0, tiled=True)  15.2 us
    pallas_call x1, Pallas kernels, layer_forward(): pl.pallas_call(forward_kernel, grid=(hist,), in_specs=[row, whole(w_in.sh...  14.2 us
    ppermute x14, waiting for transfers between devices, send_blocks(): parts.append(lax.ppermute(blocks[d], axes, pairs))  10.8 us
    all_to_all x1, starting transfers between devices, local(): recv = lax.all_to_all(shaped, AXES, split_axis=0, concat_axis=0, tiled=True)  7.3 us
    pallas_call x1, Pallas kernels, input_backward(): pl.pallas_call(input_kernel, grid=(hist,), in_specs=[block(denc), whole(w...  6.69 us
    pallas_call x1, Pallas kernels, route(): pl.pallas_call(functools.partial(route_kernel, devices, capacity), grid=(...  2.86 us
  transfers between devices with their start and end apart: 15, of which 6 were waited for; matrix products, arithmetic and copies ran while one was open for 4% of the time, Pallas kernels for 21%

profile of v8, /device:TPU:0, one launch (start us, length us, event | category | flops | bytes accessed | tf_op | source)
XLA Modules:
  0.0 101.4 jit_solution(17733991315216430189)
XLA Ops:
  0.6 2.9 %route.1 = (bf16[512,1152]{1,0:T(8,128)(2,1)}, bf16[512,256]{1,0:T(8,128)(2,1)}) custom-call(s32[1,256]{1,0:T(1,128)} %bitcast.50, s32[1,256]{1,0:T(1,128)} %bitcast.51, s32[1,256]{1,0:T(1,128)} %bitcast.52, bf16[256,512]{1,0:T(8,128)(2,1)} %cand_ref.1, bf16[256,512]{1,0:T(8,128)(2,1)} %cot_ref.1), custom_call_target="tpu_custom_call" | custom-call | flops 2000000000 | bytes 2097152 | tf_op jit(solution)/shard_map/route/pallas_call | solution.py:92
  3.5 7.3 %all-to-all-start = ((bf16[32,16,1152]{2,1,0:T(8,128)(2,1)}), bf16[32,16,1152]{2,1,0:T(8,128)(2,1)S(1)}, u32[]{:S(2)}, u32[]{:S(2)}) async-start(bf16[32,16,1152]{2,1,0:T(8,128)(2,1)} %bitcast.29), calls=%async_computation | async-start | bytes 2359296 | tf_op jit(solution)/shard_map/all_to_all | solution.py:542
  10.8 1.0 fusion.perm_ref
  11.8 14.2 %forward.1 = (bf16[4,256,512]{2,1,0:T(8,128)(2,1)}, bf16[4,256,1024]{2,1,0:T(8,128)(2,1)}, bf16[4,512,256]{2,1,0:T(8,128)(2,1)}, bf16[4,256,512]{2,1,0:T(8,128)(...) custom-call(bf16[4,256,512]{2,1,0:T(8,128)(2,1)} %x_ref.1, ...), custom_call_target="tpu_custom_call" | custom-call | flops 17999998976 | bytes 24000000 | tf_op jit(solution)/shard_map/forward/pallas_call | solution.py:180
  26.0 15.2 %all-to-all-done = bf16[32,16,1152]{2,1,0:T(8,128)(2,1)S(1)} async-done(((bf16[32,16,1152]{2,1,0:T(8,128)(2,1)}), bf16[32,16,1152]{2,1,0:T(8,128)(2,1)S(1)}, u32[]{:S(2)}, u32[]{:S(2)}) %all-to-all-start) | async-done | bytes 1179680 | tf_op jit(solution)/shard_map/all_to_all | solution.py:542
  41.2 0.0 copy-start.1
  41.2 1.0 %copy-done.1 = bf16[32,16,1152]{2,1,0:T(8,128)(2,1)} copy-done((bf16[32,16,1152]{2,1,0:T(8,128)(2,1)}, bf16[32,16,1152]{2,1,0:T(8,128)(2,1)S(1)}, u32[]{:S(2)}) %copy-start.1) | copy-done | bytes 1179672
  42.2 20.7 %owner_backward.1 = (bf16[512,512]{1,0:T(8,128)(2,1)}, bf16[4,256,512]{2,1,0:T(8,128)(2,1)}, bf16[1024,1536]{1,0:T(8,128)(2,1)}, bf16[512,1024]{1,0:T(8,128)(2,1...) custom-call(bf16[512,1152]{1,0:T(8,128)(2,1)} %bitcast.28, bf16[4,256,512]{2,1,0:T(8,128)(2,1)} %get-tuple-element.38.refs_1_, ...), custom_call_target="tpu_custom_call" | custom-call | flops 30000001024 | bytes 30000000 | tf_op jit(solution)/shard_map/owner_backward/pallas_call | solution.py:412
  62.9 0.0 copy-start
  62.9 0.1 collective-permute-start
  63.1 1.6 %convolution_convert_fusion = bf16[512,512]{1,0:T(8,128)(2,1)S(1)} fusion(bf16[512,512]{1,0:T(8,128)(2,1)} %get-tuple-element.54, s32[512]{0:T(512)S(1)} %fusion.33), kind=kOutput, calls=%fused_computation.1 | convolution fusion | flops 268959744 | bytes 1050624 | tf_op jit(solution)/shard_map/dot_general | solution.py:21
  64.7 1.5 %collective-permute-done = bf16[256,2560]{1,0:T(8,128)(2,1)S(1)} collective-permute-done((bf16[256,2560]{1,0:T(8,128)(2,1)}, bf16[256,2560]{1,0:T(8,128)(2,1)S(1)}, u32[]{:S(2)}, u32[]{:S(2)}) %collective-permute-start) | collective-permute-done | bytes 1310752 | tf_op jit(solution)/shard_map/ppermute | solution.py:521
  66.3 0.0 copy-done
  66.3 0.3 add_convert_fusion
  66.6 0.2 collective-permute-start.1
  66.8 0.1 fusion.83
  66.9 2.5 %collective-permute-start.5 = (bf16[64,2560]{1,0:T(8,128)(2,1)S(1)}, bf16[64,2560]{1,0:T(8,128)(2,1)S(1)}, u32[]{:S(2)}, u32[]{:S(2)}) collective-permute-start(bf16[64,2560]{1,0:T(8,128)(2,1)S(1)} %get-tuple-element.72), channel_id=1, source_target_pairs={{0,1},{1,0},{16,17},{17,16},{2,3},{3,2},{18,19},{19,18},{4,5},{5,4... | collective-permute-start | bytes 983048 | tf_op jit(solution)/shard_map/ppermute | solution.py:521
  69.4 0.0 collective-permute-start.6
  69.4 1.5 %collective-permute-start.7 = (bf16[64,2560]{1,0:T(8,128)(2,1)S(1)}, bf16[64,2560]{1,0:T(8,128)(2,1)S(1)}, u32[]{:S(2)}, u32[]{:S(2)}) collective-permute-start(bf16[64,2560]{1,0:T(8,128)(2,1)S(1)} %get-tuple-element.70), channel_id=1, source_target_pairs={{0,17},{1,16},{16,1},{17,0},{2,19},{3,18},{18,3},{19,2},{4,21},{5,... | collective-permute-start | bytes 983048 | tf_op jit(solution)/shard_map/ppermute | solution.py:521
  70.9 0.0 collective-permute-done.1
  71.0 2.7 %collective-permute-start.4 = (bf16[128,512]{1,0:T(8,128)(2,1)S(1)}, bf16[128,512]{1,0:T(8,128)(2,1)S(1)}, u32[]{:S(2)}, u32[]{:S(2)}) collective-permute-start(bf16[128,512]{1,0:T(8,128)(2,1)S(1)} %pad_maximum_fusion.3), channel_id=1, source_target_pairs={{0,6},{2,0},{4,2},{6,4},{1,7},{3,1},{5,3},{7,5},{8,14},{10,8},{12,... | collective-permute-start | bytes 393224 | tf_op jit(solution)/shard_map/ppermute | solution.py:521
  73.7 0.1 collective-permute-start.3
  73.8 4.2 %collective-permute-done.5 = bf16[64,2560]{1,0:T(8,128)(2,1)S(1)} collective-permute-done((bf16[64,2560]{1,0:T(8,128)(2,1)S(1)}, bf16[64,2560]{1,0:T(8,128)(2,1)S(1)}, u32[]{:S(2)}, u32[]{:S(2)}) %collective-permute-start.5) | collective-permute-done | bytes 327712 | tf_op jit(solution)/shard_map/ppermute | solution.py:521
  77.9 0.0 collective-permute-start.2
  77.9 6.7 %input_backward.1 = bf16[4,256,512]{2,1,0:T(8,128)(2,1)} custom-call(bf16[4,256,512]{2,1,0:T(8,128)(2,1)} %get-tuple-element.57.denc_ref, bf16[512,2048]{1,0:T(8,128)(2,1)} %win_ref.3, bf16[1024,1536]{1,0:T(8,128)(2,1)} %get-tuple-element.58.dpre_ref, bf16[512,1024]{1,0:T(8,128)(2,1)} %get-tuple-element.59.dk_ref), custom_call_target="tpu_custom_call" | custom-call | flops 6000000000 | bytes 8000000 | tf_op jit(solution)/shard_map/input_backward/pallas_call | solution.py:445
  84.6 1.5 %collective-permute-done.6 = bf16[64,2560]{1,0:T(8,128)(2,1)S(1)} collective-permute-done((bf16[64,2560]{1,0:T(8,128)(2,1)S(1)}, bf16[64,2560]{1,0:T(8,128)(2,1)S(1)}, u32[]{:S(2)}, u32[]{:S(2)}) %collective-permute-start.6) | collective-permute-done | bytes 327712 | tf_op jit(solution)/shard_map/ppermute | solution.py:521
  86.1 0.0 collective-permute-done.7
  86.1 0.0 collective-permute-done.4
  86.1 0.0 collective-permute-done.3
  86.1 0.0 collective-permute-done.2
  86.1 0.2 add_convert_fusion.1
  86.3 0.1 collective-permute-start.11
  86.4 2.9 %collective-permute-start.12 = (bf16[16,2560]{1,0:T(8,128)(2,1)S(1)}, bf16[16,2560]{1,0:T(8,128)(2,1)S(1)}, u32[]{:S(2)}, u32[]{:S(2)}) collective-permute-start(bf16[16,2560]{1,0:T(8,128)(2,1)S(1)} %get-tuple-element.80), channel_id=1, source_target_pairs={{0,4},{2,6},{4,0},{6,2},{1,5},{3,7},{5,1},{7,3},{8,12},{10,14},{12... | collective-permute-start | bytes 245768 | tf_op jit(solution)/shard_map/ppermute | solution.py:521
  89.3 1.7 %collective-permute-start.13 = (bf16[16,2560]{1,0:T(8,128)(2,1)S(1)}, bf16[16,2560]{1,0:T(8,128)(2,1)S(1)}, u32[]{:S(2)}, u32[]{:S(2)}) collective-permute-start(bf16[16,2560]{1,0:T(8,128)(2,1)S(1)} %get-tuple-element.79), channel_id=1, source_target_pairs={{0,6},{2,0},{4,2},{6,4},{1,7},{3,1},{5,3},{7,5},{8,14},{10,8},{12,... | collective-permute-start | bytes 245768 | tf_op jit(solution)/shard_map/ppermute | solution.py:521
  91.0 0.0 copy-start.2
  91.1 0.8 collective-permute-start.10
  91.9 2.8 %collective-permute-start.9 = (bf16[128,512]{1,0:T(8,128)(2,1)S(1)}, bf16[128,512]{1,0:T(8,128)(2,1)S(1)}, u32[]{:S(2)}, u32[]{:S(2)}) collective-permute-start(bf16[128,512]{1,0:T(8,128)(2,1)S(1)} %pad_maximum_fusion.5), channel_id=1, source_target_pairs={{0,16},{1,17},{16,0},{17,1},{2,18},{3,19},{18,2},{19,3},{4,20},{5,... | collective-permute-start | bytes 393224 | tf_op jit(solution)/shard_map/ppermute | solution.py:521
  94.8 0.0 collective-permute-done.11
  94.8 0.1 collective-permute-start.8
  94.9 0.4 collective-permute-done.12
  95.3 0.0 collective-permute-done.13
  95.3 0.7 convert_add_fusion
  96.0 0.6 convert_add_fusion.1
  96.6 3.2 %collective-permute-done.8 = bf16[128,512]{1,0:T(8,128)(2,1)S(1)} collective-permute-done((bf16[128,512]{1,0:T(8,128)(2,1)S(1)}, bf16[128,512]{1,0:T(8,128)(2,1)S(1)}, u32[]{:S(2)}, u32[]{:S(2)}) %collective-permute-start.8) | collective-permute-done | bytes 131104 | tf_op jit(solution)/shard_map/ppermute | solution.py:521
  99.8 0.0 collective-permute-done.9
  99.9 0.0 collective-permute-done.10
  99.9 0.0 copy-done.2
  99.9 1.5 %convolution_convert_fusion.1 = bf16[256,512]{1,0:T(8,128)(2,1)} fusion(bf16[512,512]{1,0:T(8,128)(2,1)S(1)} %constant_dynamic-update-slice_fusion, bf16[512,256]{1,0:T(8,128)(2,1)S(1)} %copy-done.2, s32[512]{0:T(512)S(1)} %fusion.56), kind=kOutput, calls=%fused_computation.2 | convolution fusion | flops 268959744 | bytes 1050624 | tf_op jit(solution)/shard_map/dot_general | solution.py:568
  (25 shorter events, 0.3 us)
Async XLA Ops:
  3.5 37.7 %all-to-all-start = ((bf16[32,16,1152]{2,1,0:T(8,128)(2,1)}), bf16[32,16,1152]{2,1,0:T(8,128)(2,1)S(1)}, u32[]{:S(2)}, u32[]{:S(2)}) async-start(bf16[32,16,1152]{2,1,0:T(8,128)(2,1)} %bitcast.29), calls=%async_computation | async-start | bytes 2359296 | tf_op jit(solution)/shard_map/all_to_all | solution.py:542
  41.2 1.0 %copy-start.1 = (bf16[32,16,1152]{2,1,0:T(8,128)(2,1)}, bf16[32,16,1152]{2,1,0:T(8,128)(2,1)S(1)}, u32[]{:S(2)}) copy-start(bf16[32,16,1152]{2,1,0:T(8,128)(2,1)S(1)} %all-to-all-done) | copy-start | bytes 3538948
  62.9 3.3 %copy-start = (bf16[256,2560]{1,0:T(8,128)(2,1)S(1)}, bf16[256,2560]{1,0:T(8,128)(2,1)}, u32[]{:S(2)}) copy-start(bf16[256,2560]{1,0:T(8,128)(2,1)} %get-tuple-element.52) | copy-start | bytes 3932164
  62.9 3.3 %collective-permute-start = (bf16[256,2560]{1,0:T(8,128)(2,1)}, bf16[256,2560]{1,0:T(8,128)(2,1)S(1)}, u32[]{:S(2)}, u32[]{:S(2)}) collective-permute-start(bf16[256,2560]{1,0:T(8,128)(2,1)} %get-tuple-element.53), channel_id=1, source_target_pairs={{0,8},{8,0},{1,9},{9,1},{2,10},{10,2},{3,11},{11,3},{4,12},{12,4},... | collective-permute-start | bytes 3932168 | tf_op jit(solution)/shard_map/ppermute | solution.py:521
  66.6 4.3 %collective-permute-start.1 = (bf16[256,512]{1,0:T(8,128)(2,1)S(1)}, bf16[256,512]{1,0:T(8,128)(2,1)S(1)}, u32[]{:S(2)}, u32[]{:S(2)}) collective-permute-start(bf16[256,512]{1,0:T(8,128)(2,1)S(1)} %slice.129), channel_id=1, source_target_pairs={{0,8},{8,0},{1,9},{9,1},{2,10},{10,2},{3,11},{11,3},{4,12},{12,4},... | collective-permute-start | bytes 786440 | tf_op jit(solution)/shard_map/ppermute | solution.py:521
  66.9 11.0 %collective-permute-start.5 = (bf16[64,2560]{1,0:T(8,128)(2,1)S(1)}, bf16[64,2560]{1,0:T(8,128)(2,1)S(1)}, u32[]{:S(2)}, u32[]{:S(2)}) collective-permute-start(bf16[64,2560]{1,0:T(8,128)(2,1)S(1)} %get-tuple-element.72), channel_id=1, source_target_pairs={{0,1},{1,0},{16,17},{17,16},{2,3},{3,2},{18,19},{19,18},{4,5},{5,4... | collective-permute-start | bytes 983048 | tf_op jit(solution)/shard_map/ppermute | solution.py:521
  69.4 16.7 %collective-permute-start.6 = (bf16[64,2560]{1,0:T(8,128)(2,1)S(1)}, bf16[64,2560]{1,0:T(8,128)(2,1)S(1)}, u32[]{:S(2)}, u32[]{:S(2)}) collective-permute-start(bf16[64,2560]{1,0:T(8,128)(2,1)S(1)} %get-tuple-element.71), channel_id=1, source_target_pairs={{0,16},{1,17},{16,0},{17,1},{2,18},{3,19},{18,2},{19,3},{4,20},{5,... | collective-permute-start | bytes 983048 | tf_op jit(solution)/shard_map/ppermute | solution.py:521
  69.4 16.7 %collective-permute-start.7 = (bf16[64,2560]{1,0:T(8,128)(2,1)S(1)}, bf16[64,2560]{1,0:T(8,128)(2,1)S(1)}, u32[]{:S(2)}, u32[]{:S(2)}) collective-permute-start(bf16[64,2560]{1,0:T(8,128)(2,1)S(1)} %get-tuple-element.70), channel_id=1, source_target_pairs={{0,17},{1,16},{16,1},{17,0},{2,19},{3,18},{18,3},{19,2},{4,21},{5,... | collective-permute-start | bytes 983048 | tf_op jit(solution)/shard_map/ppermute | solution.py:521
  71.0 15.1 %collective-permute-start.4 = (bf16[128,512]{1,0:T(8,128)(2,1)S(1)}, bf16[128,512]{1,0:T(8,128)(2,1)S(1)}, u32[]{:S(2)}, u32[]{:S(2)}) collective-permute-start(bf16[128,512]{1,0:T(8,128)(2,1)S(1)} %pad_maximum_fusion.3), channel_id=1, source_target_pairs={{0,6},{2,0},{4,2},{6,4},{1,7},{3,1},{5,3},{7,5},{8,14},{10,8},{12,... | collective-permute-start | bytes 393224 | tf_op jit(solution)/shard_map/ppermute | solution.py:521
  73.7 12.4 %collective-permute-start.3 = (bf16[128,512]{1,0:T(8,128)(2,1)S(1)}, bf16[128,512]{1,0:T(8,128)(2,1)S(1)}, u32[]{:S(2)}, u32[]{:S(2)}) collective-permute-start(bf16[128,512]{1,0:T(8,128)(2,1)S(1)} %pad_maximum_fusion.2), channel_id=1, source_target_pairs={{0,4},{2,6},{4,0},{6,2},{1,5},{3,7},{5,1},{7,3},{8,12},{10,14},{12... | collective-permute-start | bytes 393224 | tf_op jit(solution)/shard_map/ppermute | solution.py:521
  77.9 8.2 %collective-permute-start.2 = (bf16[128,512]{1,0:T(8,128)(2,1)S(1)}, bf16[128,512]{1,0:T(8,128)(2,1)S(1)}, u32[]{:S(2)}, u32[]{:S(2)}) collective-permute-start(bf16[128,512]{1,0:T(8,128)(2,1)S(1)} %pad_maximum_fusion.1), channel_id=1, source_target_pairs={{0,2},{2,4},{4,6},{6,0},{1,3},{3,5},{5,7},{7,1},{8,10},{10,12},{12... | collective-permute-start | bytes 393224 | tf_op jit(solution)/shard_map/ppermute | solution.py:521
  86.3 8.5 %collective-permute-start.11 = (bf16[16,2560]{1,0:T(8,128)(2,1)S(1)}, bf16[16,2560]{1,0:T(8,128)(2,1)S(1)}, u32[]{:S(2)}, u32[]{:S(2)}) collective-permute-start(bf16[16,2560]{1,0:T(8,128)(2,1)S(1)} %get-tuple-element.78), channel_id=1, source_target_pairs={{0,2},{2,4},{4,6},{6,0},{1,3},{3,5},{5,7},{7,1},{8,10},{10,12},{12... | collective-permute-start | bytes 245768 | tf_op jit(solution)/shard_map/ppermute | solution.py:521
  86.4 8.9 %collective-permute-start.12 = (bf16[16,2560]{1,0:T(8,128)(2,1)S(1)}, bf16[16,2560]{1,0:T(8,128)(2,1)S(1)}, u32[]{:S(2)}, u32[]{:S(2)}) collective-permute-start(bf16[16,2560]{1,0:T(8,128)(2,1)S(1)} %get-tuple-element.80), channel_id=1, source_target_pairs={{0,4},{2,6},{4,0},{6,2},{1,5},{3,7},{5,1},{7,3},{8,12},{10,14},{12... | collective-permute-start | bytes 245768 | tf_op jit(solution)/shard_map/ppermute | solution.py:521
  89.3 6.0 %collective-permute-start.13 = (bf16[16,2560]{1,0:T(8,128)(2,1)S(1)}, bf16[16,2560]{1,0:T(8,128)(2,1)S(1)}, u32[]{:S(2)}, u32[]{:S(2)}) collective-permute-start(bf16[16,2560]{1,0:T(8,128)(2,1)S(1)} %get-tuple-element.79), channel_id=1, source_target_pairs={{0,6},{2,0},{4,2},{6,4},{1,7},{3,1},{5,3},{7,5},{8,14},{10,8},{12,... | collective-permute-start | bytes 245768 | tf_op jit(solution)/shard_map/ppermute | solution.py:521
  91.0 8.9 %copy-start.2 = (bf16[512,256]{1,0:T(8,128)(2,1)S(1)}, bf16[512,256]{1,0:T(8,128)(2,1)}, u32[]{:S(2)}) copy-start(bf16[512,256]{1,0:T(8,128)(2,1)} %get-tuple-element.61) | copy-start | bytes 786436
  91.1 8.8 %collective-permute-start.10 = (bf16[128,512]{1,0:T(8,128)(2,1)S(1)}, bf16[128,512]{1,0:T(8,128)(2,1)S(1)}, u32[]{:S(2)}, u32[]{:S(2)}) collective-permute-start(bf16[128,512]{1,0:T(8,128)(2,1)S(1)} %pad_maximum_fusion.6), channel_id=1, source_target_pairs={{0,17},{1,16},{16,1},{17,0},{2,19},{3,18},{18,3},{19,2},{4,21},{5,... | collective-permute-start | bytes 393224 | tf_op jit(solution)/shard_map/ppermute | solution.py:521
  91.9 7.9 %collective-permute-start.9 = (bf16[128,512]{1,0:T(8,128)(2,1)S(1)}, bf16[128,512]{1,0:T(8,128)(2,1)S(1)}, u32[]{:S(2)}, u32[]{:S(2)}) collective-permute-start(bf16[128,512]{1,0:T(8,128)(2,1)S(1)} %pad_maximum_fusion.5), channel_id=1, source_target_pairs={{0,16},{1,17},{16,0},{17,1},{2,18},{3,19},{18,2},{19,3},{4,20},{5,... | collective-permute-start | bytes 393224 | tf_op jit(solution)/shard_map/ppermute | solution.py:521
  94.8 5.0 %collective-permute-start.8 = (bf16[128,512]{1,0:T(8,128)(2,1)S(1)}, bf16[128,512]{1,0:T(8,128)(2,1)S(1)}, u32[]{:S(2)}, u32[]{:S(2)}) collective-permute-start(bf16[128,512]{1,0:T(8,128)(2,1)S(1)} %pad_maximum_fusion.4), channel_id=1, source_target_pairs={{0,1},{1,0},{16,17},{17,16},{2,3},{3,2},{18,19},{19,18},{4,5},{5,4... | collective-permute-start | bytes 393224 | tf_op jit(solution)/shard_map/ppermute | solution.py:521

commit v9 on v8

--- a/solution.py
+++ b/solution.py
@@ -351,7 +351,7 @@
 
     lax.fori_loop(0, tiles, one_tile, 0)
     for h in range(hist):
-        denc_ref[h] = jnp.transpose(turned_ref[h]).astype(bf16)
+        denc_ref[h] = jnp.transpose(turned_ref[h].astype(bf16))
     back = (dest == iota((slots, padded), 1)).astype(f32).astype(bf16)
     dq_ref[...] = dot_nn(back, grouped_ref[...]).astype(bf16)
     stores = []

time: 102 us -> 102 us (level); the launches traced: 101 us -> 103 us
  starting transfers between devices: 22.7 us -> 26.7 us
  waiting for transfers between devices: 26 us -> 24 us
    ppermute x14, starting transfers between devices: 15.4 us -> 19.4 us  [send_blocks(): parts.append(lax.ppermute(blocks[d], axes, pairs))]
    ppermute x14, waiting for transfers between devices: 10.8 us -> 8.84 us  [send_blocks(): parts.append(lax.ppermute(blocks[d], axes, pairs))]
  transfers between devices with their start and end apart: 15 -> 15, of which waited for: 6 -> 7; matrix products, arithmetic and copies ran while one was open for 4% -> 4% of each run, Pallas kernels for 21% -> 20%
where the time goes in v9:
time: 102 us; the launch traced here: 103 us
  Pallas kernels  44.5 us (44%)
  starting transfers between devices  26.7 us (26%)
  waiting for transfers between devices  24 us (24%)
  matrix products  3.13 us (3%)
  other arithmetic  2.93 us (3%)
  local copies, waits for them, and re-layouts  1.29 us (1%)
    pallas_call x1, Pallas kernels, owner_backward(): pl.pallas_call(owner_kernel, grid=(1,), in_specs=[raw] * len(operands), o...  20.7 us
    ppermute x14, starting transfers between devices, send_blocks(): parts.append(lax.ppermute(blocks[d], axes, pairs))  19.4 us
    all_to_all x1, waiting for transfers between devices, local(): recv = lax.all_to_all(shaped, AXES, split_axis=0, concat_axis=0, tiled=True)  15.2 us
    pallas_call x1, Pallas kernels, layer_forward(): pl.pallas_call(forward_kernel, grid=(hist,), in_specs=[row, whole(w_in.sh...  14.2 us
    ppermute x14, waiting for transfers between devices, send_blocks(): parts.append(lax.ppermute(blocks[d], axes, pairs))  8.84 us
    all_to_all x1, starting transfers between devices, local(): recv = lax.all_to_all(shaped, AXES, split_axis=0, concat_axis=0, tiled=True)  7.3 us
    pallas_call x1, Pallas kernels, input_backward(): pl.pallas_call(input_kernel, grid=(hist,), in_specs=[block(denc), whole(w...  6.69 us
    pallas_call x1, Pallas kernels, route(): pl.pallas_call(functools.partial(route_kernel, devices, capacity), grid=(...  2.86 us
  transfers between devices with their start and end apart: 15, of which 7 were waited for; matrix products, arithmetic and copies ran while one was open for 4% of the time, Pallas kernels for 20%

profile of v9, /device:TPU:0, one launch (start us, length us, event | category | flops | bytes accessed | tf_op | source)
XLA Modules:
  0.0 103.4 jit_solution(11860880716955605559)
XLA Ops:
  0.6 2.9 %route.1 = (bf16[512,1152]{1,0:T(8,128)(2,1)}, bf16[512,256]{1,0:T(8,128)(2,1)}) custom-call(s32[1,256]{1,0:T(1,128)} %bitcast.50, s32[1,256]{1,0:T(1,128)} %bitcast.51, s32[1,256]{1,0:T(1,128)} %bitcast.52, bf16[256,512]{1,0:T(8,128)(2,1)} %cand_ref.1, bf16[256,512]{1,0:T(8,128)(2,1)} %cot_ref.1), custom_call_target="tpu_custom_call" | custom-call | flops 2000000000 | bytes 2097152 | tf_op jit(solution)/shard_map/route/pallas_call | solution.py:92
  3.5 7.3 %all-to-all-start = ((bf16[32,16,1152]{2,1,0:T(8,128)(2,1)}), bf16[32,16,1152]{2,1,0:T(8,128)(2,1)S(1)}, u32[]{:S(2)}, u32[]{:S(2)}) async-start(bf16[32,16,1152]{2,1,0:T(8,128)(2,1)} %bitcast.29), calls=%async_computation | async-start | bytes 2359296 | tf_op jit(solution)/shard_map/all_to_all | solution.py:542
  10.8 1.0 fusion.perm_ref
  11.8 14.2 %forward.1 = (bf16[4,256,512]{2,1,0:T(8,128)(2,1)}, bf16[4,256,1024]{2,1,0:T(8,128)(2,1)}, bf16[4,512,256]{2,1,0:T(8,128)(2,1)}, bf16[4,256,512]{2,1,0:T(8,128)(...) custom-call(bf16[4,256,512]{2,1,0:T(8,128)(2,1)} %x_ref.1, ...), custom_call_target="tpu_custom_call" | custom-call | flops 17999998976 | bytes 24000000 | tf_op jit(solution)/shard_map/forward/pallas_call | solution.py:180
  26.0 15.2 %all-to-all-done = bf16[32,16,1152]{2,1,0:T(8,128)(2,1)S(1)} async-done(((bf16[32,16,1152]{2,1,0:T(8,128)(2,1)}), bf16[32,16,1152]{2,1,0:T(8,128)(2,1)S(1)}, u32[]{:S(2)}, u32[]{:S(2)}) %all-to-all-start) | async-done | bytes 1179680 | tf_op jit(solution)/shard_map/all_to_all | solution.py:542
  41.2 0.0 copy-start.1
  41.2 1.0 copy-done.1
  42.2 20.7 %owner_backward.1 = (bf16[512,512]{1,0:T(8,128)(2,1)}, bf16[4,256,512]{2,1,0:T(8,128)(2,1)}, bf16[1024,1536]{1,0:T(8,128)(2,1)}, bf16[512,1024]{1,0:T(8,128)(2,1...) custom-call(bf16[512,1152]{1,0:T(8,128)(2,1)} %bitcast.28, bf16[4,256,512]{2,1,0:T(8,128)(2,1)} %get-tuple-element.38.refs_1_, ...), custom_call_target="tpu_custom_call" | custom-call | flops 30000001024 | bytes 30000000 | tf_op jit(solution)/shard_map/owner_backward/pallas_call | solution.py:412
  62.9 0.0 copy-start
  63.0 0.1 collective-permute-start
  63.1 1.6 %convolution_convert_fusion = bf16[512,512]{1,0:T(8,128)(2,1)S(1)} fusion(bf16[512,512]{1,0:T(8,128)(2,1)} %get-tuple-element.54, s32[512]{0:T(512)S(1)} %fusion.33), kind=kOutput, calls=%fused_computation.1 | convolution fusion | flops 268959744 | bytes 1050624 | tf_op jit(solution)/shard_map/dot_general | solution.py:21
  64.7 1.5 %collective-permute-done = bf16[256,2560]{1,0:T(8,128)(2,1)S(1)} collective-permute-done((bf16[256,2560]{1,0:T(8,128)(2,1)}, bf16[256,2560]{1,0:T(8,128)(2,1)S(1)}, u32[]{:S(2)}, u32[]{:S(2)}) %collective-permute-start) | collective-permute-done | bytes 1310752 | tf_op jit(solution)/shard_map/ppermute | solution.py:521
  66.3 0.0 copy-done
  66.3 0.3 add_convert_fusion
  66.6 0.2 collective-permute-start.1
  66.8 0.1 fusion.83
  66.9 2.5 %collective-permute-start.5 = (bf16[64,2560]{1,0:T(8,128)(2,1)S(1)}, bf16[64,2560]{1,0:T(8,128)(2,1)S(1)}, u32[]{:S(2)}, u32[]{:S(2)}) collective-permute-start(bf16[64,2560]{1,0:T(8,128)(2,1)S(1)} %get-tuple-element.72), channel_id=1, source_target_pairs={{0,1},{1,0},{16,17},{17,16},{2,3},{3,2},{18,19},{19,18},{4,5},{5,4... | collective-permute-start | bytes 983048 | tf_op jit(solution)/shard_map/ppermute | solution.py:521
  69.4 0.0 collective-permute-start.6
  69.5 1.5 %collective-permute-start.7 = (bf16[64,2560]{1,0:T(8,128)(2,1)S(1)}, bf16[64,2560]{1,0:T(8,128)(2,1)S(1)}, u32[]{:S(2)}, u32[]{:S(2)}) collective-permute-start(bf16[64,2560]{1,0:T(8,128)(2,1)S(1)} %get-tuple-element.70), channel_id=1, source_target_pairs={{0,17},{1,16},{16,1},{17,0},{2,19},{3,18},{18,3},{19,2},{4,21},{5,... | collective-permute-start | bytes 983048 | tf_op jit(solution)/shard_map/ppermute | solution.py:521
  71.0 0.0 collective-permute-done.1
  71.1 5.3 %collective-permute-start.4 = (bf16[128,512]{1,0:T(8,128)(2,1)S(1)}, bf16[128,512]{1,0:T(8,128)(2,1)S(1)}, u32[]{:S(2)}, u32[]{:S(2)}) collective-permute-start(bf16[128,512]{1,0:T(8,128)(2,1)S(1)} %pad_maximum_fusion.3), channel_id=1, source_target_pairs={{0,6},{2,0},{4,2},{6,4},{1,7},{3,1},{5,3},{7,5},{8,14},{10,8},{12,... | collective-permute-start | bytes 393224 | tf_op jit(solution)/shard_map/ppermute | solution.py:521
  76.4 0.1 collective-permute-start.3
  76.5 1.5 %collective-permute-done.5 = bf16[64,2560]{1,0:T(8,128)(2,1)S(1)} collective-permute-done((bf16[64,2560]{1,0:T(8,128)(2,1)S(1)}, bf16[64,2560]{1,0:T(8,128)(2,1)S(1)}, u32[]{:S(2)}, u32[]{:S(2)}) %collective-permute-start.5) | collective-permute-done | bytes 327712 | tf_op jit(solution)/shard_map/ppermute | solution.py:521
  77.9 0.0 collective-permute-start.2
  77.9 6.7 %input_backward.1 = bf16[4,256,512]{2,1,0:T(8,128)(2,1)} custom-call(bf16[4,256,512]{2,1,0:T(8,128)(2,1)} %get-tuple-element.57.denc_ref, bf16[512,2048]{1,0:T(8,128)(2,1)} %win_ref.3, bf16[1024,1536]{1,0:T(8,128)(2,1)} %get-tuple-element.58.dpre_ref, bf16[512,1024]{1,0:T(8,128)(2,1)} %get-tuple-element.59.dk_ref), custom_call_target="tpu_custom_call" | custom-call | flops 6000000000 | bytes 8000000 | tf_op jit(solution)/shard_map/input_backward/pallas_call | solution.py:445
  84.6 1.4 %collective-permute-done.6 = bf16[64,2560]{1,0:T(8,128)(2,1)S(1)} collective-permute-done((bf16[64,2560]{1,0:T(8,128)(2,1)S(1)}, bf16[64,2560]{1,0:T(8,128)(2,1)S(1)}, u32[]{:S(2)}, u32[]{:S(2)}) %collective-permute-start.6) | collective-permute-done | bytes 327712 | tf_op jit(solution)/shard_map/ppermute | solution.py:521
  86.1 0.0 collective-permute-done.7
  86.1 0.0 collective-permute-done.4
  86.1 1.5 %collective-permute-done.3 = bf16[128,512]{1,0:T(8,128)(2,1)S(1)} collective-permute-done((bf16[128,512]{1,0:T(8,128)(2,1)S(1)}, bf16[128,512]{1,0:T(8,128)(2,1)S(1)}, u32[]{:S(2)}, u32[]{:S(2)}) %collective-permute-start.3) | collective-permute-done | bytes 131104 | tf_op jit(solution)/shard_map/ppermute | solution.py:521
  87.6 0.0 collective-permute-done.2
  87.6 0.2 add_convert_fusion.1
  87.8 0.6 collective-permute-start.11
  88.4 3.6 %collective-permute-start.12 = (bf16[16,2560]{1,0:T(8,128)(2,1)S(1)}, bf16[16,2560]{1,0:T(8,128)(2,1)S(1)}, u32[]{:S(2)}, u32[]{:S(2)}) collective-permute-start(bf16[16,2560]{1,0:T(8,128)(2,1)S(1)} %get-tuple-element.80), channel_id=1, source_target_pairs={{0,4},{2,6},{4,0},{6,2},{1,5},{3,7},{5,1},{7,3},{8,12},{10,14},{12... | collective-permute-start | bytes 245768 | tf_op jit(solution)/shard_map/ppermute | solution.py:521
  92.0 1.2 %collective-permute-start.13 = (bf16[16,2560]{1,0:T(8,128)(2,1)S(1)}, bf16[16,2560]{1,0:T(8,128)(2,1)S(1)}, u32[]{:S(2)}, u32[]{:S(2)}) collective-permute-start(bf16[16,2560]{1,0:T(8,128)(2,1)S(1)} %get-tuple-element.79), channel_id=1, source_target_pairs={{0,6},{2,0},{4,2},{6,4},{1,7},{3,1},{5,3},{7,5},{8,14},{10,8},{12,... | collective-permute-start | bytes 245768 | tf_op jit(solution)/shard_map/ppermute | solution.py:521
  93.3 0.0 copy-start.2
  93.4 2.1 %collective-permute-start.10 = (bf16[128,512]{1,0:T(8,128)(2,1)S(1)}, bf16[128,512]{1,0:T(8,128)(2,1)S(1)}, u32[]{:S(2)}, u32[]{:S(2)}) collective-permute-start(bf16[128,512]{1,0:T(8,128)(2,1)S(1)} %pad_maximum_fusion.6), channel_id=1, source_target_pairs={{0,17},{1,16},{16,1},{17,0},{2,19},{3,18},{18,3},{19,2},{4,21},{5,... | collective-permute-start | bytes 393224 | tf_op jit(solution)/shard_map/ppermute | solution.py:521
  95.4 0.6 collective-permute-start.9
  96.1 0.0 collective-permute-done.11
  96.1 1.5 %collective-permute-start.8 = (bf16[128,512]{1,0:T(8,128)(2,1)S(1)}, bf16[128,512]{1,0:T(8,128)(2,1)S(1)}, u32[]{:S(2)}, u32[]{:S(2)}) collective-permute-start(bf16[128,512]{1,0:T(8,128)(2,1)S(1)} %pad_maximum_fusion.4), channel_id=1, source_target_pairs={{0,1},{1,0},{16,17},{17,16},{2,3},{3,2},{18,19},{19,18},{4,5},{5,4... | collective-permute-start | bytes 393224 | tf_op jit(solution)/shard_map/ppermute | solution.py:521
  97.7 0.0 collective-permute-done.12
  97.7 0.1 collective-permute-done.13
  97.8 0.7 convert_add_fusion
  98.5 0.6 convert_add_fusion.1
  99.1 2.7 %collective-permute-done.8 = bf16[128,512]{1,0:T(8,128)(2,1)S(1)} collective-permute-done((bf16[128,512]{1,0:T(8,128)(2,1)S(1)}, bf16[128,512]{1,0:T(8,128)(2,1)S(1)}, u32[]{:S(2)}, u32[]{:S(2)}) %collective-permute-start.8) | collective-permute-done | bytes 131104 | tf_op jit(solution)/shard_map/ppermute | solution.py:521
  101.8 0.0 collective-permute-done.9
  101.9 0.0 collective-permute-done.10
  101.9 0.0 copy-done.2
  101.9 1.5 %convolution_convert_fusion.1 = bf16[256,512]{1,0:T(8,128)(2,1)} fusion(bf16[512,512]{1,0:T(8,128)(2,1)S(1)} %constant_dynamic-update-slice_fusion, bf16[512,256]{1,0:T(8,128)(2,1)S(1)} %copy-done.2, s32[512]{0:T(512)S(1)} %fusion.56), kind=kOutput, calls=%fused_computation.2 | convolution fusion | flops 268959744 | bytes 1050624 | tf_op jit(solution)/shard_map/dot_general | solution.py:568
  (25 shorter events, 0.3 us)
Async XLA Ops:
  3.5 37.7 %all-to-all-start = ((bf16[32,16,1152]{2,1,0:T(8,128)(2,1)}), bf16[32,16,1152]{2,1,0:T(8,128)(2,1)S(1)}, u32[]{:S(2)}, u32[]{:S(2)}) async-start(bf16[32,16,1152]{2,1,0:T(8,128)(2,1)} %bitcast.29), calls=%async_computation | async-start | bytes 2359296 | tf_op jit(solution)/shard_map/all_to_all | solution.py:542
  41.2 1.0 copy-start.1
  62.9 3.3 %copy-start = (bf16[256,2560]{1,0:T(8,128)(2,1)S(1)}, bf16[256,2560]{1,0:T(8,128)(2,1)}, u32[]{:S(2)}) copy-start(bf16[256,2560]{1,0:T(8,128)(2,1)} %get-tuple-element.52) | copy-start | bytes 3932164
  63.0 3.3 %collective-permute-start = (bf16[256,2560]{1,0:T(8,128)(2,1)}, bf16[256,2560]{1,0:T(8,128)(2,1)S(1)}, u32[]{:S(2)}, u32[]{:S(2)}) collective-permute-start(bf16[256,2560]{1,0:T(8,128)(2,1)} %get-tuple-element.53), channel_id=1, source_target_pairs={{0,8},{8,0},{1,9},{9,1},{2,10},{10,2},{3,11},{11,3},{4,12},{12,4},... | collective-permute-start | bytes 3932168 | tf_op jit(solution)/shard_map/ppermute | solution.py:521
  66.6 4.4 %collective-permute-start.1 = (bf16[256,512]{1,0:T(8,128)(2,1)S(1)}, bf16[256,512]{1,0:T(8,128)(2,1)S(1)}, u32[]{:S(2)}, u32[]{:S(2)}) collective-permute-start(bf16[256,512]{1,0:T(8,128)(2,1)S(1)} %slice.129), channel_id=1, source_target_pairs={{0,8},{8,0},{1,9},{9,1},{2,10},{10,2},{3,11},{11,3},{4,12},{12,4},... | collective-permute-start | bytes 786440 | tf_op jit(solution)/shard_map/ppermute | solution.py:521
  66.9 11.0 %collective-permute-start.5 = (bf16[64,2560]{1,0:T(8,128)(2,1)S(1)}, bf16[64,2560]{1,0:T(8,128)(2,1)S(1)}, u32[]{:S(2)}, u32[]{:S(2)}) collective-permute-start(bf16[64,2560]{1,0:T(8,128)(2,1)S(1)} %get-tuple-element.72), channel_id=1, source_target_pairs={{0,1},{1,0},{16,17},{17,16},{2,3},{3,2},{18,19},{19,18},{4,5},{5,4... | collective-permute-start | bytes 983048 | tf_op jit(solution)/shard_map/ppermute | solution.py:521
  69.4 16.6 %collective-permute-start.6 = (bf16[64,2560]{1,0:T(8,128)(2,1)S(1)}, bf16[64,2560]{1,0:T(8,128)(2,1)S(1)}, u32[]{:S(2)}, u32[]{:S(2)}) collective-permute-start(bf16[64,2560]{1,0:T(8,128)(2,1)S(1)} %get-tuple-element.71), channel_id=1, source_target_pairs={{0,16},{1,17},{16,0},{17,1},{2,18},{3,19},{18,2},{19,3},{4,20},{5,... | collective-permute-start | bytes 983048 | tf_op jit(solution)/shard_map/ppermute | solution.py:521
  69.5 16.6 %collective-permute-start.7 = (bf16[64,2560]{1,0:T(8,128)(2,1)S(1)}, bf16[64,2560]{1,0:T(8,128)(2,1)S(1)}, u32[]{:S(2)}, u32[]{:S(2)}) collective-permute-start(bf16[64,2560]{1,0:T(8,128)(2,1)S(1)} %get-tuple-element.70), channel_id=1, source_target_pairs={{0,17},{1,16},{16,1},{17,0},{2,19},{3,18},{18,3},{19,2},{4,21},{5,... | collective-permute-start | bytes 983048 | tf_op jit(solution)/shard_map/ppermute | solution.py:521
  71.1 15.0 %collective-permute-start.4 = (bf16[128,512]{1,0:T(8,128)(2,1)S(1)}, bf16[128,512]{1,0:T(8,128)(2,1)S(1)}, u32[]{:S(2)}, u32[]{:S(2)}) collective-permute-start(bf16[128,512]{1,0:T(8,128)(2,1)S(1)} %pad_maximum_fusion.3), channel_id=1, source_target_pairs={{0,6},{2,0},{4,2},{6,4},{1,7},{3,1},{5,3},{7,5},{8,14},{10,8},{12,... | collective-permute-start | bytes 393224 | tf_op jit(solution)/shard_map/ppermute | solution.py:521
  76.4 11.3 %collective-permute-start.3 = (bf16[128,512]{1,0:T(8,128)(2,1)S(1)}, bf16[128,512]{1,0:T(8,128)(2,1)S(1)}, u32[]{:S(2)}, u32[]{:S(2)}) collective-permute-start(bf16[128,512]{1,0:T(8,128)(2,1)S(1)} %pad_maximum_fusion.2), channel_id=1, source_target_pairs={{0,4},{2,6},{4,0},{6,2},{1,5},{3,7},{5,1},{7,3},{8,12},{10,14},{12... | collective-permute-start | bytes 393224 | tf_op jit(solution)/shard_map/ppermute | solution.py:521
  77.9 9.7 %collective-permute-start.2 = (bf16[128,512]{1,0:T(8,128)(2,1)S(1)}, bf16[128,512]{1,0:T(8,128)(2,1)S(1)}, u32[]{:S(2)}, u32[]{:S(2)}) collective-permute-start(bf16[128,512]{1,0:T(8,128)(2,1)S(1)} %pad_maximum_fusion.1), channel_id=1, source_target_pairs={{0,2},{2,4},{4,6},{6,0},{1,3},{3,5},{5,7},{7,1},{8,10},{10,12},{12... | collective-permute-start | bytes 393224 | tf_op jit(solution)/shard_map/ppermute | solution.py:521
  87.8 8.3 %collective-permute-start.11 = (bf16[16,2560]{1,0:T(8,128)(2,1)S(1)}, bf16[16,2560]{1,0:T(8,128)(2,1)S(1)}, u32[]{:S(2)}, u32[]{:S(2)}) collective-permute-start(bf16[16,2560]{1,0:T(8,128)(2,1)S(1)} %get-tuple-element.78), channel_id=1, source_target_pairs={{0,2},{2,4},{4,6},{6,0},{1,3},{3,5},{5,7},{7,1},{8,10},{10,12},{12... | collective-permute-start | bytes 245768 | tf_op jit(solution)/shard_map/ppermute | solution.py:521
  88.4 9.2 %collective-permute-start.12 = (bf16[16,2560]{1,0:T(8,128)(2,1)S(1)}, bf16[16,2560]{1,0:T(8,128)(2,1)S(1)}, u32[]{:S(2)}, u32[]{:S(2)}) collective-permute-start(bf16[16,2560]{1,0:T(8,128)(2,1)S(1)} %get-tuple-element.80), channel_id=1, source_target_pairs={{0,4},{2,6},{4,0},{6,2},{1,5},{3,7},{5,1},{7,3},{8,12},{10,14},{12... | collective-permute-start | bytes 245768 | tf_op jit(solution)/shard_map/ppermute | solution.py:521
  92.0 5.8 %collective-permute-start.13 = (bf16[16,2560]{1,0:T(8,128)(2,1)S(1)}, bf16[16,2560]{1,0:T(8,128)(2,1)S(1)}, u32[]{:S(2)}, u32[]{:S(2)}) collective-permute-start(bf16[16,2560]{1,0:T(8,128)(2,1)S(1)} %get-tuple-element.79), channel_id=1, source_target_pairs={{0,6},{2,0},{4,2},{6,4},{1,7},{3,1},{5,3},{7,5},{8,14},{10,8},{12,... | collective-permute-start | bytes 245768 | tf_op jit(solution)/shard_map/ppermute | solution.py:521
  93.3 8.6 %copy-start.2 = (bf16[512,256]{1,0:T(8,128)(2,1)S(1)}, bf16[512,256]{1,0:T(8,128)(2,1)}, u32[]{:S(2)}) copy-start(bf16[512,256]{1,0:T(8,128)(2,1)} %get-tuple-element.61) | copy-start | bytes 786436
  93.4 8.5 %collective-permute-start.10 = (bf16[128,512]{1,0:T(8,128)(2,1)S(1)}, bf16[128,512]{1,0:T(8,128)(2,1)S(1)}, u32[]{:S(2)}, u32[]{:S(2)}) collective-permute-start(bf16[128,512]{1,0:T(8,128)(2,1)S(1)} %pad_maximum_fusion.6), channel_id=1, source_target_pairs={{0,17},{1,16},{16,1},{17,0},{2,19},{3,18},{18,3},{19,2},{4,21},{5,... | collective-permute-start | bytes 393224 | tf_op jit(solution)/shard_map/ppermute | solution.py:521
  95.4 6.4 %collective-permute-start.9 = (bf16[128,512]{1,0:T(8,128)(2,1)S(1)}, bf16[128,512]{1,0:T(8,128)(2,1)S(1)}, u32[]{:S(2)}, u32[]{:S(2)}) collective-permute-start(bf16[128,512]{1,0:T(8,128)(2,1)S(1)} %pad_maximum_fusion.5), channel_id=1, source_target_pairs={{0,16},{1,17},{16,0},{17,1},{2,18},{3,19},{18,2},{19,3},{4,20},{5,... | collective-permute-start | bytes 393224 | tf_op jit(solution)/shard_map/ppermute | solution.py:521
  96.1 5.7 %collective-permute-start.8 = (bf16[128,512]{1,0:T(8,128)(2,1)S(1)}, bf16[128,512]{1,0:T(8,128)(2,1)S(1)}, u32[]{:S(2)}, u32[]{:S(2)}) collective-permute-start(bf16[128,512]{1,0:T(8,128)(2,1)S(1)} %pad_maximum_fusion.4), channel_id=1, source_target_pairs={{0,1},{1,0},{16,17},{17,16},{2,3},{3,2},{18,19},{19,18},{4,5},{5,4... | collective-permute-start | bytes 393224 | tf_op jit(solution)/shard_map/ppermute | solution.py:521
